TPU v7x, 32 devices: a whole 2x2x4 slice. The times are simulated.
32 devices in a mesh: sample: 4 (over z), landmark: 8 (over y, x, core).
Axes of the slice: x: 2, y: 2, z: 4, core: 2. Of those that a mesh axis runs over, the one named last changes fastest.
Arguments:
- embeddings: bfloat16 [4096, 4096], P('sample'), may hold values from -6 to 6
- landmarks: bfloat16 [16384, 4096], P('landmark'), may hold values from -6 to 6
- factor: bfloat16 [16384, 16384], P('landmark', 'sample')
- flips: int32 [512, 4096], P(None, 'sample'), may hold values from 0 to 1
- labels: int32 [4096], P('sample'), may hold values from 0 to 1, as said below
- counts: int32 [4], replicated, may hold values from 256 to 1024, as said below
Outputs:
- whitened: bfloat16 [16384, 512], P(('sample', 'landmark'))
- statistic: float32 [512], replicated
Inputs may be any that keep to these rules, and one draw needn't show every extreme that they name: `counts`: one slab holds exactly 1024 live rows. `labels`: 0 or 1; the first slot of every slab is of corpus 0 and the second of corpus 1.
All inputs are finite; a program needn't handle non-finite values.
Results may differ from a plain program's by a relative error of at most 0.029.
Values may be sent and summed in bfloat16 or wider, within the bound.
No kernel may reach another device: no remote copies, remote signals or barrier semaphores. Data moves between devices by JAX's collectives and lax.ppermute only.
A program may use at most 128 MiB of HBM per device.

v0:
```python
import math

import jax
import jax.numpy as jnp
from jax import lax
from jax.sharding import PartitionSpec as P

D = 4096
LANDMARKS = 16384


def whiten_maker(factor, moments_half):
    return lax.dot_general(
        factor, moments_half, (((0,), (1,)), ((), ())), preferred_element_type=jnp.float32
    )


def local(embeddings, landmarks, factor, flips, labels, counts):
    slot_count = embeddings.shape[0]
    slab_total = counts.shape[0]
    here_index = lax.axis_index("sample")
    own_count = jnp.sum(jnp.where(jnp.arange(slab_total, dtype=jnp.int32) == here_index, counts, 0))
    live_rows = (jnp.arange(slot_count, dtype=jnp.int32) < own_count).astype(jnp.float32)
    corpus = labels.astype(jnp.float32)
    count_a, count_b = lax.psum(
        (jnp.sum(live_rows * (1.0 - corpus)), jnp.sum(live_rows * corpus)), "sample"
    )
    balance = jnp.sqrt(count_a * count_b / (count_a + count_b))
    row_weight = live_rows * ((1.0 - corpus) / count_a - corpus / count_b) * balance
    wide_x = embeddings.astype(jnp.float32)
    row_scale = lax.rsqrt(jnp.mean(wide_x * wide_x, axis=1) + 1e-06)
    wide_z = landmarks.astype(jnp.float32)
    point_scale = lax.rsqrt(jnp.mean(wide_z * wide_z, axis=1) + 1e-06)
    signs = (2 * flips - 1).astype(jnp.bfloat16)
    cross = lax.dot_general(
        embeddings, landmarks, (((1,), (1,)), ((), ())), preferred_element_type=jnp.float32
    )
    kern = jnp.exp(0.5 * cross * row_scale[:, None] * point_scale[None, :] / math.sqrt(D))
    weighted = (row_weight[:, None] * kern).astype(jnp.bfloat16)
    partial_value = jnp.dot(signs, weighted, preferred_element_type=jnp.float32)
    summed = lax.psum(partial_value.astype(jnp.bfloat16), "sample")
    wide = lax.psum_scatter(
        whiten_maker(factor, summed).astype(jnp.bfloat16),
        "landmark",
        scatter_dimension=0,
        tiled=True,
    ).astype(jnp.float32)
    share = jnp.sum(wide * wide, axis=0)
    statistic = lax.psum(share, ("sample", "landmark")) / LANDMARKS
    return (wide.astype(jnp.bfloat16), statistic)


def solution(mesh):
    return jax.shard_map(
        local,
        mesh=mesh,
        in_specs=(
            P("sample", None),
            P("landmark", None),
            P("landmark", "sample"),
            P(None, "sample"),
            P("sample"),
            P(),
        ),
        out_specs=(P(("sample", "landmark"), None), P()),
        check_vma=False,
    )
```

profile of v0, /device:TPU:0, one launch (start us, length us, event | category | flops | bytes accessed | tf_op | source)
XLA Modules:
  0.0 281.4 jit_solution(13544255103580048074)
XLA Ops:
  7.2 0.0 all-reduce.3.cloned.1.call-start
  7.2 1.3 fusion.3
  8.5 2.0 select_reduce_fusion
  10.5 14.1 %all-reduce = (f32[]{:T(128)}, f32[]{:T(128)}) all-reduce(f32[]{:T(128)} %get-tuple-element.5, f32[]{:T(128)} %get-tuple-element.4), channel_id=1, replica_groups=mesh['sample'=4,'landmark'=8] {'sample'}, use_global_device_ids=true, to_apply=%region_2.3 | all-reduce | flops 2 | bytes 16 | tf_op jit(solution)/shard_map/psum | solution.py:25
  27.1 2.5 select_multiply_fusion
  29.6 5.1 %multiply_reduce_fusion.1 = f32[1024]{0:T(1024)S(1)} fusion(bf16[1024,4096]{1,0:T(8,128)(2,1)} %param.6), kind=kLoop, calls=%fused_computation.1 | loop fusion | flops 12581888 | bytes 8392704 | tf_op jit(solution)/shard_map/reduce_sum | solution.py:31
  34.7 0.0 copy-start
  34.7 7.5 %multiply_reduce_fusion = f32[2048]{0:T(1024)S(1)} fusion(bf16[2048,4096]{1,0:T(8,128)(2,1)} %param.7), kind=kLoop, calls=%fused_computation | loop fusion | flops 25163776 | bytes 16785408 | tf_op jit(solution)/shard_map/reduce_sum | solution.py:33
  42.2 3.2 %copy-done = bf16[2048,4096]{1,0:T(8,128)(2,1)S(1)} copy-done((bf16[2048,4096]{1,0:T(8,128)(2,1)S(1)}, bf16[2048,4096]{1,0:T(8,128)(2,1)}, u32[]{:S(2)}) %copy-start) | copy-done | bytes 16777240
  45.4 0.0 copy-start.1
  45.4 30.4 %multiply_convert_fusion = bf16[1024,2048]{1,0:T(8,128)(2,1)} fusion(bf16[1024,4096]{1,0:T(8,128)(2,1)} %param.6, bf16[2048,4096]{1,0:T(8,128)(2,1)S(1)} %copy-done, f32[2048]{0:T(1024)S(1)} %add_rsqrt_fusion, f32[1024]{0:T(1024)S(1)} %rsqrt_multiply_fusion, f32[1024]{0:T(1024)S(1)} %select_multiply_fusion), kind=kOutput, calls=%fused_computation.2 | convolution fusion | flops 17190354944 | bytes 29376512 | tf_op jit(solution)/shard_map/dot_general | solution.py:35
  75.8 0.0 copy-done.1
  75.8 5.9 %convolution_convert_fusion.1 = bf16[512,2048]{1,0:T(8,128)(2,1)} fusion(bf16[1024,2048]{1,0:T(8,128)(2,1)} %multiply_convert_fusion, s32[512,1024]{1,0:T(8,128)S(1)} %copy-done.1), kind=kOutput, calls=%fused_computation.5 | convolution fusion | flops 2150105088 | bytes 8388608 | tf_op jit(solution)/shard_map/dot_general | solution.py:40
  81.6 0.0 all-reduce.3.cloned.1.call-update
  81.7 0.2 reduce-scatter.2.cloned.1.call-start
  81.9 84.7 %all-reduce.3.cloned.1.call-done = bf16[512,2048]{1,0:T(8,128)(2,1)} async-done(((bf16[512,2048]{1,0:T(8,128)(2,1)}), bf16[512,2048]{1,0:T(8,128)(2,1)}) %all-reduce.3.cloned.1.call-update) | async-done | bytes 2097168 | tf_op jit(solution)/shard_map/psum | solution.py:41
  166.6 14.3 %fusion = bf16[4096,512]{0,1:T(8,128)(2,1)} fusion(bf16[512,2048]{1,0:T(8,128)(2,1)} %all-reduce.3.cloned.1.call-done, bf16[2048,4096]{1,0:T(8,128)(2,1)} %param.8), kind=kOutput, calls=%fused_computation.4 | convolution fusion | flops 8592031744 | bytes 23068672 | tf_op jit(solution)/shard_map/dot_general | solution.py:13
  180.9 0.0 reduce-scatter.2.cloned.1.call-update
  180.9 50.4 %reduce-scatter.2.cloned.1.call-done = bf16[512,512]{0,1:T(8,128)(2,1)} async-done(((bf16[4096,512]{0,1:T(8,128)(2,1)}), bf16[512,512]{0,1:T(8,128)(2,1)}) %reduce-scatter.2.cloned.1.call-update) | async-done | bytes 524304 | tf_op jit(solution)/shard_map/reduce_scatter | solution.py:42
  231.3 1.2 multiply_reduce_fusion.2
  232.6 39.4 %psum.31 = f32[512]{0:T(512)S(1)} all-reduce(f32[512]{0:T(512)S(1)} %multiply_reduce_fusion.2), channel_id=1, replica_groups=mesh['sample'=4,'landmark'=8] {'sample','landmark'}, use_global_device_ids=true, to_apply=%region_10.11 | all-reduce | flops 512 | bytes 4096 | tf_op jit(solution)/shard_map/psum | solution.py:49
  271.9 0.6 broadcast_multiply_fusion
  272.5 2.0 copy.8
  (2 shorter events, 0.0 us)
Async XLA Ops:
  7.2 159.4 %all-reduce.3.cloned.1.call-start = ((), (), s32[]{:S(2)}) async-start(), calls=%async_computation.1 | async-start | bytes 4194304 | tf_op jit(solution)/shard_map/psum | solution.py:41
  34.7 10.7 %copy-start = (bf16[2048,4096]{1,0:T(8,128)(2,1)S(1)}, bf16[2048,4096]{1,0:T(8,128)(2,1)}, u32[]{:S(2)}) copy-start(bf16[2048,4096]{1,0:T(8,128)(2,1)} %param.7) | copy-start | bytes 50331652
  45.4 30.4 %copy-start.1 = (s32[512,1024]{1,0:T(8,128)S(1)}, s32[512,1024]{1,0:T(8,128)}, u32[]{:S(2)}) copy-start(s32[512,1024]{1,0:T(8,128)} %param.9) | copy-start | bytes 6291460
  81.7 149.7 %reduce-scatter.2.cloned.1.call-start = ((), (), s32[]{:S(2)}) async-start(), calls=%async_computation.2 | async-start | bytes 4718592 | tf_op jit(solution)/shard_map/reduce_scatter | solution.py:42
Sparse Core Ops, SparseCore 0:
  81.8 84.7 all-reduce.2
  181.0 50.2 reduce-scatter.1
where the time goes:
time: 282 us; the launch traced here: 281 us
  waiting for transfers between devices  135 us (48%)
  blocking collectives  53.4 us (19%)
  matrix products  50.6 us (18%)
  other arithmetic  20.2 us (7%)
  between operations  16.6 us (6%)
  local copies, waits for them, and re-layouts  5.23 us (2%)
    psum x1, waiting for transfers between devices, local(): summed = lax.psum(partial_value.astype(jnp.bfloat16), 'sample')  84.7 us
    reduce_scatter x1, waiting for transfers between devices, local(): lax.psum_scatter(whiten_maker(factor, summed).astype(jnp.bfloat16), 'land...  50.4 us
    psum x1, blocking collectives, local(): statistic = lax.psum(share, ('sample', 'landmark')) / LANDMARKS  39.4 us
    dot_general x1, matrix products, local(): lax.dot_general(embeddings, landmarks, (((1,), (1,)), ((), ())), preferre...  30.4 us
    dot_general x1, matrix products, whiten_maker(): lax.dot_general(factor, moments_half, (((0,), (1,)), ((), ())), preferred...  14.3 us
    psum x1, blocking collectives, local(): lax.psum((jnp.sum(live_rows * (1.0 - corpus)), jnp.sum(live_rows * corpus...  14.1 us
    reduce_sum x1, other arithmetic, local(): point_scale = lax.rsqrt(jnp.mean(wide_z * wide_z, axis=1) + 1e-06)  7.46 us
    dot_general x1, matrix products, local(): partial_value = jnp.dot(signs, weighted, preferred_element_type=jnp.float32)  5.88 us
  transfers between devices with their start and end apart: 2, of which 2 were waited for; matrix products, arithmetic and copies ran while one was open for 0% of the time, Pallas kernels for 0%

commit v1 on v0

v1 whole, which is shorter than its diff:
```python
import functools
import math

import jax
import jax.numpy as jnp
from jax import lax
from jax.experimental import pallas as pl
from jax.experimental.pallas import tpu as pltpu
from jax.sharding import PartitionSpec as P

VMEM_LIMIT = 40 * 1024 * 1024
L_CHUNKS = 4
P_SPLIT = 2
NT = (((1,), (1,)), ((), ()))


def row_stats_kernel(x_ref, flips_ref, scale_ref, signs_ref):
    x = x_ref[...].astype(jnp.float32)
    mean = jnp.sum(x * x, axis=1, keepdims=True) * (1.0 / x.shape[1])
    scale_ref[...] = lax.rsqrt(mean + 1e-06) * (0.5 / math.sqrt(x.shape[1]))
    signs_ref[...] = (2 * flips_ref[...] - 1).astype(jnp.bfloat16)


def row_stats(x, flips):
    rows, width = x.shape
    perms = flips.shape[0]
    steps = 8
    return pl.pallas_call(
        row_stats_kernel,
        grid=(steps,),
        in_specs=[
            pl.BlockSpec((rows // steps, width), lambda i: (i, 0)),
            pl.BlockSpec((perms // steps, rows), lambda i: (i, 0)),
        ],
        out_specs=[
            pl.BlockSpec((rows // steps, 1), lambda i: (i, 0)),
            pl.BlockSpec((perms // steps, rows), lambda i: (i, 0)),
        ],
        out_shape=[
            jax.ShapeDtypeStruct((rows, 1), jnp.float32),
            jax.ShapeDtypeStruct((perms, rows), jnp.bfloat16),
        ],
        compiler_params=pltpu.CompilerParams(vmem_limit_bytes=VMEM_LIMIT),
        cost_estimate=pl.CostEstimate(flops=2 * rows * width, bytes_accessed=rows * width * 2, transcendentals=0),
        name="row_stats",
    )(x, flips)


def moments_kernel(x_ref, z_ref, scale_ref, weight_ref, signs_ref, *outs):
    rows = x_ref.shape[0]
    z = z_ref[...]
    z32 = z.astype(jnp.float32)
    mean = jnp.sum(z32 * z32, axis=1, keepdims=True) * (1.0 / z.shape[1])
    point = jnp.broadcast_to(lax.rsqrt(mean + 1e-06), (z.shape[0], 128))
    point_row = jnp.transpose(point)[0:1, :]
    parts = []
    block = 256
    for r in range(0, rows, block):
        here = pl.ds(r, block)
        cross = lax.dot_general(x_ref[here, :], z, NT, preferred_element_type=jnp.float32)
        kern = jnp.exp(cross * scale_ref[here, :] * point_row)
        parts.append((weight_ref[here, :] * kern).astype(jnp.bfloat16))
    weighted = jnp.concatenate(parts, axis=0)
    at = 0
    for out in outs:
        here = pl.ds(at, out.shape[0])
        out[...] = jnp.dot(signs_ref[here, :], weighted, preferred_element_type=jnp.float32).astype(jnp.bfloat16)
        at += out.shape[0]


def moments_part(x, z, scale, weight, signs, first, count, sizes):
    rows, width = x.shape
    tile = 256
    per = count // tile
    perms = signs.shape[0]
    return pl.pallas_call(
        moments_kernel,
        grid=(per,),
        in_specs=[
            pl.BlockSpec((rows, width), lambda i: (0, 0)),
            pl.BlockSpec((tile, width), lambda i: (first // tile + i, 0)),
            pl.BlockSpec((rows, 1), lambda i: (0, 0)),
            pl.BlockSpec((rows, 1), lambda i: (0, 0)),
            pl.BlockSpec((perms, rows), lambda i: (0, 0)),
        ],
        out_specs=[pl.BlockSpec((size, tile), lambda i: (0, i)) for size in sizes],
        out_shape=[jax.ShapeDtypeStruct((size, count), jnp.bfloat16) for size in sizes],
        compiler_params=pltpu.CompilerParams(vmem_limit_bytes=VMEM_LIMIT),
        cost_estimate=pl.CostEstimate(
            flops=2 * rows * width * count + 2 * perms * rows * count,
            bytes_accessed=(rows + count) * width * 2,
            transcendentals=rows * count,
        ),
        name="moments",
    )(x, z, scale, weight, signs)


def whiten_kernel(table_ref, factor_ref, *refs):
    out = refs[-1]
    depth = refs[0].shape[1]
    total = None
    for i, part in enumerate(refs[:-1]):
        term = jnp.dot(part[...], factor_ref[pl.ds(i * depth, depth), :], preferred_element_type=jnp.float32)
        total = term if total is None else total + term
    out[0] = total.astype(jnp.bfloat16)


def whiten(table, factor, parts, blocks):
    depth, columns = factor.shape
    perms, piece = parts[0].shape
    count = table.shape[0]
    wide = columns // blocks
    return pl.pallas_call(
        whiten_kernel,
        grid_spec=pltpu.PrefetchScalarGridSpec(
            num_scalar_prefetch=1,
            grid=(count,),
            in_specs=[pl.BlockSpec((depth, wide), lambda i, t: (0, t[i]))]
            + [pl.BlockSpec((perms, piece), lambda i, t: (0, 0)) for _ in parts],
            out_specs=pl.BlockSpec((1, perms, wide), lambda i, t: (i, 0, 0)),
        ),
        out_shape=jax.ShapeDtypeStruct((count, perms, wide), jnp.bfloat16),
        compiler_params=pltpu.CompilerParams(vmem_limit_bytes=VMEM_LIMIT),
        cost_estimate=pl.CostEstimate(
            flops=2 * perms * depth * wide * count,
            bytes_accessed=depth * wide * count * 2,
            transcendentals=0,
        ),
        name="whiten",
    )(table, factor, *parts)


def finish_kernel(*refs):
    half = (len(refs) - 2) // 2
    out, share = refs[-2:]
    at = 0
    for i in range(half):
        a = refs[2 * i][...].astype(jnp.float32) + refs[2 * i + 1][...].astype(jnp.float32)
        here = pl.ds(at, a.shape[0])
        wide = jnp.transpose(a)
        out[:, here] = wide.astype(jnp.bfloat16)
        share[:, here] = jnp.broadcast_to(jnp.sum(wide * wide, axis=0, keepdims=True), (8, a.shape[0]))
        at += a.shape[0]


def finish(pairs):
    flat = [a for pair in pairs for a in pair]
    perms = sum(pair[0].shape[0] for pair in pairs)
    wide = flat[0].shape[1]
    return pl.pallas_call(
        finish_kernel,
        out_shape=[
            jax.ShapeDtypeStruct((wide, perms), jnp.bfloat16),
            jax.ShapeDtypeStruct((8, perms), jnp.float32),
        ],
        compiler_params=pltpu.CompilerParams(vmem_limit_bytes=VMEM_LIMIT),
        cost_estimate=pl.CostEstimate(flops=4 * perms * wide, bytes_accessed=perms * wide * 6, transcendentals=0),
        name="finish",
    )(*flat)


def pick(options, here):
    items = sorted(options.items())
    value = items[0][1]
    for position, array in items[1:]:
        value = jnp.where(here == position, array, value)
    return value


class Chain:
    def __init__(self, size, here, pieces):
        self.size, self.here, self.pieces = size, here, pieces
        self.right, self.left = [], []

    def steps(self):
        return len(self.pieces) + self.size - 2

    def _send(self, t, recv, mirror):
        n, count = self.size, len(self.pieces)
        options = {}
        for r in range(n - 1):
            if 0 <= t - r < count:
                options[n - 1 - r if mirror else r] = self.pieces[t - r]
        own = pick(options, self.here)
        if t > 0:
            own = (own.astype(jnp.float32) + recv[t - 1].astype(jnp.float32)).astype(jnp.bfloat16)
        return own

    def step(self, t):
        n = self.size
        to_right = self._send(t, self.right, False)
        to_left = self._send(t, self.left, True)
        self.right.append(lax.ppermute(to_right, "sample", [(i, i + 1) for i in range(n - 1)]))
        self.left.append(lax.ppermute(to_left, "sample", [(i + 1, i) for i in range(n - 1)]))

    def total(self, i):
        n = self.size
        total = self.pieces[i].astype(jnp.float32)
        from_left = {z: self.right[i + z - 1] for z in range(1, n)}
        from_right = {z: self.left[i + n - 2 - z] for z in range(n - 1)}
        total = total + pick(from_left, self.here).astype(jnp.float32)
        total = total + pick(from_right, self.here).astype(jnp.float32)
        return total.astype(jnp.bfloat16)


def exchange_sum(value, axis, size):
    total = value
    for shift in range(1, size):
        total = total + lax.ppermute(value, axis, [(i, (i + shift) % size) for i in range(size)])
    return total


def make_local(mesh):
    n_sample = mesh.shape["sample"]
    n_landmark = mesh.shape["landmark"]
    bits = n_landmark.bit_length() - 1

    def order_of(core):
        rest = list(range(1, bits))
        return [0] + (rest if core == 0 else rest[::-1])

    def place_of(core, q):
        return sum(((q >> t) & 1) << bit for t, bit in enumerate(order_of(core)))

    def local(embeddings, landmarks, factor, flips, labels, counts):
        slot_count = embeddings.shape[0]
        slab_total = counts.shape[0]
        here = lax.axis_index("sample")
        spot = lax.axis_index("landmark")
        own_count = jnp.sum(jnp.where(jnp.arange(slab_total, dtype=jnp.int32) == here, counts, 0))
        live_rows = (jnp.arange(slot_count, dtype=jnp.int32) < own_count).astype(jnp.float32)
        corpus = labels.astype(jnp.float32)
        own_pair = jnp.stack([jnp.sum(live_rows * (1.0 - corpus)), jnp.sum(live_rows * corpus)])
        pair = exchange_sum(own_pair, "sample", n_sample)
        count_a, count_b = pair[0], pair[1]
        balance = jnp.sqrt(count_a * count_b / (count_a + count_b))
        row_weight = live_rows * ((1.0 - corpus) / count_a - corpus / count_b) * balance
        row_weight = row_weight[:, None]
        row_scale, signs = row_stats(embeddings, flips)

        perms = flips.shape[0]
        points = landmarks.shape[0]
        chunk = points // L_CHUNKS
        sizes = [perms // P_SPLIT] * P_SPLIT
        chains = [Chain(n_sample, here, []) for _ in sizes]
        for k in range(L_CHUNKS):
            outs = moments_part(embeddings, landmarks, row_scale, row_weight, signs, k * chunk, chunk, sizes)
            for chain, out in zip(chains, outs):
                chain.pieces.append(out)

        core = spot % 2
        half = n_landmark // 2
        sent_places = [1 + 2 * q for q in range(half)]
        kept_places = [2 * q for q in range(half)]

        def table_of(places, order_core):
            zero = jnp.array([place_of(0, q) for q in places], jnp.int32)
            one = jnp.array([place_of(1, q) for q in places], jnp.int32)
            return jnp.bitwise_xor(jnp.where(order_core == 0, zero, one), spot.astype(jnp.int32))

        kept_order = sorted(kept_places, key=lambda q: [-((q >> t) & 1) for t in range(1, bits)])
        sent_order = [q + 1 for q in kept_order]
        kept_table = table_of(kept_order, core)
        sent_table = table_of(sent_order, 1 - core)

        def pairs_of(t):
            return [(m, m ^ (1 << order_of(m % 2)[t])) for m in range(n_landmark)]

        pairs = []
        for chain in chains:
            for t in range(chain.steps()):
                chain.step(t)
            totals = [chain.total(i) for i in range(len(chain.pieces))]
            sent = whiten(sent_table, factor, totals, n_landmark)
            recv = lax.ppermute(sent, "landmark", pairs_of(0))
            kept = whiten(kept_table, factor, totals, n_landmark)
            for t in range(1, bits):
                middle = kept.shape[0] // 2
                both = lambda a, b: (a.astype(jnp.float32) + b.astype(jnp.float32)).astype(jnp.bfloat16)
                sent = both(kept[:middle], recv[:middle])
                kept = both(kept[middle:], recv[middle:])
                recv = lax.ppermute(sent, "landmark", pairs_of(t))
            pairs.append((kept[0], recv[0]))
        whitened, share = finish(pairs)
        share = exchange_sum(share[0], "landmark", n_landmark)
        share = exchange_sum(share, "sample", n_sample)
        total_points = points * n_landmark
        return whitened, share / total_points

    return local


def solution(mesh):
    return jax.shard_map(
        make_local(mesh),
        mesh=mesh,
        in_specs=(
            P("sample", None),
            P("landmark", None),
            P("landmark", "sample"),
            P(None, "sample"),
            P("sample"),
            P(),
        ),
        out_specs=(P(("sample", "landmark"), None), P()),
        check_vma=False,
    )
```

time: 282 us -> 205 us (0.73)
  waiting for transfers between devices: 135 us -> 34.9 us
  starting transfers between devices: 0.26 us -> 82.6 us
  Pallas kernels: 0 us -> 57.8 us
  blocking collectives: 53.4 us -> 0 us
  matrix products: 50.6 us -> 0 us
  between operations: 16.6 us -> 3.88 us
  other arithmetic: 20.2 us -> 15.6 us
  local copies, waits for them, and re-layouts: 5.23 us -> 9.19 us
    psum x1 -> x0, waiting for transfers between devices: 84.7 us -> none  [local(): summed = lax.psum(partial_value.astype(jnp.bfloat16), 'sample')]
    ppermute x0 -> x43, starting transfers between devices: none -> 82.6 us  [the longest x12 42.6 us: step(): lax.ppermute(to_right, 'sample', [(i, i + 1) for i in range(n - 1)])]
    pallas_call x0 -> x10, Pallas kernels: none -> 57.8 us  [the longest x4 29.2 us: moments_part(): pl.pallas_call(moments_kernel, grid=(per,), in_specs=[pl.BlockSpec((rows,...]
    psum x2 -> x0, blocking collectives: 53.4 us -> none  [the longest x1 39.4 us: local(): statistic = lax.psum(share, ('sample', 'landmark')) / LANDMARKS]
    dot_general x3 -> x0, matrix products: 50.6 us -> none  [the longest x1 30.4 us: local(): lax.dot_general(embeddings, landmarks, (((1,), (1,)), ((), ())), preferre...]
    reduce_scatter x1 -> x0, waiting for transfers between devices: 50.4 us -> none  [local(): lax.psum_scatter(whiten_maker(factor, summed).astype(jnp.bfloat16), 'land...]
    ppermute x0 -> x43, waiting for transfers between devices: none -> 34.9 us  [the longest x4 17.8 us: local(): recv = lax.ppermute(sent, 'landmark', pairs_of(t))]
    reduce_sum x5 -> x2, other arithmetic: 17.1 us -> 3.26 us  [the longest x1 1.97 us: local(): jnp.sum(live_rows * (1.0 - corpus))]
  transfers between devices with their start and end apart: 2 -> 43, of which waited for: 2 -> 15; matrix products, arithmetic and copies ran while one was open for 0% -> 3% of each run, Pallas kernels for 0% -> 21%
where the time goes in v1:
time: 205 us; the launch traced here: 204 us
  starting transfers between devices  82.6 us (40%)
  Pallas kernels  57.8 us (28%)
  waiting for transfers between devices  34.9 us (17%)
  other arithmetic  15.6 us (8%)
  local copies, waits for them, and re-layouts  9.19 us (4%)
  between operations  3.88 us (2%)
    ppermute x12, starting transfers between devices, step(): lax.ppermute(to_right, 'sample', [(i, i + 1) for i in range(n - 1)])  42.6 us
    pallas_call x4, Pallas kernels, moments_part(): pl.pallas_call(moments_kernel, grid=(per,), in_specs=[pl.BlockSpec((rows,...  29.2 us
    pallas_call x4, Pallas kernels, whiten(): pl.pallas_call(whiten_kernel, grid_spec=pltpu.PrefetchScalarGridSpec(num_...  25 us
    ppermute x13, starting transfers between devices, exchange_sum(): lax.ppermute(value, axis, [(i, (i + shift) % size) for i in range(size)])  19.1 us
    ppermute x4, waiting for transfers between devices, local(): recv = lax.ppermute(sent, 'landmark', pairs_of(t))  17.8 us
    ppermute x12, starting transfers between devices, step(): lax.ppermute(to_left, 'sample', [(i + 1, i) for i in range(n - 1)])  15.7 us
    ppermute x12, waiting for transfers between devices, step(): lax.ppermute(to_left, 'sample', [(i + 1, i) for i in range(n - 1)])  12.9 us
    unnamed x14, local copies, waits for them, and re-layouts  8.38 us
  transfers between devices with their start and end apart: 43, of which 15 were waited for; matrix products, arithmetic and copies ran while one was open for 3% of the time, Pallas kernels for 21%

profile of v1, /device:TPU:0, one launch (start us, length us, event | category | flops | bytes accessed | tf_op | source)
XLA Modules:
  0.0 204.0 jit_solution(2412878738835258732)
XLA Ops:
  5.2 3.0 %collective-permute-start = (f32[2]{0:T(128)S(1)}, f32[2]{0:T(128)S(1)}, u32[]{:S(2)}, u32[]{:S(2)}) collective-permute-start(f32[2]{0:T(128)S(1)} %pad_maximum_fusion), channel_id=1, source_target_pairs={{0,8},{8,16},{16,24},{24,0},{1,9},{9,17},{17,25},{25,1},{2,10},{10... | collective-permute-start | bytes 32 | tf_op jit(solution)/shard_map/ppermute | solution.py:209
  12.2 3.4 %copy-done = bf16[1024,4096]{1,0:T(8,128)(2,1)S(1)} copy-done((bf16[1024,4096]{1,0:T(8,128)(2,1)S(1)}, bf16[1024,4096]{1,0:T(8,128)(2,1)}, u32[]{:S(2)}) %copy-start) | copy-done | bytes 8388632
  27.1 3.4 %copy-done.1 = bf16[1024,4096]{1,0:T(8,128)(2,1)S(1)} copy-done((bf16[1024,4096]{1,0:T(8,128)(2,1)S(1)}, bf16[1024,4096]{1,0:T(8,128)(2,1)}, u32[]{:S(2)}) %copy-start.1) | copy-done | bytes 8388632
  30.4 7.3 %moments.5 = (bf16[256,512]{1,0:T(8,128)(2,1)S(1)}, bf16[256,512]{1,0:T(8,128)(2,1)S(1)}) custom-call(bf16[1024,4096]{1,0:T(8,128)(2,1)S(1)} %copy-done.1, bf16[2048,4096]{1,0:T(8,128)(2,1)} %z_ref.7, f32[1024,1]{1,0:T(8,128)S(1)} %get-tuple-element.14.scale_ref, f32[1024,1]{1,0:T(8,128)S(1)} %copy.12.weight_ref, ...), custom_call_target="tpu_custom_call" | custom-call | flops 4831838208 | bytes 12582912 | tf_op jit(solution)/shard_map/moments/pallas_call | solution.py:76
  37.8 7.3 %moments.4 = (bf16[256,512]{1,0:T(8,128)(2,1)S(1)}, bf16[256,512]{1,0:T(8,128)(2,1)S(1)}) custom-call(bf16[1024,4096]{1,0:T(8,128)(2,1)S(1)} %copy-done.1, bf16[2048,4096]{1,0:T(8,128)(2,1)} %z_ref.7, f32[1024,1]{1,0:T(8,128)S(1)} %get-tuple-element.14.scale_ref, f32[1024,1]{1,0:T(8,128)S(1)} %copy.12.weight_ref, ...), custom_call_target="tpu_custom_call" | custom-call | flops 4831838208 | bytes 12582912 | tf_op jit(solution)/shard_map/moments/pallas_call | solution.py:76
  49.0 7.3 %moments.6 = (bf16[256,512]{1,0:T(8,128)(2,1)S(1)}, bf16[256,512]{1,0:T(8,128)(2,1)S(1)}) custom-call(bf16[1024,4096]{1,0:T(8,128)(2,1)S(1)} %copy-done.1, bf16[2048,4096]{1,0:T(8,128)(2,1)} %z_ref.7, f32[1024,1]{1,0:T(8,128)S(1)} %get-tuple-element.14.scale_ref, f32[1024,1]{1,0:T(8,128)S(1)} %copy.12.weight_ref, ...), custom_call_target="tpu_custom_call" | custom-call | flops 4831838208 | bytes 12582912 | tf_op jit(solution)/shard_map/moments/pallas_call | solution.py:76
  56.3 4.6 %collective-permute-start.3 = (bf16[256,512]{1,0:T(8,128)(2,1)S(1)}, bf16[256,512]{1,0:T(8,128)(2,1)S(1)}, u32[]{:S(2)}, u32[]{:S(2)}) collective-permute-start(bf16[256,512]{1,0:T(8,128)(2,1)S(1)} %get-tuple-element.16), channel_id=1, source_target_pairs={{0,8},{8,16},{16,24},{1,9},{9,17},{17,25},{2,10},{10,18},{18,26},{... | collective-permute-start | bytes 786440 | tf_op jit(solution)/shard_map/ppermute | solution.py:193
  62.2 7.3 %moments.7 = (bf16[256,512]{1,0:T(8,128)(2,1)S(1)}, bf16[256,512]{1,0:T(8,128)(2,1)S(1)}) custom-call(bf16[1024,4096]{1,0:T(8,128)(2,1)S(1)} %copy-done.1, bf16[2048,4096]{1,0:T(8,128)(2,1)} %z_ref.7, f32[1024,1]{1,0:T(8,128)S(1)} %get-tuple-element.14.scale_ref, f32[1024,1]{1,0:T(8,128)S(1)} %copy.12.weight_ref, ...), custom_call_target="tpu_custom_call" | custom-call | flops 4831838208 | bytes 12582912 | tf_op jit(solution)/shard_map/moments/pallas_call | solution.py:76
  69.7 4.5 %collective-permute-start.19 = (bf16[256,512]{1,0:T(8,128)(2,1)S(1)}, bf16[256,512]{1,0:T(8,128)(2,1)S(1)}, u32[]{:S(2)}, u32[]{:S(2)}) collective-permute-start(bf16[256,512]{1,0:T(8,128)(2,1)S(1)} %get-tuple-element.54), channel_id=1, source_target_pairs={{0,8},{8,16},{16,24},{1,9},{9,17},{17,25},{2,10},{10,18},{18,26},{... | collective-permute-start | bytes 786440 | tf_op jit(solution)/shard_map/ppermute | solution.py:193
  75.8 4.6 %collective-permute-start.4 = (bf16[256,512]{1,0:T(8,128)(2,1)S(1)}, bf16[256,512]{1,0:T(8,128)(2,1)S(1)}, u32[]{:S(2)}, u32[]{:S(2)}) collective-permute-start(bf16[256,512]{1,0:T(8,128)(2,1)S(1)} %get-tuple-element.58), channel_id=1, source_target_pairs={{0,8},{8,16},{16,24},{1,9},{9,17},{17,25},{2,10},{10,18},{18,26},{... | collective-permute-start | bytes 786440 | tf_op jit(solution)/shard_map/ppermute | solution.py:193
  83.4 3.3 %collective-permute-start.20 = (bf16[256,512]{1,0:T(8,128)(2,1)S(1)}, bf16[256,512]{1,0:T(8,128)(2,1)S(1)}, u32[]{:S(2)}, u32[]{:S(2)}) collective-permute-start(bf16[256,512]{1,0:T(8,128)(2,1)S(1)} %get-tuple-element.46), channel_id=1, source_target_pairs={{0,8},{8,16},{16,24},{1,9},{9,17},{17,25},{2,10},{10,18},{18,26},{... | collective-permute-start | bytes 786440 | tf_op jit(solution)/shard_map/ppermute | solution.py:193
  89.8 3.0 %collective-permute-start.5 = (bf16[256,512]{1,0:T(8,128)(2,1)S(1)}, bf16[256,512]{1,0:T(8,128)(2,1)S(1)}, u32[]{:S(2)}, u32[]{:S(2)}) collective-permute-start(bf16[256,512]{1,0:T(8,128)(2,1)S(1)} %get-tuple-element.50), channel_id=1, source_target_pairs={{0,8},{8,16},{16,24},{1,9},{9,17},{17,25},{2,10},{10,18},{18,26},{... | collective-permute-start | bytes 786440 | tf_op jit(solution)/shard_map/ppermute | solution.py:193
  100.2 3.2 %collective-permute-done.8 = bf16[256,512]{1,0:T(8,128)(2,1)S(1)} collective-permute-done((bf16[256,512]{1,0:T(8,128)(2,1)S(1)}, bf16[256,512]{1,0:T(8,128)(2,1)S(1)}, u32[]{:S(2)}, u32[]{:S(2)}) %collective-permute-start.8) | collective-permute-done | bytes 262176 | tf_op jit(solution)/shard_map/ppermute | solution.py:194
  104.9 4.6 %collective-permute-start.9 = (bf16[256,512]{1,0:T(8,128)(2,1)S(1)}, bf16[256,512]{1,0:T(8,128)(2,1)S(1)}, u32[]{:S(2)}, u32[]{:S(2)}) collective-permute-start(bf16[256,512]{1,0:T(8,128)(2,1)S(1)} %get-tuple-element.48), channel_id=1, source_target_pairs={{0,8},{8,16},{16,24},{1,9},{9,17},{17,25},{2,10},{10,18},{18,26},{... | collective-permute-start | bytes 786440 | tf_op jit(solution)/shard_map/ppermute | solution.py:193
  115.2 4.4 %collective-permute-start.11 = (bf16[256,512]{1,0:T(8,128)(2,1)S(1)}, bf16[256,512]{1,0:T(8,128)(2,1)S(1)}, u32[]{:S(2)}, u32[]{:S(2)}) collective-permute-start(bf16[256,512]{1,0:T(8,128)(2,1)S(1)} %get-tuple-element.56), channel_id=1, source_target_pairs={{0,8},{8,16},{16,24},{1,9},{9,17},{17,25},{2,10},{10,18},{18,26},{... | collective-permute-start | bytes 786440 | tf_op jit(solution)/shard_map/ppermute | solution.py:193
  121.5 4.1 %collective-permute-start.28 = (bf16[256,512]{1,0:T(8,128)(2,1)S(1)}, bf16[256,512]{1,0:T(8,128)(2,1)S(1)}, u32[]{:S(2)}, u32[]{:S(2)}) collective-permute-start(bf16[256,512]{1,0:T(8,128)(2,1)S(1)} %get-tuple-element.60), channel_id=1, source_target_pairs={{0,8},{8,16},{16,24},{1,9},{9,17},{17,25},{2,10},{10,18},{18,26},{... | collective-permute-start | bytes 786440 | tf_op jit(solution)/shard_map/ppermute | solution.py:193
  128.6 3.1 %collective-permute-start.13 = (bf16[256,512]{1,0:T(8,128)(2,1)S(1)}, bf16[256,512]{1,0:T(8,128)(2,1)S(1)}, u32[]{:S(2)}, u32[]{:S(2)}) collective-permute-start(bf16[256,512]{1,0:T(8,128)(2,1)S(1)} %get-tuple-element.62), channel_id=1, source_target_pairs={{0,8},{8,16},{16,24},{1,9},{9,17},{17,25},{2,10},{10,18},{18,26},{... | collective-permute-start | bytes 786440 | tf_op jit(solution)/shard_map/ppermute | solution.py:193
  134.6 6.0 %whiten.7 = bf16[4,256,512]{2,1,0:T(8,128)(2,1)S(1)} custom-call(s32[4]{0:T(128)S(1)} %fusion.11.table_ref, bf16[2048,4096]{1,0:T(8,128)(2,1)} %factor_ref.7, bf16[256,512]{1,0:T(8,128)(2,1)S(1)} %get-tuple-element.37.refs_0_, bf16[256,512]{1,0:T(8,128)(2,1)S(1)} %get-tuple-element.36.refs_1_, bf16[256,512]{1,0:T(8,128)(2,1)S(1)} %get-tuple-element.35.refs_2_, ...), custom_call_target="tpu_custom_call" | custom-call | flops 2147483648 | bytes 8388608 | tf_op jit(solution)/shard_map/whiten/pallas_call | solution.py:113
  141.5 6.8 %whiten.5 = bf16[4,256,512]{2,1,0:T(8,128)(2,1)} custom-call(s32[4]{0:T(128)S(1)} %fusion.11.table_ref, bf16[2048,4096]{1,0:T(8,128)(2,1)} %factor_ref.7, bf16[256,512]{1,0:T(8,128)(2,1)S(1)} %get-tuple-element.43.refs_0_, bf16[256,512]{1,0:T(8,128)(2,1)S(1)} %get-tuple-element.42.refs_1_, bf16[256,512]{1,0:T(8,128)(2,1)S(1)} %get-tuple-element.41.refs_2_, ...), custom_call_target="tpu_custom_call" | custom-call | flops 2147483648 | bytes 8388608 | tf_op jit(solution)/shard_map/whiten/pallas_call | solution.py:113
  148.9 6.0 %whiten.6 = bf16[4,256,512]{2,1,0:T(8,128)(2,1)S(1)} custom-call(s32[4]{0:T(128)S(1)} %fusion.10.table_ref, bf16[2048,4096]{1,0:T(8,128)(2,1)} %factor_ref.7, bf16[256,512]{1,0:T(8,128)(2,1)S(1)} %get-tuple-element.37.refs_0_, bf16[256,512]{1,0:T(8,128)(2,1)S(1)} %get-tuple-element.36.refs_1_, bf16[256,512]{1,0:T(8,128)(2,1)S(1)} %get-tuple-element.35.refs_2_, ...), custom_call_target="tpu_custom_call" | custom-call | flops 2147483648 | bytes 8388608 | tf_op jit(solution)/shard_map/whiten/pallas_call | solution.py:113
  154.9 6.0 %whiten.4 = bf16[4,256,512]{2,1,0:T(8,128)(2,1)S(1)} custom-call(s32[4]{0:T(128)S(1)} %fusion.10.table_ref, bf16[2048,4096]{1,0:T(8,128)(2,1)} %factor_ref.7, bf16[256,512]{1,0:T(8,128)(2,1)S(1)} %get-tuple-element.43.refs_0_, bf16[256,512]{1,0:T(8,128)(2,1)S(1)} %get-tuple-element.42.refs_1_, bf16[256,512]{1,0:T(8,128)(2,1)S(1)} %get-tuple-element.41.refs_2_, ...), custom_call_target="tpu_custom_call" | custom-call | flops 2147483648 | bytes 8388608 | tf_op jit(solution)/shard_map/whiten/pallas_call | solution.py:113
  166.1 5.6 %collective-permute-done.31 = bf16[2,256,512]{2,1,0:T(8,128)(2,1)S(1)} collective-permute-done((bf16[2,256,512]{2,1,0:T(8,128)(2,1)S(1)}, bf16[2,256,512]{2,1,0:T(8,128)(2,1)S(1)}, u32[]{:S(2)}, u32[]{:S(2)}) %collective-permute-start.31) | collective-permute-done | bytes 524320 | tf_op jit(solution)/shard_map/ppermute | solution.py:282
  173.1 7.0 %collective-permute-done.16 = bf16[2,256,512]{2,1,0:T(8,128)(2,1)S(1)} collective-permute-done((bf16[2,256,512]{2,1,0:T(8,128)(2,1)S(1)}, bf16[2,256,512]{2,1,0:T(8,128)(2,1)S(1)}, u32[]{:S(2)}, u32[]{:S(2)}) %collective-permute-start.16) | collective-permute-done | bytes 524320 | tf_op jit(solution)/shard_map/ppermute | solution.py:282
  181.6 5.2 %collective-permute-done.17 = bf16[1,256,512]{2,1,0:T(8,128)(2,1)S(1)} collective-permute-done((bf16[1,256,512]{2,1,0:T(8,128)(2,1)S(1)}, bf16[1,256,512]{2,1,0:T(8,128)(2,1)S(1)}, u32[]{:S(2)}, u32[]{:S(2)}) %collective-permute-start.17) | collective-permute-done | bytes 262176 | tf_op jit(solution)/shard_map/ppermute | solution.py:282
  (114 shorter events, 79.0 us)
Async XLA Ops:
  5.2 14.3 %collective-permute-start = (f32[2]{0:T(128)S(1)}, f32[2]{0:T(128)S(1)}, u32[]{:S(2)}, u32[]{:S(2)}) collective-permute-start(f32[2]{0:T(128)S(1)} %pad_maximum_fusion), channel_id=1, source_target_pairs={{0,8},{8,16},{16,24},{24,0},{1,9},{9,17},{17,25},{25,1},{2,10},{10... | collective-permute-start | bytes 32 | tf_op jit(solution)/shard_map/ppermute | solution.py:209
  8.3 11.3 %collective-permute-start.1 = (f32[2]{0:T(128)S(1)}, f32[2]{0:T(128)S(1)}, u32[]{:S(2)}, u32[]{:S(2)}) collective-permute-start(f32[2]{0:T(128)S(1)} %pad_maximum_fusion), channel_id=1, source_target_pairs={{0,16},{8,24},{16,0},{24,8},{1,17},{9,25},{17,1},{25,9},{2,18},{10... | collective-permute-start | bytes 32 | tf_op jit(solution)/shard_map/ppermute | solution.py:209
  45.1 24.5 %collective-permute-start.18 = (bf16[256,512]{1,0:T(8,128)(2,1)S(1)}, bf16[256,512]{1,0:T(8,128)(2,1)S(1)}, u32[]{:S(2)}, u32[]{:S(2)}) collective-permute-start(bf16[256,512]{1,0:T(8,128)(2,1)S(1)} %get-tuple-element.20), channel_id=1, source_target_pairs={{0,8},{8,16},{16,24},{1,9},{9,17},{17,25},{2,10},{10,18},{18,26},{... | collective-permute-start | bytes 786440 | tf_op jit(solution)/shard_map/ppermute | solution.py:193
  47.7 21.9 %collective-permute-start.21 = (bf16[256,512]{1,0:T(8,128)(2,1)S(1)}, bf16[256,512]{1,0:T(8,128)(2,1)S(1)}, u32[]{:S(2)}, u32[]{:S(2)}) collective-permute-start(bf16[256,512]{1,0:T(8,128)(2,1)S(1)} %get-tuple-element.20), channel_id=1, source_target_pairs={{8,0},{16,8},{24,16},{9,1},{17,9},{25,17},{10,2},{18,10},{26,18},{... | collective-permute-start | bytes 786440 | tf_op jit(solution)/shard_map/ppermute | solution.py:194
  56.3 19.3 %collective-permute-start.3 = (bf16[256,512]{1,0:T(8,128)(2,1)S(1)}, bf16[256,512]{1,0:T(8,128)(2,1)S(1)}, u32[]{:S(2)}, u32[]{:S(2)}) collective-permute-start(bf16[256,512]{1,0:T(8,128)(2,1)S(1)} %get-tuple-element.16), channel_id=1, source_target_pairs={{0,8},{8,16},{16,24},{1,9},{9,17},{17,25},{2,10},{10,18},{18,26},{... | collective-permute-start | bytes 786440 | tf_op jit(solution)/shard_map/ppermute | solution.py:193
  60.9 14.7 %collective-permute-start.6 = (bf16[256,512]{1,0:T(8,128)(2,1)S(1)}, bf16[256,512]{1,0:T(8,128)(2,1)S(1)}, u32[]{:S(2)}, u32[]{:S(2)}) collective-permute-start(bf16[256,512]{1,0:T(8,128)(2,1)S(1)} %get-tuple-element.16), channel_id=1, source_target_pairs={{8,0},{16,8},{24,16},{9,1},{17,9},{25,17},{10,2},{18,10},{26,18},{... | collective-permute-start | bytes 786440 | tf_op jit(solution)/shard_map/ppermute | solution.py:194
  69.7 12.1 %collective-permute-start.19 = (bf16[256,512]{1,0:T(8,128)(2,1)S(1)}, bf16[256,512]{1,0:T(8,128)(2,1)S(1)}, u32[]{:S(2)}, u32[]{:S(2)}) collective-permute-start(bf16[256,512]{1,0:T(8,128)(2,1)S(1)} %get-tuple-element.54), channel_id=1, source_target_pairs={{0,8},{8,16},{16,24},{1,9},{9,17},{17,25},{2,10},{10,18},{18,26},{... | collective-permute-start | bytes 786440 | tf_op jit(solution)/shard_map/ppermute | solution.py:193
  75.8 12.2 %collective-permute-start.4 = (bf16[256,512]{1,0:T(8,128)(2,1)S(1)}, bf16[256,512]{1,0:T(8,128)(2,1)S(1)}, u32[]{:S(2)}, u32[]{:S(2)}) collective-permute-start(bf16[256,512]{1,0:T(8,128)(2,1)S(1)} %get-tuple-element.58), channel_id=1, source_target_pairs={{0,8},{8,16},{16,24},{1,9},{9,17},{17,25},{2,10},{10,18},{18,26},{... | collective-permute-start | bytes 786440 | tf_op jit(solution)/shard_map/ppermute | solution.py:193
  83.4 10.7 %collective-permute-start.20 = (bf16[256,512]{1,0:T(8,128)(2,1)S(1)}, bf16[256,512]{1,0:T(8,128)(2,1)S(1)}, u32[]{:S(2)}, u32[]{:S(2)}) collective-permute-start(bf16[256,512]{1,0:T(8,128)(2,1)S(1)} %get-tuple-element.46), channel_id=1, source_target_pairs={{0,8},{8,16},{16,24},{1,9},{9,17},{17,25},{2,10},{10,18},{18,26},{... | collective-permute-start | bytes 786440 | tf_op jit(solution)/shard_map/ppermute | solution.py:193
  86.6 10.0 %collective-permute-start.23 = (bf16[256,512]{1,0:T(8,128)(2,1)S(1)}, bf16[256,512]{1,0:T(8,128)(2,1)S(1)}, u32[]{:S(2)}, u32[]{:S(2)}) collective-permute-start(bf16[256,512]{1,0:T(8,128)(2,1)S(1)} %get-tuple-element.47), channel_id=1, source_target_pairs={{8,0},{16,8},{24,16},{9,1},{17,9},{25,17},{10,2},{18,10},{26,18},{... | collective-permute-start | bytes 786440 | tf_op jit(solution)/shard_map/ppermute | solution.py:194
  89.8 10.4 %collective-permute-start.5 = (bf16[256,512]{1,0:T(8,128)(2,1)S(1)}, bf16[256,512]{1,0:T(8,128)(2,1)S(1)}, u32[]{:S(2)}, u32[]{:S(2)}) collective-permute-start(bf16[256,512]{1,0:T(8,128)(2,1)S(1)} %get-tuple-element.50), channel_id=1, source_target_pairs={{0,8},{8,16},{16,24},{1,9},{9,17},{17,25},{2,10},{10,18},{18,26},{... | collective-permute-start | bytes 786440 | tf_op jit(solution)/shard_map/ppermute | solution.py:193
  92.8 10.6 %collective-permute-start.8 = (bf16[256,512]{1,0:T(8,128)(2,1)S(1)}, bf16[256,512]{1,0:T(8,128)(2,1)S(1)}, u32[]{:S(2)}, u32[]{:S(2)}) collective-permute-start(bf16[256,512]{1,0:T(8,128)(2,1)S(1)} %get-tuple-element.51), channel_id=1, source_target_pairs={{8,0},{16,8},{24,16},{9,1},{17,9},{25,17},{10,2},{18,10},{26,18},{... | collective-permute-start | bytes 786440 | tf_op jit(solution)/shard_map/ppermute | solution.py:194
  96.9 12.6 %collective-permute-start.24 = (bf16[256,512]{1,0:T(8,128)(2,1)S(1)}, bf16[256,512]{1,0:T(8,128)(2,1)S(1)}, u32[]{:S(2)}, u32[]{:S(2)}) collective-permute-start(bf16[256,512]{1,0:T(8,128)(2,1)S(1)} %get-tuple-element.44), channel_id=1, source_target_pairs={{0,8},{8,16},{16,24},{1,9},{9,17},{17,25},{2,10},{10,18},{18,26},{... | collective-permute-start | bytes 786440 | tf_op jit(solution)/shard_map/ppermute | solution.py:193
  98.9 10.6 %collective-permute-start.25 = (bf16[256,512]{1,0:T(8,128)(2,1)S(1)}, bf16[256,512]{1,0:T(8,128)(2,1)S(1)}, u32[]{:S(2)}, u32[]{:S(2)}) collective-permute-start(bf16[256,512]{1,0:T(8,128)(2,1)S(1)} %get-tuple-element.45), channel_id=1, source_target_pairs={{8,0},{16,8},{24,16},{9,1},{17,9},{25,17},{10,2},{18,10},{26,18},{... | collective-permute-start | bytes 786440 | tf_op jit(solution)/shard_map/ppermute | solution.py:194
  103.6 10.6 %collective-permute-start.10 = (bf16[256,512]{1,0:T(8,128)(2,1)S(1)}, bf16[256,512]{1,0:T(8,128)(2,1)S(1)}, u32[]{:S(2)}, u32[]{:S(2)}) collective-permute-start(bf16[256,512]{1,0:T(8,128)(2,1)S(1)} %get-tuple-element.49), channel_id=1, source_target_pairs={{8,0},{16,8},{24,16},{9,1},{17,9},{25,17},{10,2},{18,10},{26,18},{... | collective-permute-start | bytes 786440 | tf_op jit(solution)/shard_map/ppermute | solution.py:194
  104.9 10.1 %collective-permute-start.9 = (bf16[256,512]{1,0:T(8,128)(2,1)S(1)}, bf16[256,512]{1,0:T(8,128)(2,1)S(1)}, u32[]{:S(2)}, u32[]{:S(2)}) collective-permute-start(bf16[256,512]{1,0:T(8,128)(2,1)S(1)} %get-tuple-element.48), channel_id=1, source_target_pairs={{0,8},{8,16},{16,24},{1,9},{9,17},{17,25},{2,10},{10,18},{18,26},{... | collective-permute-start | bytes 786440 | tf_op jit(solution)/shard_map/ppermute | solution.py:193
  109.7 11.3 %collective-permute-start.26 = (bf16[256,512]{1,0:T(8,128)(2,1)S(1)}, bf16[256,512]{1,0:T(8,128)(2,1)S(1)}, u32[]{:S(2)}, u32[]{:S(2)}) collective-permute-start(bf16[256,512]{1,0:T(8,128)(2,1)S(1)} %get-tuple-element.52), channel_id=1, source_target_pairs={{0,8},{8,16},{16,24},{1,9},{9,17},{17,25},{2,10},{10,18},{18,26},{... | collective-permute-start | bytes 786440 | tf_op jit(solution)/shard_map/ppermute | solution.py:193
  111.6 9.8 %collective-permute-start.27 = (bf16[256,512]{1,0:T(8,128)(2,1)S(1)}, bf16[256,512]{1,0:T(8,128)(2,1)S(1)}, u32[]{:S(2)}, u32[]{:S(2)}) collective-permute-start(bf16[256,512]{1,0:T(8,128)(2,1)S(1)} %get-tuple-element.53), channel_id=1, source_target_pairs={{8,0},{16,8},{24,16},{9,1},{17,9},{25,17},{10,2},{18,10},{26,18},{... | collective-permute-start | bytes 786440 | tf_op jit(solution)/shard_map/ppermute | solution.py:194
  115.2 11.8 %collective-permute-start.11 = (bf16[256,512]{1,0:T(8,128)(2,1)S(1)}, bf16[256,512]{1,0:T(8,128)(2,1)S(1)}, u32[]{:S(2)}, u32[]{:S(2)}) collective-permute-start(bf16[256,512]{1,0:T(8,128)(2,1)S(1)} %get-tuple-element.56), channel_id=1, source_target_pairs={{0,8},{8,16},{16,24},{1,9},{9,17},{17,25},{2,10},{10,18},{18,26},{... | collective-permute-start | bytes 786440 | tf_op jit(solution)/shard_map/ppermute | solution.py:193
  121.5 11.5 %collective-permute-start.28 = (bf16[256,512]{1,0:T(8,128)(2,1)S(1)}, bf16[256,512]{1,0:T(8,128)(2,1)S(1)}, u32[]{:S(2)}, u32[]{:S(2)}) collective-permute-start(bf16[256,512]{1,0:T(8,128)(2,1)S(1)} %get-tuple-element.60), channel_id=1, source_target_pairs={{0,8},{8,16},{16,24},{1,9},{9,17},{17,25},{2,10},{10,18},{18,26},{... | collective-permute-start | bytes 786440 | tf_op jit(solution)/shard_map/ppermute | solution.py:193
  128.6 12.2 %collective-permute-start.13 = (bf16[256,512]{1,0:T(8,128)(2,1)S(1)}, bf16[256,512]{1,0:T(8,128)(2,1)S(1)}, u32[]{:S(2)}, u32[]{:S(2)}) collective-permute-start(bf16[256,512]{1,0:T(8,128)(2,1)S(1)} %get-tuple-element.62), channel_id=1, source_target_pairs={{0,8},{8,16},{16,24},{1,9},{9,17},{17,25},{2,10},{10,18},{18,26},{... | collective-permute-start | bytes 786440 | tf_op jit(solution)/shard_map/ppermute | solution.py:193
  140.7 20.3 %collective-permute-start.30 = (bf16[4,256,512]{2,1,0:T(8,128)(2,1)S(1)}, bf16[4,256,512]{2,1,0:T(8,128)(2,1)}, u32[]{:S(2)}, u32[]{:S(2)}) collective-permute-start(bf16[4,256,512]{2,1,0:T(8,128)(2,1)S(1)} %whiten.7), channel_id=1, source_target_pairs={{0,1},{1,0},{2,3},{3,2},{4,5},{5,4},{6,7},{7,6},{8,9},{9,8},{10,11... | collective-permute-start | bytes 3145736 | tf_op jit(solution)/shard_map/ppermute | solution.py:275
  148.4 15.5 %collective-permute-start.15 = (bf16[4,256,512]{2,1,0:T(8,128)(2,1)}, bf16[4,256,512]{2,1,0:T(8,128)(2,1)}, u32[]{:S(2)}, u32[]{:S(2)}) collective-permute-start(bf16[4,256,512]{2,1,0:T(8,128)(2,1)} %whiten.5), channel_id=1, source_target_pairs={{0,1},{1,0},{2,3},{3,2},{4,5},{5,4},{6,7},{7,6},{8,9},{9,8},{10,11... | collective-permute-start | bytes 3145736 | tf_op jit(solution)/shard_map/ppermute | solution.py:275
  165.4 14.7 %collective-permute-start.16 = (bf16[2,256,512]{2,1,0:T(8,128)(2,1)S(1)}, bf16[2,256,512]{2,1,0:T(8,128)(2,1)S(1)}, u32[]{:S(2)}, u32[]{:S(2)}) collective-permute-start(bf16[2,256,512]{2,1,0:T(8,128)(2,1)S(1)} %get-tuple-element.31), channel_id=1, source_target_pairs={{0,2},{1,5},{2,0},{3,7},{4,6},{5,1},{6,4},{7,3},{8,10},{9,13},{10,... | collective-permute-start | bytes 1572872 | tf_op jit(solution)/shard_map/ppermute | solution.py:282
  (26 other events, 290.2 us)

commit v2 on v0

v2 whole, which is shorter than its diff:
```python
import functools
import math

import jax
import jax.numpy as jnp
from jax import lax
from jax.experimental import pallas as pl
from jax.experimental.pallas import tpu as pltpu
from jax.sharding import PartitionSpec as P

VMEM_LIMIT = 14 * 1024 * 1024
TILE = 256
NT = (((1,), (1,)), ((), ()))


VMEM = pl.BlockSpec(memory_space=pltpu.VMEM)
SMEM = pl.BlockSpec(memory_space=pltpu.SMEM)
HBM = pl.BlockSpec(memory_space=pltpu.HBM)
ANY = pl.BlockSpec(memory_space=pl.ANY)


def in_hbm(x):
    return pltpu.with_memory_space_constraint(x, pltpu.HBM)


def call(kernel, name, out_shape, in_specs, args, flops=0, bytes_accessed=0, transcendentals=0, scratch=()):
    return pl.pallas_call(
        kernel,
        out_shape=out_shape,
        in_specs=in_specs,
        out_specs=jax.tree.map(lambda _: VMEM, out_shape),
        scratch_shapes=list(scratch),
        compiler_params=pltpu.CompilerParams(vmem_limit_bytes=VMEM_LIMIT),
        cost_estimate=pl.CostEstimate(
            flops=flops, bytes_accessed=bytes_accessed, transcendentals=transcendentals
        ),
        name=name,
    )(*args)


def slot_masks(labels, own_count, slots):
    live = slots < own_count
    return (live & (labels == 0)).astype(jnp.float32), (live & (labels != 0)).astype(jnp.float32)


def counts_kernel(here_ref, counts_ref, labels_ref, out_ref):
    own_count = counts_ref[here_ref[0]]
    shape = labels_ref.shape
    slots = lax.broadcasted_iota(jnp.int32, shape, 0) * shape[1] + lax.broadcasted_iota(jnp.int32, shape, 1)
    mask_a, mask_b = slot_masks(labels_ref[...], own_count, slots)
    first = lax.broadcasted_iota(jnp.int32, out_ref.shape[1:], 0) == 0
    pair = jnp.where(first, jnp.sum(mask_a), jnp.sum(mask_b))
    out_ref[...] = jnp.broadcast_to(pair[None], out_ref.shape)


def own_counts(here, counts, labels, copies):
    return call(
        counts_kernel,
        "own_counts",
        jax.ShapeDtypeStruct((copies, 8, 128), jnp.float32),
        [SMEM, SMEM, VMEM],
        (here, counts, labels.reshape(-1, 128)),
    )


def rows_kernel(parts, here_ref, counts_ref, x_ref, z_ref, flips_ref, labels_ref,
                held_ref, first_ref, scale_ref, signs_ref, mask_a_ref, mask_b_ref, flips_buf, x_sem, z_sem, f_sem):
    rows, width = x_ref.shape
    block = rows // parts

    def x_copy(i):
        here = pl.ds(i * block, block)
        return pltpu.make_async_copy(x_ref.at[here, :], held_ref.at[here, :], x_sem.at[i])

    flips_copy = pltpu.make_async_copy(flips_ref, flips_buf, f_sem)
    z_copy = pltpu.make_async_copy(z_ref.at[pl.ds(0, first_ref.shape[0]), :], first_ref, z_sem)
    for i in range(parts):
        x_copy(i).start()
    z_copy.start()
    flips_copy.start()
    own_count = counts_ref[here_ref[0]]
    for j in range(rows // 128):
        here = pl.ds(j * 128, 128)
        labels = jnp.transpose(jnp.broadcast_to(labels_ref[pl.ds(j, 1), :], (128, 128)))[:, 0:1]
        slots = j * 128 + lax.broadcasted_iota(jnp.int32, (128, 1), 0)
        mask_a_ref[here, :], mask_b_ref[here, :] = slot_masks(labels, own_count, slots)
    for i in range(parts):
        x_copy(i).wait()
        here = pl.ds(i * block, block)
        x = held_ref[here, :].astype(jnp.float32)
        mean = jnp.sum(x * x, axis=1, keepdims=True) * (1.0 / width)
        scale_ref[here, :] = lax.rsqrt(mean + 1e-06) * (0.5 / math.sqrt(width))
    flips_copy.wait()
    signs_ref[...] = (2 * flips_buf[...] - 1).astype(jnp.bfloat16)
    z_copy.wait()


def prepare_rows(here, counts, x, z, flips, labels):
    rows, width = x.shape
    perms = flips.shape[0]
    parts = 8
    column = jax.ShapeDtypeStruct((rows, 1), jnp.float32)
    return call(
        functools.partial(rows_kernel, parts),
        "prepare_rows",
        [
            pltpu.VMEM((rows, width), x.dtype),
            jax.ShapeDtypeStruct((TILE, width), z.dtype),
            column,
            jax.ShapeDtypeStruct((perms, rows), jnp.bfloat16),
            column,
            column,
        ],
        [SMEM, SMEM, HBM, HBM, HBM, VMEM],
        (here, counts, in_hbm(x), in_hbm(z), in_hbm(flips), labels.reshape(-1, 128)),
        flops=3 * rows * width,
        bytes_accessed=(rows + TILE) * width * 2 + perms * rows * 4,
        scratch=[
            pltpu.VMEM(flips.shape, flips.dtype),
            pltpu.SemaphoreType.DMA((parts,)),
            pltpu.SemaphoreType.DMA,
            pltpu.SemaphoreType.DMA,
        ],
    )


def moments_kernel(following, after, pair_ref, x_ref, z_ref, scale_ref, signs_ref, mask_a_ref, mask_b_ref, z_all_ref,
                   *rest):
    out_ref, *rest = rest[after:]
    rows, width = x_ref.shape
    if following is not None:
        next_ref, sem = rest
        next_copy = pltpu.make_async_copy(z_all_ref.at[pl.ds(following, TILE), :], next_ref, sem)
        next_copy.start()
    pair = jnp.sum(pair_ref[...], axis=0)
    count_a, count_b = pair[0:1, 0:1], pair[1:2, 0:1]
    balance = jnp.sqrt(count_a * count_b / (count_a + count_b))
    weight_a, weight_b = balance / count_a, balance / count_b
    z = z_ref[...]
    z32 = z.astype(jnp.float32)
    mean = jnp.sum(z32 * z32, axis=1, keepdims=True) * (1.0 / width)
    point = jnp.broadcast_to(lax.rsqrt(mean + 1e-06), (TILE, 128))
    point_row = jnp.transpose(point)[0:1, :]
    cross = lax.dot_general(x_ref[...], z, NT, preferred_element_type=jnp.float32)
    kern = jnp.exp(cross * scale_ref[...] * point_row)
    weight = mask_a_ref[...] * weight_a - mask_b_ref[...] * weight_b
    weighted = (weight * kern).astype(jnp.bfloat16)
    out_ref[...] = jnp.dot(signs_ref[...], weighted, preferred_element_type=jnp.float32).astype(jnp.bfloat16)
    if following is not None:
        next_copy.wait()


def moments_part(pair, x, z, scale, signs, mask_a, mask_b, z_all, following, after):
    rows, width = x.shape
    perms = signs.shape[0]
    out_shape = [jax.ShapeDtypeStruct((perms, TILE), jnp.bfloat16)]
    scratch = []
    if following is not None:
        out_shape.append(jax.ShapeDtypeStruct((TILE, width), z.dtype))
        scratch.append(pltpu.SemaphoreType.DMA)
    return call(
        functools.partial(moments_kernel, following, len(after)),
        "moments",
        out_shape,
        [VMEM] * 7 + [HBM] + [ANY] * len(after),
        (pair, x, z, scale, signs, mask_a, mask_b, in_hbm(z_all), *after),
        flops=2 * rows * width * TILE + 2 * perms * rows * TILE,
        bytes_accessed=TILE * width * 2,
        transcendentals=rows * TILE,
        scratch=scratch,
    )


def whiten_kernel(table_ref, factor_ref, *refs):
    out = refs[-1]
    moments = jnp.concatenate([part[...] for part in refs[:-1]], axis=1)
    wide = out.shape[2]
    for i in range(out.shape[0]):
        here = pl.ds(pl.multiple_of(table_ref[i] * wide, wide), wide)
        out[i] = jnp.dot(moments, factor_ref[:, here], preferred_element_type=jnp.float32).astype(jnp.bfloat16)


def whiten(table, factor, parts, blocks):
    depth, columns = factor.shape
    perms = parts[0].shape[0]
    count = table.shape[0]
    wide = columns // blocks
    return call(
        whiten_kernel,
        "whiten",
        jax.ShapeDtypeStruct((count, perms, wide), jnp.bfloat16),
        [SMEM] + [VMEM] * (1 + len(parts)),
        (table, factor, *parts),
        flops=2 * perms * depth * wide * count,
        bytes_accessed=depth * wide * count * 2,
    )


def finish_kernel(a_ref, b_ref, out_ref, share_ref):
    wide = jnp.transpose(a_ref[...].astype(jnp.float32) + b_ref[...].astype(jnp.float32))
    out_ref[...] = wide.astype(jnp.bfloat16)
    share = jnp.sum(wide * wide, axis=0, keepdims=True)
    for j in range(share_ref.shape[1]):
        row = share[:, j * 128:(j + 1) * 128]
        share_ref[:, j, :] = jnp.broadcast_to(row, (share_ref.shape[0], 128))


def finish(a, b, copies):
    perms, wide = a.shape
    return call(
        finish_kernel,
        "finish",
        [
            jax.ShapeDtypeStruct((wide, perms), jnp.bfloat16),
            jax.ShapeDtypeStruct((copies, perms // 128, 128), jnp.float32),
        ],
        [VMEM, VMEM],
        (a, b),
        flops=4 * perms * wide,
        bytes_accessed=perms * wide * 6,
    )


def add(a, b):
    return (a.astype(jnp.float32) + b.astype(jnp.float32)).astype(jnp.bfloat16)


def each_place(place, options, body):
    low, high = options[0], options[-1]
    for r in options:
        if low == high:
            body(r)
        elif r == low:
            pl.when(place <= r)(functools.partial(body, r))
        elif r == high:
            pl.when(place >= r)(functools.partial(body, r))
        else:
            pl.when(place == r)(functools.partial(body, r))


def outgoing_kernel(options, has_recv, first, place_ref, *refs):
    out = refs[-1]
    half = out.shape[1]
    rows = pl.ds(first, half)
    owns, others = refs[:len(options)], refs[len(options):2 * len(options)]

    def body(r):
        i = options.index(r)
        for j, piece in enumerate((owns[i], others[i])):
            value = piece[rows, :]
            out[j] = add(value, refs[2 * len(options)][j]) if has_recv else value

    each_place(place_ref[0], options, body)


def incoming_kernel(size, mine, place_ref, *refs):
    out = refs[-1]
    half = out.shape[0] // 2
    count = size - 1

    def body(p):
        for j in range(2):
            rows = pl.ds(j * half, half)
            value = refs[j * count + p - 1][0 if mine else 1]
            if mine:
                value = value.astype(jnp.float32) + refs[2 * count][rows, :].astype(jnp.float32)
                value = (value + refs[2 * count + 1][rows, :].astype(jnp.float32)).astype(jnp.bfloat16)
            out[rows, :] = value

    each_place(place_ref[0], list(range(1, size)), body)


class Chain:
    def __init__(self, size, siblings, place, first, half):
        self.size, self.place, self.first, self.half = size, place, first, half
        self.recv = []
        self.pairs = []
        for z in range(size):
            for m in range(siblings):
                to = z + 1 if m % 2 == 0 else z - 1
                if 0 <= to < size:
                    self.pairs.append((z * siblings + m, to * siblings + m))

    def outgoing(self, t, own, other, after):
        options = [r for r in range(self.size - 1) if 0 <= t - r < len(other)]
        recv = [self.recv[t - 1]] if t > 0 else []
        shape = (2, self.half, own[0].shape[1])
        args = [own[t - r] for r in options] + [other[t - r] for r in options] + recv
        return call(
            functools.partial(outgoing_kernel, options, bool(recv), self.first),
            "outgoing",
            jax.ShapeDtypeStruct(shape, jnp.bfloat16),
            [SMEM] + [VMEM] * len(args) + [ANY] * len(after),
            (self.place, *args, *after),
            bytes_accessed=6 * math.prod(shape),
        )

    def send(self, value):
        self.recv.append(lax.ppermute(value, ("sample", "landmark"), self.pairs))


def incoming(upper, lower, i, own=None, other=None):
    size = upper.size
    args = [chain.recv[i + p - 1] for chain in (upper, lower) for p in range(1, size)]
    mine = own is not None
    if mine:
        args += [own, other]
    shape = (2 * upper.half, args[0].shape[2])
    return call(
        functools.partial(incoming_kernel, size, mine),
        "total" if mine else "incoming",
        jax.ShapeDtypeStruct(shape, jnp.bfloat16),
        [SMEM] + [VMEM] * len(args),
        (upper.place, *args),
        bytes_accessed=8 * math.prod(shape),
    )


def make_local(mesh):
    n_sample = mesh.shape["sample"]
    n_landmark = mesh.shape["landmark"]
    n_all = n_sample * n_landmark
    bits = n_landmark.bit_length() - 1
    siblings = [(m, m ^ 1) for m in range(n_landmark)]

    def order_of(core):
        rest = list(range(1, bits))
        return [0] + (rest if core == 0 else rest[::-1])

    def place_of(core, q):
        return sum(((q >> t) & 1) << bit for t, bit in enumerate(order_of(core)))

    def local(embeddings, landmarks, factor, flips, labels, counts):
        here = lax.axis_index("sample").astype(jnp.int32)
        spot = lax.axis_index("landmark").astype(jnp.int32)
        core = spot % 2
        place = jnp.where(core == 0, here, n_sample - 1 - here).reshape(1)
        here_ref = here.reshape(1)

        pair = own_counts(here_ref, counts, labels, n_sample)
        pair = lax.all_to_all(pair, "sample", 0, 0, tiled=True)
        held, z, scale, signs, mask_a, mask_b = prepare_rows(here_ref, counts, embeddings, landmarks, flips, labels)

        perms = flips.shape[0]
        half = perms // 2
        points = landmarks.shape[0]
        count = points // TILE
        upper = Chain(n_sample, n_landmark, place, 0, half)
        lower = Chain(n_sample, n_landmark, place, half, half)
        own, other, totals = [], [], []
        steps = count + n_sample - 2
        value = None
        for t in range(steps + 1):
            if t < count:
                following = (t + 1) * TILE if t + 1 < count else None
                after = [value] if t > 0 else []
                outs = moments_part(pair, held, z, scale, signs, mask_a, mask_b, landmarks, following, after)
                own.append(outs[0])
                if following is not None:
                    z = outs[1]
            if t > 0:
                after = [own[t]] if t < count else [value]
                lower.send(lower.outgoing(t - 1, own, other, after))
            if t < count:
                other.append(lax.ppermute(own[t], "landmark", siblings))
            if t < steps:
                value = upper.outgoing(t, own, other, totals[-1:])
                upper.send(value)
            i = t - (n_sample - 1)
            if i >= 0:
                share = lax.ppermute(incoming(upper, lower, i), "landmark", siblings)
                totals.append(incoming(upper, lower, i, own[i], share))

        kept_places = [2 * q for q in range(n_landmark // 2)]
        kept_order = sorted(kept_places, key=lambda q: [-((q >> t) & 1) for t in range(1, bits)])
        sent_order = [q + 1 for q in kept_order]

        def table_of(places, order_core):
            zero = jnp.array([place_of(0, q) for q in places], jnp.int32)
            one = jnp.array([place_of(1, q) for q in places], jnp.int32)
            return jnp.bitwise_xor(jnp.where(order_core == 0, zero, one), spot)

        def pairs_of(t):
            return [(m, m ^ (1 << order_of(m % 2)[t])) for m in range(n_landmark)]

        middle = len(kept_order) // 2
        sums = []
        for part in (slice(0, middle), slice(middle, None)):
            sent = whiten(table_of(sent_order[part], 1 - core), factor, totals, n_landmark)
            recv = lax.ppermute(sent, "landmark", siblings)
            kept = whiten(table_of(kept_order[part], core), factor, totals, n_landmark)
            sums.append((kept, recv))
        recv = lax.ppermute(add(*sums[0]), "landmark", pairs_of(1))
        kept = add(*sums[1])
        for t in range(2, bits):
            middle = kept.shape[0] // 2
            sent = add(kept[:middle], recv[:middle])
            kept = add(kept[middle:], recv[middle:])
            recv = lax.ppermute(sent, "landmark", pairs_of(t))
        whitened, share = finish(kept[0], recv[0], n_all)
        share = lax.all_to_all(share, ("sample", "landmark"), 0, 0, tiled=True)
        statistic = jnp.sum(share, axis=0).reshape(perms)
        return whitened, statistic / (points * n_landmark)

    return local


def solution(mesh):
    return jax.shard_map(
        make_local(mesh),
        mesh=mesh,
        in_specs=(
            P("sample", None),
            P("landmark", None),
            P("landmark", "sample"),
            P(None, "sample"),
            P("sample"),
            P(),
        ),
        out_specs=(P(("sample", "landmark"), None), P()),
        check_vma=False,
    )
```

time: 282 us -> 218 us (0.77)
  waiting for transfers between devices: 135 us -> 32.9 us
  starting transfers between devices: 0.26 us -> 79.8 us
  Pallas kernels: 0 us -> 56.3 us
  matrix products: 50.6 us -> 0 us
  blocking collectives: 53.4 us -> 12.2 us
  local copies, waits for them, and re-layouts: 5.23 us -> 32.2 us
  other arithmetic: 20.2 us -> 1.54 us
  between operations: 16.6 us -> 1.78 us
    psum x1 -> x0, waiting for transfers between devices: 84.7 us -> none  [local(): summed = lax.psum(partial_value.astype(jnp.bfloat16), 'sample')]
    ppermute x0 -> x40, starting transfers between devices: none -> 73.5 us  [the longest x20 67.8 us: send(): self.recv.append(lax.ppermute(value, ('sample', 'landmark'), self.pairs))]
    pallas_call x0 -> x51, Pallas kernels: none -> 56.3 us  [call(): pl.pallas_call(kernel, out_shape=out_shape, in_specs=in_specs, out_specs=...]
    psum x2 -> x0, blocking collectives: 53.4 us -> none  [the longest x1 39.4 us: local(): statistic = lax.psum(share, ('sample', 'landmark')) / LANDMARKS]
    dot_general x3 -> x0, matrix products: 50.6 us -> none  [the longest x1 30.4 us: local(): lax.dot_general(embeddings, landmarks, (((1,), (1,)), ((), ())), preferre...]
    reduce_scatter x1 -> x0, waiting for transfers between devices: 50.4 us -> none  [local(): lax.psum_scatter(whiten_maker(factor, summed).astype(jnp.bfloat16), 'land...]
    ppermute x0 -> x40, waiting for transfers between devices: none -> 32.9 us  [the longest x20 13.6 us: send(): self.recv.append(lax.ppermute(value, ('sample', 'landmark'), self.pairs))]
    unnamed x5 -> x80, local copies, waits for them, and re-layouts: 5.23 us -> 32.2 us
  transfers between devices with their start and end apart: 2 -> 41, of which waited for: 2 -> 9; matrix products, arithmetic and copies ran while one was open for 0% -> 0% of each run, Pallas kernels for 0% -> 21%
where the time goes in v2:
time: 218 us; the launch traced here: 217 us
  starting transfers between devices  79.8 us (37%)
  Pallas kernels  56.3 us (26%)
  waiting for transfers between devices  32.9 us (15%)
  local copies, waits for them, and re-layouts  32.2 us (15%)
  blocking collectives  12.2 us (6%)
    ppermute x20, starting transfers between devices, send(): self.recv.append(lax.ppermute(value, ('sample', 'landmark'), self.pairs))  67.8 us
    pallas_call x51, Pallas kernels, call(): pl.pallas_call(kernel, out_shape=out_shape, in_specs=in_specs, out_specs=...  56.3 us
    unnamed x80, local copies, waits for them, and re-layouts  32.2 us
    ppermute x20, waiting for transfers between devices, send(): self.recv.append(lax.ppermute(value, ('sample', 'landmark'), self.pairs))  13.6 us
    all_to_all x1, blocking collectives, local(): share = lax.all_to_all(share, ('sample', 'landmark'), 0, 0, tiled=True)  12.2 us
    ppermute x1, waiting for transfers between devices, local(): recv = lax.ppermute(add(*sums[0]), 'landmark', pairs_of(1))  10.1 us
    ppermute x1, waiting for transfers between devices, local(): recv = lax.ppermute(sent, 'landmark', pairs_of(t))  7.67 us
    all_to_all x1, starting transfers between devices, local(): pair = lax.all_to_all(pair, 'sample', 0, 0, tiled=True)  6.32 us
  transfers between devices with their start and end apart: 41, of which 9 were waited for; matrix products, arithmetic and copies ran while one was open for 0% of the time, Pallas kernels for 21%

profile of v2, /device:TPU:0, one launch (start us, length us, event | category | flops | bytes accessed | tf_op | source)
XLA Modules:
  0.0 216.7 jit_solution(15794676794935643287)
XLA Ops:
  3.2 6.3 %all-to-all-start = ((f32[4,8,128]{2,1,0:T(8,128)}), f32[4,8,128]{2,1,0:T(8,128)S(1)}, u32[]{:S(2)}, u32[]{:S(2)}) async-start(f32[4,8,128]{2,1,0:T(8,128)} %own_counts.1), calls=%async_computation | async-start | bytes 32768 | tf_op jit(solution)/shard_map/all_to_all | solution.py:341
  10.9 5.6 %prepare_rows.1 = (bf16[1024,4096]{1,0:T(8,128)(2,1)S(1)}, bf16[256,4096]{1,0:T(8,128)(2,1)S(1)}, f32[1024,1]{1,0:T(8,128)S(1)}, bf16[512,1024]{1,0:T(8,128)(2,1...) custom-call(s32[1]{0:T(128)} %bitcast.1.here_ref, s32[4]{0:T(128)S(1)} %copy-done.27, bf16[1024,4096]{1,0:T(8,128)(2,1)} %x_ref.1, ...), custom_call_target="tpu_custom_call" | custom-call | flops 12582912 | bytes 12582912 | tf_op jit(solution)/shard_map/prepare_rows/pallas_call | solution.py:27
  26.1 3.9 %moments.8 = (bf16[512,256]{1,0:T(8,128)(2,1)S(1)}, bf16[256,4096]{1,0:T(8,128)(2,1)S(1)}) custom-call(f32[4,8,128]{2,1,0:T(8,128)S(1)} %all-to-all-done.pair_ref, bf16[1024,4096]{1,0:T(8,128)(2,1)S(1)} %copy-done.1, bf16[256,4096]{1,0:T(8,128)(2,1)S(1)} %copy-done.19, f32[1024,1]{1,0:T(8,128)S(1)} %get-tuple-element.26.scale_ref, ...), custom_call_target="tpu_custom_call" | custom-call | flops 2415919104 | bytes 2097152 | tf_op jit(solution)/shard_map/moments/pallas_call | solution.py:27
  32.8 3.9 %collective-permute-start.1 = (bf16[2,256,256]{2,1,0:T(8,128)(2,1)S(1)}, bf16[2,256,256]{2,1,0:T(8,128)(2,1)S(1)}, u32[]{:S(2)}, u32[]{:S(2)}) collective-permute-start(bf16[2,256,256]{2,1,0:T(8,128)(2,1)S(1)} %outgoing.20.rest_0_), channel_id=1, source_target_pairs={{0,8},{2,10},{4,12},{6,14},{8,16},{9,1},{10,18},{11,3},{12,20},{13... | collective-permute-start | bytes 786440 | tf_op jit(solution)/shard_map/ppermute | solution.py:299
  41.8 4.0 %moments.9 = (bf16[512,256]{1,0:T(8,128)(2,1)S(1)}, bf16[256,4096]{1,0:T(8,128)(2,1)S(1)}) custom-call(f32[4,8,128]{2,1,0:T(8,128)S(1)} %all-to-all-done.pair_ref, bf16[1024,4096]{1,0:T(8,128)(2,1)S(1)} %copy-done.2, bf16[256,4096]{1,0:T(8,128)(2,1)S(1)} %copy-done.17, f32[1024,1]{1,0:T(8,128)S(1)} %get-tuple-element.26.scale_ref, ...), custom_call_target="tpu_custom_call" | custom-call | flops 2415919104 | bytes 2097152 | tf_op jit(solution)/shard_map/moments/pallas_call | solution.py:27
  52.7 3.9 %moments.10 = (bf16[512,256]{1,0:T(8,128)(2,1)S(1)}, bf16[256,4096]{1,0:T(8,128)(2,1)S(1)}) custom-call(f32[4,8,128]{2,1,0:T(8,128)S(1)} %all-to-all-done.pair_ref, bf16[1024,4096]{1,0:T(8,128)(2,1)S(1)} %copy-done.3, bf16[256,4096]{1,0:T(8,128)(2,1)S(1)} %get-tuple-element.33.z_ref, f32[1024,1]{1,0:T(8,128)S(1)} %get-tuple-element.26.scale_ref, ...), custom_call_target="tpu_custom_call" | custom-call | flops 2415919104 | bytes 2097152 | tf_op jit(solution)/shard_map/moments/pallas_call | solution.py:27
  61.9 3.9 %moments.11 = (bf16[512,256]{1,0:T(8,128)(2,1)S(1)}, bf16[256,4096]{1,0:T(8,128)(2,1)S(1)}) custom-call(f32[4,8,128]{2,1,0:T(8,128)S(1)} %all-to-all-done.pair_ref, bf16[1024,4096]{1,0:T(8,128)(2,1)S(1)} %copy-done.3, bf16[256,4096]{1,0:T(8,128)(2,1)S(1)} %get-tuple-element.35.z_ref, f32[1024,1]{1,0:T(8,128)S(1)} %get-tuple-element.26.scale_ref, ...), custom_call_target="tpu_custom_call" | custom-call | flops 2415919104 | bytes 2097152 | tf_op jit(solution)/shard_map/moments/pallas_call | solution.py:27
  72.9 3.9 %moments.12 = (bf16[512,256]{1,0:T(8,128)(2,1)S(1)}, bf16[256,4096]{1,0:T(8,128)(2,1)S(1)}) custom-call(f32[4,8,128]{2,1,0:T(8,128)S(1)} %all-to-all-done.pair_ref, bf16[1024,4096]{1,0:T(8,128)(2,1)S(1)} %copy-done.3, bf16[256,4096]{1,0:T(8,128)(2,1)S(1)} %get-tuple-element.37.z_ref, f32[1024,1]{1,0:T(8,128)S(1)} %get-tuple-element.26.scale_ref, ...), custom_call_target="tpu_custom_call" | custom-call | flops 2415919104 | bytes 2097152 | tf_op jit(solution)/shard_map/moments/pallas_call | solution.py:27
  83.4 4.4 %collective-permute-start.15 = (bf16[2,256,256]{2,1,0:T(8,128)(2,1)S(1)}, bf16[2,256,256]{2,1,0:T(8,128)(2,1)S(1)}, u32[]{:S(2)}, u32[]{:S(2)}) collective-permute-start(bf16[2,256,256]{2,1,0:T(8,128)(2,1)S(1)} %outgoing.28.rest_0_), channel_id=1, source_target_pairs={{0,8},{2,10},{4,12},{6,14},{8,16},{9,1},{10,18},{11,3},{12,20},{13... | collective-permute-start | bytes 786440 | tf_op jit(solution)/shard_map/ppermute | solution.py:299
  87.8 3.9 %moments.13 = (bf16[512,256]{1,0:T(8,128)(2,1)S(1)}, bf16[256,4096]{1,0:T(8,128)(2,1)S(1)}) custom-call(f32[4,8,128]{2,1,0:T(8,128)S(1)} %all-to-all-done.pair_ref, bf16[1024,4096]{1,0:T(8,128)(2,1)S(1)} %copy-done.3, bf16[256,4096]{1,0:T(8,128)(2,1)S(1)} %get-tuple-element.39.z_ref, f32[1024,1]{1,0:T(8,128)S(1)} %get-tuple-element.26.scale_ref, ...), custom_call_target="tpu_custom_call" | custom-call | flops 2415919104 | bytes 2097152 | tf_op jit(solution)/shard_map/moments/pallas_call | solution.py:27
  94.5 3.6 %collective-permute-start.19 = (bf16[2,256,256]{2,1,0:T(8,128)(2,1)S(1)}, bf16[2,256,256]{2,1,0:T(8,128)(2,1)S(1)}, u32[]{:S(2)}, u32[]{:S(2)}) collective-permute-start(bf16[2,256,256]{2,1,0:T(8,128)(2,1)S(1)} %outgoing.30.rest_0_), channel_id=1, source_target_pairs={{0,8},{2,10},{4,12},{6,14},{8,16},{9,1},{10,18},{11,3},{12,20},{13... | collective-permute-start | bytes 786440 | tf_op jit(solution)/shard_map/ppermute | solution.py:299
  98.1 3.9 %moments.14 = (bf16[512,256]{1,0:T(8,128)(2,1)S(1)}, bf16[256,4096]{1,0:T(8,128)(2,1)S(1)}) custom-call(f32[4,8,128]{2,1,0:T(8,128)S(1)} %all-to-all-done.pair_ref, bf16[1024,4096]{1,0:T(8,128)(2,1)S(1)} %copy-done.3, bf16[256,4096]{1,0:T(8,128)(2,1)S(1)} %get-tuple-element.41.z_ref, f32[1024,1]{1,0:T(8,128)S(1)} %get-tuple-element.26.scale_ref, ...), custom_call_target="tpu_custom_call" | custom-call | flops 2415919104 | bytes 2097152 | tf_op jit(solution)/shard_map/moments/pallas_call | solution.py:27
  108.5 4.4 %collective-permute-start.23 = (bf16[2,256,256]{2,1,0:T(8,128)(2,1)S(1)}, bf16[2,256,256]{2,1,0:T(8,128)(2,1)S(1)}, u32[]{:S(2)}, u32[]{:S(2)}) collective-permute-start(bf16[2,256,256]{2,1,0:T(8,128)(2,1)S(1)} %outgoing.32.rest_0_), channel_id=1, source_target_pairs={{0,8},{2,10},{4,12},{6,14},{8,16},{9,1},{10,18},{11,3},{12,20},{13... | collective-permute-start | bytes 786440 | tf_op jit(solution)/shard_map/ppermute | solution.py:299
  119.0 3.5 %collective-permute-start.27 = (bf16[2,256,256]{2,1,0:T(8,128)(2,1)S(1)}, bf16[2,256,256]{2,1,0:T(8,128)(2,1)S(1)}, u32[]{:S(2)}, u32[]{:S(2)}) collective-permute-start(bf16[2,256,256]{2,1,0:T(8,128)(2,1)S(1)} %outgoing.34.refs_7_), channel_id=1, source_target_pairs={{0,8},{2,10},{4,12},{6,14},{8,16},{9,1},{10,18},{11,3},{12,20},{13... | collective-permute-start | bytes 786440 | tf_op jit(solution)/shard_map/ppermute | solution.py:299
  122.7 4.4 %collective-permute-start.28 = (bf16[2,256,256]{2,1,0:T(8,128)(2,1)S(1)}, bf16[2,256,256]{2,1,0:T(8,128)(2,1)S(1)}, u32[]{:S(2)}, u32[]{:S(2)}) collective-permute-start(bf16[2,256,256]{2,1,0:T(8,128)(2,1)S(1)} %outgoing.35), channel_id=1, source_target_pairs={{0,8},{2,10},{4,12},{6,14},{8,16},{9,1},{10,18},{11,3},{12,20},{13... | collective-permute-start | bytes 786440 | tf_op jit(solution)/shard_map/ppermute | solution.py:299
  127.2 3.7 %collective-permute-done.28.refs_5_.refs_4_.refs_3_ = bf16[2,256,256]{2,1,0:T(8,128)(2,1)S(1)} collective-permute-done((bf16[2,256,256]{2,1,0:T(8,128)(2,1)S(1)}, bf16[2,256,256]{2,1,0:T(8,128)(2,1)S(1)}, u32[]{:S(2)}, u32[]{:S(2)}) %collective-permute-start.28) | collective-permute-done | bytes 262176 | tf_op jit(solution)/shard_map/ppermute | solution.py:299
  131.3 4.3 %collective-permute-start.30 = (bf16[2,256,256]{2,1,0:T(8,128)(2,1)S(1)}, bf16[2,256,256]{2,1,0:T(8,128)(2,1)S(1)}, u32[]{:S(2)}, u32[]{:S(2)}) collective-permute-start(bf16[2,256,256]{2,1,0:T(8,128)(2,1)S(1)} %outgoing.36.refs_5_), channel_id=1, source_target_pairs={{0,8},{2,10},{4,12},{6,14},{8,16},{9,1},{10,18},{11,3},{12,20},{13... | collective-permute-start | bytes 786440 | tf_op jit(solution)/shard_map/ppermute | solution.py:299
  139.6 4.4 %collective-permute-start.33 = (bf16[2,256,256]{2,1,0:T(8,128)(2,1)S(1)}, bf16[2,256,256]{2,1,0:T(8,128)(2,1)S(1)}, u32[]{:S(2)}, u32[]{:S(2)}) collective-permute-start(bf16[2,256,256]{2,1,0:T(8,128)(2,1)S(1)} %outgoing.38.refs_3_), channel_id=1, source_target_pairs={{0,8},{2,10},{4,12},{6,14},{8,16},{9,1},{10,18},{11,3},{12,20},{13... | collective-permute-start | bytes 786440 | tf_op jit(solution)/shard_map/ppermute | solution.py:299
  144.2 3.6 %collective-permute-start.34 = (bf16[2,256,256]{2,1,0:T(8,128)(2,1)S(1)}, bf16[2,256,256]{2,1,0:T(8,128)(2,1)S(1)}, u32[]{:S(2)}, u32[]{:S(2)}) collective-permute-start(bf16[2,256,256]{2,1,0:T(8,128)(2,1)S(1)} %outgoing.39), channel_id=1, source_target_pairs={{0,8},{2,10},{4,12},{6,14},{8,16},{9,1},{10,18},{11,3},{12,20},{13... | collective-permute-start | bytes 786440 | tf_op jit(solution)/shard_map/ppermute | solution.py:299
  157.1 5.8 %copy-done.4 = bf16[2048,4096]{1,0:T(8,128)(2,1)S(1)} copy-done((bf16[2048,4096]{1,0:T(8,128)(2,1)S(1)}, bf16[2048,4096]{1,0:T(8,128)(2,1)}, u32[]{:S(2)}) %copy-start.4) | copy-done | bytes 16777240
  166.3 5.8 %copy-done.5 = bf16[2048,4096]{1,0:T(8,128)(2,1)S(1)} copy-done((bf16[2048,4096]{1,0:T(8,128)(2,1)S(1)}, bf16[2048,4096]{1,0:T(8,128)(2,1)}, u32[]{:S(2)}) %copy-start.5) | copy-done | bytes 16777240
  183.1 10.1 %collective-permute-done.38 = bf16[2,512,512]{2,1,0:T(8,128)(2,1)S(1)} collective-permute-done((bf16[2,512,512]{2,1,0:T(8,128)(2,1)S(1)}, bf16[2,512,512]{2,1,0:T(8,128)(2,1)S(1)}, u32[]{:S(2)}, u32[]{:S(2)}) %collective-permute-start.38) | collective-permute-done | bytes 1048608 | tf_op jit(solution)/shard_map/ppermute | solution.py:393
  195.0 7.7 %collective-permute-done.39 = bf16[1,512,512]{2,1,0:T(8,128)(2,1)S(1)} collective-permute-done((bf16[1,512,512]{2,1,0:T(8,128)(2,1)S(1)}, bf16[1,512,512]{2,1,0:T(8,128)(2,1)S(1)}, u32[]{:S(2)}, u32[]{:S(2)}) %collective-permute-start.39) | collective-permute-done | bytes 524320 | tf_op jit(solution)/shard_map/ppermute | solution.py:399
  203.8 12.2 %all_to_all.10 = f32[32,4,128]{2,1,0:T(4,128)S(1)} all-to-all(f32[32,4,128]{2,1,0:T(4,128)S(1)} %get-tuple-element.45), channel_id=1, replica_groups=mesh['sample'=4,'landmark'=8] {'sample','landmark'}, dimensions={0} | all-to-all | bytes 131072 | tf_op jit(solution)/shard_map/all_to_all | solution.py:401
  (198 shorter events, 93.9 us)
Async XLA Ops:
  3.2 17.9 %all-to-all-start = ((f32[4,8,128]{2,1,0:T(8,128)}), f32[4,8,128]{2,1,0:T(8,128)S(1)}, u32[]{:S(2)}, u32[]{:S(2)}) async-start(f32[4,8,128]{2,1,0:T(8,128)} %own_counts.1), calls=%async_computation | async-start | bytes 32768 | tf_op jit(solution)/shard_map/all_to_all | solution.py:341
  32.8 16.4 %collective-permute-start.1 = (bf16[2,256,256]{2,1,0:T(8,128)(2,1)S(1)}, bf16[2,256,256]{2,1,0:T(8,128)(2,1)S(1)}, u32[]{:S(2)}, u32[]{:S(2)}) collective-permute-start(bf16[2,256,256]{2,1,0:T(8,128)(2,1)S(1)} %outgoing.20.rest_0_), channel_id=1, source_target_pairs={{0,8},{2,10},{4,12},{6,14},{8,16},{9,1},{10,18},{11,3},{12,20},{13... | collective-permute-start | bytes 786440 | tf_op jit(solution)/shard_map/ppermute | solution.py:299
  45.9 10.8 %collective-permute-start.6 = (bf16[2,256,256]{2,1,0:T(8,128)(2,1)S(1)}, bf16[2,256,256]{2,1,0:T(8,128)(2,1)S(1)}, u32[]{:S(2)}, u32[]{:S(2)}) collective-permute-start(bf16[2,256,256]{2,1,0:T(8,128)(2,1)S(1)} %outgoing.23), channel_id=1, source_target_pairs={{0,8},{2,10},{4,12},{6,14},{8,16},{9,1},{10,18},{11,3},{12,20},{13... | collective-permute-start | bytes 786440 | tf_op jit(solution)/shard_map/ppermute | solution.py:299
  49.3 9.8 %collective-permute-start.3 = (bf16[2,256,256]{2,1,0:T(8,128)(2,1)S(1)}, bf16[2,256,256]{2,1,0:T(8,128)(2,1)S(1)}, u32[]{:S(2)}, u32[]{:S(2)}) collective-permute-start(bf16[2,256,256]{2,1,0:T(8,128)(2,1)S(1)} %outgoing.21.rest_0_), channel_id=1, source_target_pairs={{0,8},{2,10},{4,12},{6,14},{8,16},{9,1},{10,18},{11,3},{12,20},{13... | collective-permute-start | bytes 786440 | tf_op jit(solution)/shard_map/ppermute | solution.py:299
  56.8 9.1 %collective-permute-start.7 = (bf16[2,256,256]{2,1,0:T(8,128)(2,1)S(1)}, bf16[2,256,256]{2,1,0:T(8,128)(2,1)S(1)}, u32[]{:S(2)}, u32[]{:S(2)}) collective-permute-start(bf16[2,256,256]{2,1,0:T(8,128)(2,1)S(1)} %outgoing.24), channel_id=1, source_target_pairs={{0,8},{2,10},{4,12},{6,14},{8,16},{9,1},{10,18},{11,3},{12,20},{13... | collective-permute-start | bytes 786440 | tf_op jit(solution)/shard_map/ppermute | solution.py:299
  59.2 10.2 %collective-permute-start.5 = (bf16[2,256,256]{2,1,0:T(8,128)(2,1)S(1)}, bf16[2,256,256]{2,1,0:T(8,128)(2,1)S(1)}, u32[]{:S(2)}, u32[]{:S(2)}) collective-permute-start(bf16[2,256,256]{2,1,0:T(8,128)(2,1)S(1)} %outgoing.22.rest_0_), channel_id=1, source_target_pairs={{0,8},{2,10},{4,12},{6,14},{8,16},{9,1},{10,18},{11,3},{12,20},{13... | collective-permute-start | bytes 786440 | tf_op jit(solution)/shard_map/ppermute | solution.py:299
  66.0 10.7 %collective-permute-start.8 = (bf16[2,256,256]{2,1,0:T(8,128)(2,1)S(1)}, bf16[2,256,256]{2,1,0:T(8,128)(2,1)S(1)}, u32[]{:S(2)}, u32[]{:S(2)}) collective-permute-start(bf16[2,256,256]{2,1,0:T(8,128)(2,1)S(1)} %outgoing.25), channel_id=1, source_target_pairs={{0,8},{2,10},{4,12},{6,14},{8,16},{9,1},{10,18},{11,3},{12,20},{13... | collective-permute-start | bytes 786440 | tf_op jit(solution)/shard_map/ppermute | solution.py:299
  69.5 10.3 %collective-permute-start.11 = (bf16[2,256,256]{2,1,0:T(8,128)(2,1)S(1)}, bf16[2,256,256]{2,1,0:T(8,128)(2,1)S(1)}, u32[]{:S(2)}, u32[]{:S(2)}) collective-permute-start(bf16[2,256,256]{2,1,0:T(8,128)(2,1)S(1)} %outgoing.26.rest_0_), channel_id=1, source_target_pairs={{0,8},{2,10},{4,12},{6,14},{8,16},{9,1},{10,18},{11,3},{12,20},{13... | collective-permute-start | bytes 786440 | tf_op jit(solution)/shard_map/ppermute | solution.py:299
  83.1 11.2 %collective-permute-start.13 = (bf16[512,256]{1,0:T(8,128)(2,1)S(1)}, bf16[512,256]{1,0:T(8,128)(2,1)S(1)}, u32[]{:S(2)}, u32[]{:S(2)}) collective-permute-start(bf16[512,256]{1,0:T(8,128)(2,1)S(1)} %incoming.9), channel_id=1, source_target_pairs={{0,1},{1,0},{2,3},{3,2},{4,5},{5,4},{6,7},{7,6},{8,9},{9,8},{10,11... | collective-permute-start | bytes 786440 | tf_op jit(solution)/shard_map/ppermute | solution.py:371
  83.4 11.0 %collective-permute-start.15 = (bf16[2,256,256]{2,1,0:T(8,128)(2,1)S(1)}, bf16[2,256,256]{2,1,0:T(8,128)(2,1)S(1)}, u32[]{:S(2)}, u32[]{:S(2)}) collective-permute-start(bf16[2,256,256]{2,1,0:T(8,128)(2,1)S(1)} %outgoing.28.rest_0_), channel_id=1, source_target_pairs={{0,8},{2,10},{4,12},{6,14},{8,16},{9,1},{10,18},{11,3},{12,20},{13... | collective-permute-start | bytes 786440 | tf_op jit(solution)/shard_map/ppermute | solution.py:299
  91.8 10.2 %collective-permute-start.16 = (bf16[2,256,256]{2,1,0:T(8,128)(2,1)S(1)}, bf16[2,256,256]{2,1,0:T(8,128)(2,1)S(1)}, u32[]{:S(2)}, u32[]{:S(2)}) collective-permute-start(bf16[2,256,256]{2,1,0:T(8,128)(2,1)S(1)} %outgoing.29), channel_id=1, source_target_pairs={{0,8},{2,10},{4,12},{6,14},{8,16},{9,1},{10,18},{11,3},{12,20},{13... | collective-permute-start | bytes 786440 | tf_op jit(solution)/shard_map/ppermute | solution.py:299
  94.5 10.2 %collective-permute-start.19 = (bf16[2,256,256]{2,1,0:T(8,128)(2,1)S(1)}, bf16[2,256,256]{2,1,0:T(8,128)(2,1)S(1)}, u32[]{:S(2)}, u32[]{:S(2)}) collective-permute-start(bf16[2,256,256]{2,1,0:T(8,128)(2,1)S(1)} %outgoing.30.rest_0_), channel_id=1, source_target_pairs={{0,8},{2,10},{4,12},{6,14},{8,16},{9,1},{10,18},{11,3},{12,20},{13... | collective-permute-start | bytes 786440 | tf_op jit(solution)/shard_map/ppermute | solution.py:299
  107.9 10.8 %collective-permute-start.21 = (bf16[512,256]{1,0:T(8,128)(2,1)S(1)}, bf16[512,256]{1,0:T(8,128)(2,1)S(1)}, u32[]{:S(2)}, u32[]{:S(2)}) collective-permute-start(bf16[512,256]{1,0:T(8,128)(2,1)S(1)} %incoming.11), channel_id=1, source_target_pairs={{0,1},{1,0},{2,3},{3,2},{4,5},{5,4},{6,7},{7,6},{8,9},{9,8},{10,11... | collective-permute-start | bytes 786440 | tf_op jit(solution)/shard_map/ppermute | solution.py:371
  108.5 10.4 %collective-permute-start.23 = (bf16[2,256,256]{2,1,0:T(8,128)(2,1)S(1)}, bf16[2,256,256]{2,1,0:T(8,128)(2,1)S(1)}, u32[]{:S(2)}, u32[]{:S(2)}) collective-permute-start(bf16[2,256,256]{2,1,0:T(8,128)(2,1)S(1)} %outgoing.32.rest_0_), channel_id=1, source_target_pairs={{0,8},{2,10},{4,12},{6,14},{8,16},{9,1},{10,18},{11,3},{12,20},{13... | collective-permute-start | bytes 786440 | tf_op jit(solution)/shard_map/ppermute | solution.py:299
  119.0 8.2 %collective-permute-start.27 = (bf16[2,256,256]{2,1,0:T(8,128)(2,1)S(1)}, bf16[2,256,256]{2,1,0:T(8,128)(2,1)S(1)}, u32[]{:S(2)}, u32[]{:S(2)}) collective-permute-start(bf16[2,256,256]{2,1,0:T(8,128)(2,1)S(1)} %outgoing.34.refs_7_), channel_id=1, source_target_pairs={{0,8},{2,10},{4,12},{6,14},{8,16},{9,1},{10,18},{11,3},{12,20},{13... | collective-permute-start | bytes 786440 | tf_op jit(solution)/shard_map/ppermute | solution.py:299
  122.7 8.3 %collective-permute-start.28 = (bf16[2,256,256]{2,1,0:T(8,128)(2,1)S(1)}, bf16[2,256,256]{2,1,0:T(8,128)(2,1)S(1)}, u32[]{:S(2)}, u32[]{:S(2)}) collective-permute-start(bf16[2,256,256]{2,1,0:T(8,128)(2,1)S(1)} %outgoing.35), channel_id=1, source_target_pairs={{0,8},{2,10},{4,12},{6,14},{8,16},{9,1},{10,18},{11,3},{12,20},{13... | collective-permute-start | bytes 786440 | tf_op jit(solution)/shard_map/ppermute | solution.py:299
  131.0 8.3 %collective-permute-start.29 = (bf16[512,256]{1,0:T(8,128)(2,1)S(1)}, bf16[512,256]{1,0:T(8,128)(2,1)S(1)}, u32[]{:S(2)}, u32[]{:S(2)}) collective-permute-start(bf16[512,256]{1,0:T(8,128)(2,1)S(1)} %incoming.13), channel_id=1, source_target_pairs={{0,1},{1,0},{2,3},{3,2},{4,5},{5,4},{6,7},{7,6},{8,9},{9,8},{10,11... | collective-permute-start | bytes 786440 | tf_op jit(solution)/shard_map/ppermute | solution.py:371
  131.3 8.2 %collective-permute-start.30 = (bf16[2,256,256]{2,1,0:T(8,128)(2,1)S(1)}, bf16[2,256,256]{2,1,0:T(8,128)(2,1)S(1)}, u32[]{:S(2)}, u32[]{:S(2)}) collective-permute-start(bf16[2,256,256]{2,1,0:T(8,128)(2,1)S(1)} %outgoing.36.refs_5_), channel_id=1, source_target_pairs={{0,8},{2,10},{4,12},{6,14},{8,16},{9,1},{10,18},{11,3},{12,20},{13... | collective-permute-start | bytes 786440 | tf_op jit(solution)/shard_map/ppermute | solution.py:299
  135.8 8.3 %collective-permute-start.31 = (bf16[2,256,256]{2,1,0:T(8,128)(2,1)S(1)}, bf16[2,256,256]{2,1,0:T(8,128)(2,1)S(1)}, u32[]{:S(2)}, u32[]{:S(2)}) collective-permute-start(bf16[2,256,256]{2,1,0:T(8,128)(2,1)S(1)} %outgoing.37), channel_id=1, source_target_pairs={{0,8},{2,10},{4,12},{6,14},{8,16},{9,1},{10,18},{11,3},{12,20},{13... | collective-permute-start | bytes 786440 | tf_op jit(solution)/shard_map/ppermute | solution.py:299
  139.6 8.9 %collective-permute-start.33 = (bf16[2,256,256]{2,1,0:T(8,128)(2,1)S(1)}, bf16[2,256,256]{2,1,0:T(8,128)(2,1)S(1)}, u32[]{:S(2)}, u32[]{:S(2)}) collective-permute-start(bf16[2,256,256]{2,1,0:T(8,128)(2,1)S(1)} %outgoing.38.refs_3_), channel_id=1, source_target_pairs={{0,8},{2,10},{4,12},{6,14},{8,16},{9,1},{10,18},{11,3},{12,20},{13... | collective-permute-start | bytes 786440 | tf_op jit(solution)/shard_map/ppermute | solution.py:299
  165.8 12.2 %collective-permute-start.37 = (bf16[2,512,512]{2,1,0:T(8,128)(2,1)S(1)}, bf16[2,512,512]{2,1,0:T(8,128)(2,1)S(1)}, u32[]{:S(2)}, u32[]{:S(2)}) collective-permute-start(bf16[2,512,512]{2,1,0:T(8,128)(2,1)S(1)} %whiten.7), channel_id=1, source_target_pairs={{0,1},{1,0},{2,3},{3,2},{4,5},{5,4},{6,7},{7,6},{8,9},{9,8},{10,11... | collective-permute-start | bytes 3145736 | tf_op jit(solution)/shard_map/ppermute | solution.py:390
  175.0 7.8 %collective-permute-start.36 = (bf16[2,512,512]{2,1,0:T(8,128)(2,1)S(1)}, bf16[2,512,512]{2,1,0:T(8,128)(2,1)S(1)}, u32[]{:S(2)}, u32[]{:S(2)}) collective-permute-start(bf16[2,512,512]{2,1,0:T(8,128)(2,1)S(1)} %whiten.5), channel_id=1, source_target_pairs={{0,1},{1,0},{2,3},{3,2},{4,5},{5,4},{6,7},{7,6},{8,9},{9,8},{10,11... | collective-permute-start | bytes 3145736 | tf_op jit(solution)/shard_map/ppermute | solution.py:390
  178.3 14.9 %collective-permute-start.38 = (bf16[2,512,512]{2,1,0:T(8,128)(2,1)S(1)}, bf16[2,512,512]{2,1,0:T(8,128)(2,1)S(1)}, u32[]{:S(2)}, u32[]{:S(2)}) collective-permute-start(bf16[2,512,512]{2,1,0:T(8,128)(2,1)S(1)} %add_convert_fusion), channel_id=1, source_target_pairs={{0,2},{1,5},{2,0},{3,7},{4,6},{5,1},{6,4},{7,3},{8,10},{9,13},{10,... | collective-permute-start | bytes 3145736 | tf_op jit(solution)/shard_map/ppermute | solution.py:393
  193.5 9.2 %collective-permute-start.39 = (bf16[1,512,512]{2,1,0:T(8,128)(2,1)S(1)}, bf16[1,512,512]{2,1,0:T(8,128)(2,1)S(1)}, u32[]{:S(2)}, u32[]{:S(2)}) collective-permute-start(bf16[1,512,512]{2,1,0:T(8,128)(2,1)S(1)} %get-tuple-element.46), channel_id=1, source_target_pairs={{0,4},{1,3},{2,6},{3,1},{4,0},{5,7},{6,2},{7,5},{8,12},{9,11},{10,... | collective-permute-start | bytes 1572872 | tf_op jit(solution)/shard_map/ppermute | solution.py:399
  (57 other events, 246.2 us)

commit v3 on v2

v3 whole, which is shorter than its diff:
```python
import functools
import math

import jax
import jax.numpy as jnp
from jax import lax
from jax.experimental import pallas as pl
from jax.experimental.pallas import tpu as pltpu
from jax.sharding import PartitionSpec as P

VMEM_LIMIT = 14 * 1024 * 1024
TILE = 256
NT = (((1,), (1,)), ((), ()))


VMEM = pl.BlockSpec(memory_space=pltpu.VMEM)
SMEM = pl.BlockSpec(memory_space=pltpu.SMEM)
HBM = pl.BlockSpec(memory_space=pltpu.HBM)
ANY = pl.BlockSpec(memory_space=pl.ANY)


def in_hbm(x):
    return pltpu.with_memory_space_constraint(x, pltpu.HBM)


def call(kernel, name, out_shape, in_specs, args, flops=0, bytes_accessed=0, transcendentals=0, scratch=()):
    return pl.pallas_call(
        kernel,
        out_shape=out_shape,
        in_specs=in_specs,
        out_specs=jax.tree.map(lambda _: VMEM, out_shape),
        scratch_shapes=list(scratch),
        compiler_params=pltpu.CompilerParams(vmem_limit_bytes=VMEM_LIMIT),
        cost_estimate=pl.CostEstimate(
            flops=flops, bytes_accessed=bytes_accessed, transcendentals=transcendentals
        ),
        name=name,
    )(*args)


def slot_masks(labels, own_count, slots):
    live = slots < own_count
    return (live & (labels == 0)).astype(jnp.float32), (live & (labels != 0)).astype(jnp.float32)


def counts_kernel(here_ref, counts_ref, labels_ref, *refs):
    out_ref = refs[-1]
    own_count = counts_ref[here_ref[0]]
    shape = labels_ref.shape
    slots = lax.broadcasted_iota(jnp.int32, shape, 0) * shape[1] + lax.broadcasted_iota(jnp.int32, shape, 1)
    mask_a, mask_b = slot_masks(labels_ref[...], own_count, slots)
    first = lax.broadcasted_iota(jnp.int32, out_ref.shape[1:], 0) == 0
    pair = jnp.where(first, jnp.sum(mask_a), jnp.sum(mask_b))
    out_ref[...] = jnp.broadcast_to(pair[None], out_ref.shape)


def own_counts(here, counts, labels, copies, after):
    return call(
        counts_kernel,
        "own_counts",
        jax.ShapeDtypeStruct((copies, 8, 128), jnp.float32),
        [SMEM, SMEM, VMEM] + [ANY] * len(after),
        (here, counts, labels.reshape(-1, 128), *after),
    )


def rows_kernel(parts, here_ref, counts_ref, pair_ref, x_ref, z_ref, flips_ref, labels_ref,
                held_ref, first_ref, scale_ref, signs_ref, weight_ref, flips_buf, x_sem, z_sem, f_sem):
    rows, width = x_ref.shape
    block = rows // parts

    def x_copy(i):
        here = pl.ds(i * block, block)
        return pltpu.make_async_copy(x_ref.at[here, :], held_ref.at[here, :], x_sem.at[i])

    flips_copy = pltpu.make_async_copy(flips_ref, flips_buf, f_sem)
    z_copy = pltpu.make_async_copy(z_ref.at[pl.ds(0, first_ref.shape[0]), :], first_ref, z_sem)
    for i in range(parts):
        x_copy(i).start()
    z_copy.start()
    flips_copy.start()
    own_count = counts_ref[here_ref[0]]
    pair = jnp.sum(pair_ref[...], axis=0)
    count_a, count_b = pair[0:1, 0:1], pair[1:2, 0:1]
    balance = jnp.sqrt(count_a * count_b / (count_a + count_b))
    weight_a, weight_b = balance / count_a, balance / count_b
    for j in range(rows // 128):
        here = pl.ds(j * 128, 128)
        labels = jnp.transpose(jnp.broadcast_to(labels_ref[pl.ds(j, 1), :], (128, 128)))[:, 0:1]
        slots = j * 128 + lax.broadcasted_iota(jnp.int32, (128, 1), 0)
        mask_a, mask_b = slot_masks(labels, own_count, slots)
        weight_ref[here, :] = mask_a * weight_a - mask_b * weight_b
    for i in range(parts):
        x_copy(i).wait()
        here = pl.ds(i * block, block)
        x = held_ref[here, :].astype(jnp.float32)
        mean = jnp.sum(x * x, axis=1, keepdims=True) * (1.0 / width)
        scale_ref[here, :] = lax.rsqrt(mean + 1e-06) * (0.5 / math.sqrt(width))
    flips_copy.wait()
    signs_ref[...] = (2 * flips_buf[...] - 1).astype(jnp.bfloat16)
    z_copy.wait()


def prepare_rows(here, counts, pair, x, z, flips, labels):
    rows, width = x.shape
    perms = flips.shape[0]
    parts = 8
    column = jax.ShapeDtypeStruct((rows, 1), jnp.float32)
    return call(
        functools.partial(rows_kernel, parts),
        "prepare_rows",
        [
            pltpu.VMEM((rows, width), x.dtype),
            jax.ShapeDtypeStruct((TILE, width), z.dtype),
            column,
            jax.ShapeDtypeStruct((perms, rows), jnp.bfloat16),
            column,
        ],
        [SMEM, SMEM, VMEM, HBM, HBM, HBM, VMEM],
        (here, counts, pair, in_hbm(x), in_hbm(z), in_hbm(flips), labels.reshape(-1, 128)),
        flops=3 * rows * width,
        bytes_accessed=(rows + TILE) * width * 2 + perms * rows * 4,
        scratch=[
            pltpu.VMEM(flips.shape, flips.dtype),
            pltpu.SemaphoreType.DMA((parts,)),
            pltpu.SemaphoreType.DMA,
            pltpu.SemaphoreType.DMA,
        ],
    )


def moments_kernel(after, next_at_ref, x_ref, z_ref, scale_ref, signs_ref, weight_ref, z_all_ref, *rest):
    out_ref, next_ref, sem = rest[after:]
    at = pl.multiple_of(next_at_ref[0], TILE)
    next_copy = pltpu.make_async_copy(z_all_ref.at[pl.ds(at, TILE), :], next_ref, sem)
    next_copy.start()
    z = z_ref[...]
    z32 = z.astype(jnp.float32)
    mean = jnp.sum(z32 * z32, axis=1, keepdims=True) * (1.0 / z.shape[1])
    point = jnp.broadcast_to(lax.rsqrt(mean + 1e-06), (TILE, 128))
    point_row = jnp.transpose(point)[0:1, :]
    cross = lax.dot_general(x_ref[...], z, NT, preferred_element_type=jnp.float32)
    kern = jnp.exp(cross * scale_ref[...] * point_row)
    weighted = (weight_ref[...] * kern).astype(jnp.bfloat16)
    out_ref[...] = jnp.dot(signs_ref[...], weighted, preferred_element_type=jnp.float32).astype(jnp.bfloat16)
    next_copy.wait()


def moments_part(next_at, x, z, scale, signs, weight, z_all, after):
    rows, width = x.shape
    perms = signs.shape[0]
    return call(
        functools.partial(moments_kernel, len(after)),
        "moments",
        [
            jax.ShapeDtypeStruct((perms, TILE), jnp.bfloat16),
            jax.ShapeDtypeStruct((TILE, width), z.dtype),
        ],
        [SMEM] + [VMEM] * 5 + [HBM] + [ANY] * len(after),
        (next_at, x, z, scale, signs, weight, in_hbm(z_all), *after),
        flops=2 * rows * width * TILE + 2 * perms * rows * TILE,
        bytes_accessed=TILE * width * 2,
        transcendentals=rows * TILE,
        scratch=[pltpu.SemaphoreType.DMA],
    )


def whiten_kernel(table_ref, factor_ref, *refs):
    parts, (out, moments) = refs[:-2], refs[-2:]
    piece = parts[0].shape[1]

    @pl.when(pl.program_id(0) == 0)
    def _():
        for i, part in enumerate(parts):
            moments[:, pl.ds(i * piece, piece)] = part[...]

    out[0] = jnp.dot(moments[...], factor_ref[...], preferred_element_type=jnp.float32).astype(jnp.bfloat16)


def whiten(table, factor, parts, blocks):
    depth, columns = factor.shape
    perms = parts[0].shape[0]
    count = table.shape[0]
    wide = columns // blocks
    return pl.pallas_call(
        whiten_kernel,
        grid_spec=pltpu.PrefetchScalarGridSpec(
            num_scalar_prefetch=1,
            grid=(count,),
            in_specs=[pl.BlockSpec((depth, wide), lambda i, t: (0, t[i]))] + [VMEM] * len(parts),
            out_specs=pl.BlockSpec((1, perms, wide), lambda i, t: (i, 0, 0)),
            scratch_shapes=[pltpu.VMEM((perms, depth), jnp.bfloat16)],
        ),
        out_shape=jax.ShapeDtypeStruct((count, perms, wide), jnp.bfloat16),
        compiler_params=pltpu.CompilerParams(vmem_limit_bytes=VMEM_LIMIT),
        cost_estimate=pl.CostEstimate(
            flops=2 * perms * depth * wide * count,
            bytes_accessed=depth * wide * count * 2,
            transcendentals=0,
        ),
        name="whiten",
    )(table, in_hbm(factor), *parts)


def add_kernel(a_ref, b_ref, *outs):
    at = 0
    for out in outs:
        here = pl.ds(at, out.shape[0])
        out[...] = add(a_ref[here], b_ref[here])
        at += out.shape[0]


def add_blocks(a, b, counts):
    outs = [jax.ShapeDtypeStruct((count,) + a.shape[1:], a.dtype) for count in counts]
    return call(add_kernel, "add_blocks", outs, [VMEM, VMEM], (a, b), bytes_accessed=6 * a.size)


def finish_kernel(a_ref, b_ref, out_ref, share_ref):
    wide = jnp.transpose(a_ref[...].astype(jnp.float32) + b_ref[...].astype(jnp.float32))
    out_ref[...] = wide.astype(jnp.bfloat16)
    share = jnp.sum(wide * wide, axis=0, keepdims=True)
    for j in range(share_ref.shape[1]):
        row = share[:, j * 128:(j + 1) * 128]
        share_ref[:, j, :] = jnp.broadcast_to(row, (share_ref.shape[0], 128))


def finish(a, b, copies):
    perms, wide = a.shape
    return call(
        finish_kernel,
        "finish",
        [
            jax.ShapeDtypeStruct((wide, perms), jnp.bfloat16),
            jax.ShapeDtypeStruct((copies, perms // 128, 128), jnp.float32),
        ],
        [VMEM, VMEM],
        (a, b),
        flops=4 * perms * wide,
        bytes_accessed=perms * wide * 6,
    )


def add(a, b):
    return (a.astype(jnp.float32) + b.astype(jnp.float32)).astype(jnp.bfloat16)


def each_place(place, options, body):
    low, high = options[0], options[-1]
    for r in options:
        if low == high:
            body(r)
        elif r == low:
            pl.when(place <= r)(functools.partial(body, r))
        elif r == high:
            pl.when(place >= r)(functools.partial(body, r))
        else:
            pl.when(place == r)(functools.partial(body, r))


def sum_kernel(terms, depth_ref, *refs):
    out = refs[-1]

    def body(d):
        first, *rest = terms[d]
        if not rest:
            out[...] = refs[first][...]
            return
        value = refs[first][...].astype(jnp.float32)
        for i in rest:
            value = value + refs[i][...].astype(jnp.float32)
        out[...] = value.astype(out.dtype)

    each_place(depth_ref[0], sorted(terms), body)


def sum_at(name, depth, options, after=()):
    args = []
    for arrays in options.values():
        args += [a for a in arrays if not any(a is b for b in args)]
    place = lambda a: next(i for i, b in enumerate(args) if a is b)
    terms = {d: [place(a) for a in arrays] for d, arrays in options.items()}
    return call(
        functools.partial(sum_kernel, terms),
        name,
        jax.ShapeDtypeStruct(args[0].shape, args[0].dtype),
        [SMEM] + [VMEM] * len(args) + [ANY] * len(after),
        (depth, *args, *after),
        bytes_accessed=8 * args[0].size,
    )


class SampleSum:
    def __init__(self, n, depth):
        self.n, self.depth, self.last = n, depth, n // 2 - 1
        self.pieces, self.sent, self.recv = [], {}, {}

    def has(self, c):
        return 0 <= c < len(self.pieces)

    def inner(self, d, c):
        return [self.pieces[c]] + ([self.recv[(d - 1) % 2, c + d - 1]] if d > 0 else [])

    def whole(self, d, c):
        if d == self.last:
            key = (d % 2, c + d)
            return [self.sent[key], self.recv[key]]
        return [self.recv[d % 2, c + self.n - 2 - d]]

    def exchange(self, parity, period, after=()):
        options = {}
        for d in range(self.last + 1):
            if d % 2 == parity:
                if self.has(period - d):
                    options[d] = self.inner(d, period - d)
            elif d > 0 and self.has(period - (self.n - 1 - d)):
                options[d] = self.whole(d, period - (self.n - 1 - d))
        if not options:
            return None
        value = sum_at("exchanged", self.depth, options, after)
        pairs = []
        for i in range(parity, self.n - 1, 2):
            pairs += [(i, i + 1), (i + 1, i)]
        self.sent[parity, period] = value
        self.recv[parity, period] = lax.ppermute(value, "sample", pairs)
        return value

    def total(self, c):
        return sum_at("total", self.depth, {d: self.whole(d, c) for d in range(self.last + 1)})


def make_local(mesh):
    n_sample = mesh.shape["sample"]
    n_landmark = mesh.shape["landmark"]
    n_all = n_sample * n_landmark
    bits = n_landmark.bit_length() - 1
    siblings = [(m, m ^ 1) for m in range(n_landmark)]

    def order_of(core):
        rest = list(range(1, bits))
        return [0] + (rest if core == 0 else rest[::-1])

    def place_of(core, q):
        return sum(((q >> t) & 1) << bit for t, bit in enumerate(order_of(core)))

    def local(embeddings, landmarks, factor, flips, labels, counts):
        here = lax.axis_index("sample").astype(jnp.int32)
        spot = lax.axis_index("landmark").astype(jnp.int32)
        core = spot % 2
        depth = jnp.minimum(here, n_sample - 1 - here).reshape(1)
        here = here.reshape(1)
        points = landmarks.shape[0]
        perms = flips.shape[0]
        count = points // TILE

        kept_places = [2 * q for q in range(n_landmark // 2)]
        kept_order = sorted(kept_places, key=lambda q: [-((q >> t) & 1) for t in range(1, bits)])
        sent_order = [q + 1 for q in kept_order]

        def table_of(places, order_core):
            zero = jnp.array([place_of(0, q) for q in places], jnp.int32)
            one = jnp.array([place_of(1, q) for q in places], jnp.int32)
            return jnp.bitwise_xor(jnp.where(order_core == 0, zero, one), spot)

        def pairs_of(t):
            return [(m, m ^ (1 << order_of(m % 2)[t])) for m in range(n_landmark)]

        middle = len(kept_order) // 2
        tables = [
            (table_of(sent_order[part], 1 - core), table_of(kept_order[part], core))
            for part in (slice(0, middle), slice(middle, None))
        ]
        starts = [jnp.full((1,), (t + 1) % count * TILE, jnp.int32) for t in range(count)]
        after = [depth, *starts, *tables[0], *tables[1]]
        depth, *starts, first_sent, first_kept, second_sent, second_kept = lax.optimization_barrier(after)

        pair = own_counts(here, counts, labels, n_sample, [depth, first_sent, first_kept, second_sent, second_kept])
        pair = lax.all_to_all(pair, "sample", 0, 0, tiled=True)
        held, z, scale, signs, weight = prepare_rows(here, counts, pair, embeddings, landmarks, flips, labels)

        line = SampleSum(n_sample, depth)
        totals = []
        value = None
        for t in range(count + n_sample - 2):
            if t < count:
                after = [value] if t > 0 else []
                piece, z = moments_part(starts[t], held, z, scale, signs, weight, landmarks, after)
                line.pieces.append(piece)
            after = totals[-1:] + line.pieces[-1:]
            value = line.exchange(0, t, after)
            odd = line.exchange(1, t, after)
            value = value if odd is None else odd
            if t >= n_sample - 1:
                totals.append(line.total(t - (n_sample - 1)))
        totals.append(line.total(count - 1))

        sums = []
        for sent_table, kept_table in ((first_sent, first_kept), (second_sent, second_kept)):
            sent = whiten(sent_table, factor, totals, n_landmark)
            recv = lax.ppermute(sent, "landmark", siblings)
            kept = whiten(kept_table, factor, totals, n_landmark)
            (total,) = add_blocks(kept, recv, [kept.shape[0]])
            sums.append(total)
        recv = lax.ppermute(sums[0], "landmark", pairs_of(1))
        kept = sums[1]
        for t in range(2, bits):
            half = kept.shape[0] // 2
            sent, kept = add_blocks(kept, recv, [half, half])
            recv = lax.ppermute(sent, "landmark", pairs_of(t))
        whitened, share = finish(kept[0], recv[0], n_all)
        share = lax.all_to_all(share, ("sample", "landmark"), 0, 0, tiled=True)
        statistic = jnp.sum(share, axis=0).reshape(perms)
        return whitened, statistic / (points * n_landmark)

    return local


def solution(mesh):
    return jax.shard_map(
        make_local(mesh),
        mesh=mesh,
        in_specs=(
            P("sample", None),
            P("landmark", None),
            P("landmark", "sample"),
            P(None, "sample"),
            P("sample"),
            P(),
        ),
        out_specs=(P(("sample", "landmark"), None), P()),
        check_vma=False,
    )
```

time: 218 us -> 168 us (0.77)
  starting transfers between devices: 79.8 us -> 47 us
  local copies, waits for them, and re-layouts: 32.2 us -> 1.34 us
  blocking collectives: 12.2 us -> 23.5 us
  Pallas kernels: 56.3 us -> 66.4 us
  waiting for transfers between devices: 32.9 us -> 26 us
    unnamed x80 -> x4, local copies, waits for them, and re-layouts: 32.2 us -> 1.34 us
    ppermute x37 -> x19, starting transfers between devices: 71.3 us -> 44.8 us  [the longest x18 43.2 us: exchange(): self.recv[parity, period] = lax.ppermute(value, 'sample', pairs)]
    pallas_call x0 -> x4, Pallas kernels: none -> 19.8 us  [whiten(): pl.pallas_call(whiten_kernel, grid_spec=pltpu.PrefetchScalarGridSpec(num_...]
    all_to_all x0 -> x1, blocking collectives: none -> 11.7 us  [local(): pair = lax.all_to_all(pair, 'sample', 0, 0, tiled=True)]
    pallas_call x51 -> x40, Pallas kernels: 56.3 us -> 46.5 us  [call(): pl.pallas_call(kernel, out_shape=out_shape, in_specs=in_specs, out_specs=...]
    ppermute x37 -> x19, waiting for transfers between devices: 25.2 us -> 18.3 us  [the longest x18 10.2 us: exchange(): self.recv[parity, period] = lax.ppermute(value, 'sample', pairs)]
    all_to_all x1 -> x0, starting transfers between devices: 6.32 us -> none  [local(): pair = lax.all_to_all(pair, 'sample', 0, 0, tiled=True)]
  transfers between devices with their start and end apart: 41 -> 22, of which waited for: 9 -> 8; matrix products, arithmetic and copies ran while one was open for 0% -> 0% of each run, Pallas kernels for 21% -> 29%
where the time goes in v3:
time: 168 us; the launch traced here: 167 us
  Pallas kernels  66.4 us (40%)
  starting transfers between devices  47 us (28%)
  waiting for transfers between devices  26 us (15%)
  blocking collectives  23.5 us (14%)
  other arithmetic  2 us (1%)
    pallas_call x40, Pallas kernels, call(): pl.pallas_call(kernel, out_shape=out_shape, in_specs=in_specs, out_specs=...  46.5 us
    ppermute x18, starting transfers between devices, exchange(): self.recv[parity, period] = lax.ppermute(value, 'sample', pairs)  43.2 us
    pallas_call x4, Pallas kernels, whiten(): pl.pallas_call(whiten_kernel, grid_spec=pltpu.PrefetchScalarGridSpec(num_...  19.8 us
    all_to_all x1, blocking collectives, local(): share = lax.all_to_all(share, ('sample', 'landmark'), 0, 0, tiled=True)  11.8 us
    all_to_all x1, blocking collectives, local(): pair = lax.all_to_all(pair, 'sample', 0, 0, tiled=True)  11.7 us
    ppermute x18, waiting for transfers between devices, exchange(): self.recv[parity, period] = lax.ppermute(value, 'sample', pairs)  10.2 us
    ppermute x1, waiting for transfers between devices, local(): recv = lax.ppermute(sums[0], 'landmark', pairs_of(1))  8.06 us
    ppermute x1, waiting for transfers between devices, local(): recv = lax.ppermute(sent, 'landmark', pairs_of(t))  7.65 us
  transfers between devices with their start and end apart: 22, of which 8 were waited for; matrix products, arithmetic and copies ran while one was open for 0% of the time, Pallas kernels for 29%

profile of v3, /device:TPU:0, one launch (start us, length us, event | category | flops | bytes accessed | tf_op | source)
XLA Modules:
  0.0 167.3 jit_solution(786165007062288199)
XLA Ops:
  4.0 11.7 %all_to_all.10.pair_ref = f32[4,8,128]{2,1,0:T(8,128)S(1)} all-to-all(f32[4,8,128]{2,1,0:T(8,128)S(1)} %own_counts.1), channel_id=1, replica_groups=mesh['sample'=4,'landmark'=8] {'sample'}, dimensions={0} | all-to-all | bytes 32768 | tf_op jit(solution)/shard_map/all_to_all | solution.py:377
  15.8 5.6 %prepare_rows.1 = (bf16[1024,4096]{1,0:T(8,128)(2,1)S(1)}, bf16[256,4096]{1,0:T(8,128)(2,1)S(1)}, f32[1024,1]{1,0:T(8,128)S(1)}, bf16[512,1024]{1,0:T(8,128)(2,1)S(1)}, f32[1024,1]{1,0:T(8,128)S(1)}) custom-call(s32[1]{0:T(128)} %bitcast.1.here_ref, s32[4]{0:T(128)S(1)} %copy-done.1, f32[4,8,128]{2,1,0:T(8,128)S(1)} %all_to_all.10.pair_ref, ...), custom_call_target="tpu_custom_call" | custom-call | flops 12582912 | bytes 12582912 | tf_op jit(solution)/shard_map/prepare_rows/pallas_call | solution.py:27
  21.3 4.6 %moments.8 = (bf16[512,256]{1,0:T(8,128)(2,1)S(1)}, bf16[256,4096]{1,0:T(8,128)(2,1)S(1)}) custom-call(s32[1]{0:T(128)} %constant.26.clone.1.next_at_ref, bf16[1024,4096]{1,0:T(8,128)(2,1)S(1)} %get-tuple-element.45.x_ref, bf16[256,4096]{1,0:T(8,128)(2,1)S(1)} %get-tuple-element.48.z_ref, f32[1024,1]{1,0:T(8,128)S(1)} %get-tuple-element.49.scale_ref, ...), custom_call_target="tpu_custom_call" | custom-call | flops 2415919104 | bytes 2097152 | tf_op jit(solution)/shard_map/moments/pallas_call | solution.py:27
  26.7 4.6 %moments.9 = (bf16[512,256]{1,0:T(8,128)(2,1)S(1)}, bf16[256,4096]{1,0:T(8,128)(2,1)S(1)}) custom-call(s32[1]{0:T(128)} %constant.19.clone.1.next_at_ref, bf16[1024,4096]{1,0:T(8,128)(2,1)S(1)} %get-tuple-element.45.x_ref, bf16[256,4096]{1,0:T(8,128)(2,1)S(1)} %get-tuple-element.52.z_ref, f32[1024,1]{1,0:T(8,128)S(1)} %get-tuple-element.49.scale_ref, ...), custom_call_target="tpu_custom_call" | custom-call | flops 2415919104 | bytes 2097152 | tf_op jit(solution)/shard_map/moments/pallas_call | solution.py:27
  33.9 4.6 %moments.10 = (bf16[512,256]{1,0:T(8,128)(2,1)S(1)}, bf16[256,4096]{1,0:T(8,128)(2,1)S(1)}) custom-call(s32[1]{0:T(128)} %constant.20.clone.1.next_at_ref, bf16[1024,4096]{1,0:T(8,128)(2,1)S(1)} %get-tuple-element.45.x_ref, bf16[256,4096]{1,0:T(8,128)(2,1)S(1)} %get-tuple-element.54.z_ref, f32[1024,1]{1,0:T(8,128)S(1)} %get-tuple-element.49.scale_ref, ...), custom_call_target="tpu_custom_call" | custom-call | flops 2415919104 | bytes 2097152 | tf_op jit(solution)/shard_map/moments/pallas_call | solution.py:27
  39.3 5.0 %collective-permute-start.2 = (bf16[512,256]{1,0:T(8,128)(2,1)S(1)}, bf16[512,256]{1,0:T(8,128)(2,1)S(1)}, u32[]{:S(2)}, u32[]{:S(2)}) collective-permute-start(bf16[512,256]{1,0:T(8,128)(2,1)S(1)} %exchanged.20), channel_id=1, source_target_pairs={{0,8},{8,0},{16,24},{24,16},{1,9},{9,1},{17,25},{25,17},{2,10},{10... | collective-permute-start | bytes 786440 | tf_op jit(solution)/shard_map/ppermute | solution.py:324
  44.3 4.6 %moments.11 = (bf16[512,256]{1,0:T(8,128)(2,1)S(1)}, bf16[256,4096]{1,0:T(8,128)(2,1)S(1)}) custom-call(s32[1]{0:T(128)} %constant.21.clone.1.next_at_ref, bf16[1024,4096]{1,0:T(8,128)(2,1)S(1)} %get-tuple-element.45.x_ref, bf16[256,4096]{1,0:T(8,128)(2,1)S(1)} %get-tuple-element.58.z_ref, f32[1024,1]{1,0:T(8,128)S(1)} %get-tuple-element.49.scale_ref, ...), custom_call_target="tpu_custom_call" | custom-call | flops 2415919104 | bytes 2097152 | tf_op jit(solution)/shard_map/moments/pallas_call | solution.py:27
  51.0 4.6 %moments.12 = (bf16[512,256]{1,0:T(8,128)(2,1)S(1)}, bf16[256,4096]{1,0:T(8,128)(2,1)S(1)}) custom-call(s32[1]{0:T(128)} %constant.22.clone.1.next_at_ref, bf16[1024,4096]{1,0:T(8,128)(2,1)S(1)} %get-tuple-element.45.x_ref, bf16[256,4096]{1,0:T(8,128)(2,1)S(1)} %get-tuple-element.61.z_ref, f32[1024,1]{1,0:T(8,128)S(1)} %get-tuple-element.49.scale_ref, ...), custom_call_target="tpu_custom_call" | custom-call | flops 2415919104 | bytes 2097152 | tf_op jit(solution)/shard_map/moments/pallas_call | solution.py:27
  56.5 7.1 %collective-permute-start.7 = (bf16[512,256]{1,0:T(8,128)(2,1)S(1)}, bf16[512,256]{1,0:T(8,128)(2,1)S(1)}, u32[]{:S(2)}, u32[]{:S(2)}) collective-permute-start(bf16[512,256]{1,0:T(8,128)(2,1)S(1)} %exchanged.25), channel_id=1, source_target_pairs={{0,8},{8,0},{16,24},{24,16},{1,9},{9,1},{17,25},{25,17},{2,10},{10... | collective-permute-start | bytes 786440 | tf_op jit(solution)/shard_map/ppermute | solution.py:324
  63.6 4.6 %moments.13 = (bf16[512,256]{1,0:T(8,128)(2,1)S(1)}, bf16[256,4096]{1,0:T(8,128)(2,1)S(1)}) custom-call(s32[1]{0:T(128)} %constant.23.clone.1.next_at_ref, bf16[1024,4096]{1,0:T(8,128)(2,1)S(1)} %get-tuple-element.45.x_ref, bf16[256,4096]{1,0:T(8,128)(2,1)S(1)} %get-tuple-element.64.z_ref, f32[1024,1]{1,0:T(8,128)S(1)} %get-tuple-element.49.scale_ref, ...), custom_call_target="tpu_custom_call" | custom-call | flops 2415919104 | bytes 2097152 | tf_op jit(solution)/shard_map/moments/pallas_call | solution.py:27
  71.3 4.6 %moments.14 = (bf16[512,256]{1,0:T(8,128)(2,1)S(1)}, bf16[256,4096]{1,0:T(8,128)(2,1)S(1)}) custom-call(s32[1]{0:T(128)} %constant.54.clone.1.next_at_ref, bf16[1024,4096]{1,0:T(8,128)(2,1)S(1)} %get-tuple-element.45.x_ref, bf16[256,4096]{1,0:T(8,128)(2,1)S(1)} %get-tuple-element.67.z_ref, f32[1024,1]{1,0:T(8,128)S(1)} %get-tuple-element.49.scale_ref, ...), custom_call_target="tpu_custom_call" | custom-call | flops 2415919104 | bytes 2097152 | tf_op jit(solution)/shard_map/moments/pallas_call | solution.py:27
  76.7 4.6 %moments.15 = (bf16[512,256]{1,0:T(8,128)(2,1)S(1)}, bf16[256,4096]{1,0:T(8,128)(2,1)}) custom-call(s32[1]{0:T(128)} %constant.55.clone.1.next_at_ref, bf16[1024,4096]{1,0:T(8,128)(2,1)S(1)} %get-tuple-element.45.x_ref, bf16[256,4096]{1,0:T(8,128)(2,1)S(1)} %get-tuple-element.70.z_ref, f32[1024,1]{1,0:T(8,128)S(1)} %get-tuple-element.49.scale_ref, ...), custom_call_target="tpu_custom_call" | custom-call | flops 2415919104 | bytes 2097152 | tf_op jit(solution)/shard_map/moments/pallas_call | solution.py:27
  81.4 6.0 %collective-permute-start.11 = (bf16[512,256]{1,0:T(8,128)(2,1)S(1)}, bf16[512,256]{1,0:T(8,128)(2,1)S(1)}, u32[]{:S(2)}, u32[]{:S(2)}) collective-permute-start(bf16[512,256]{1,0:T(8,128)(2,1)S(1)} %exchanged.29), channel_id=1, source_target_pairs={{0,8},{8,0},{16,24},{24,16},{1,9},{9,1},{17,25},{25,17},{2,10},{10... | collective-permute-start | bytes 786440 | tf_op jit(solution)/shard_map/ppermute | solution.py:324
  91.7 2.8 %collective-permute-done.13.refs_0_.refs_1_ = bf16[512,256]{1,0:T(8,128)(2,1)S(1)} collective-permute-done((bf16[512,256]{1,0:T(8,128)(2,1)S(1)}, bf16[512,256]{1,0:T(8,128)(2,1)S(1)}, u32[]{:S(2)}, u32[]{:S(2)}) %collective-permute-start.13) | collective-permute-done | bytes 262176 | tf_op jit(solution)/shard_map/ppermute | solution.py:324
  96.1 8.9 %collective-permute-start.17 = (bf16[512,256]{1,0:T(8,128)(2,1)S(1)}, bf16[512,256]{1,0:T(8,128)(2,1)S(1)}, u32[]{:S(2)}, u32[]{:S(2)}) collective-permute-start(bf16[512,256]{1,0:T(8,128)(2,1)S(1)} %exchanged.35), channel_id=1, source_target_pairs={{0,8},{8,0},{16,24},{24,16},{1,9},{9,1},{17,25},{25,17},{2,10},{10... | collective-permute-start | bytes 786440 | tf_op jit(solution)/shard_map/ppermute | solution.py:324
  105.0 3.9 %collective-permute-start.15 = (bf16[512,256]{1,0:T(8,128)(2,1)S(1)}, bf16[512,256]{1,0:T(8,128)(2,1)S(1)}, u32[]{:S(2)}, u32[]{:S(2)}) collective-permute-start(bf16[512,256]{1,0:T(8,128)(2,1)S(1)} %exchanged.33), channel_id=1, source_target_pairs={{0,8},{8,0},{16,24},{24,16},{1,9},{9,1},{17,25},{25,17},{2,10},{10... | collective-permute-start | bytes 786440 | tf_op jit(solution)/shard_map/ppermute | solution.py:324
  109.3 4.0 %collective-permute-done.15.refs_0_ = bf16[512,256]{1,0:T(8,128)(2,1)S(1)} collective-permute-done((bf16[512,256]{1,0:T(8,128)(2,1)S(1)}, bf16[512,256]{1,0:T(8,128)(2,1)S(1)}, u32[]{:S(2)}, u32[]{:S(2)}) %collective-permute-start.15) | collective-permute-done | bytes 262176 | tf_op jit(solution)/shard_map/ppermute | solution.py:324
  113.6 5.0 %whiten.7 = bf16[2,512,512]{2,1,0:T(8,128)(2,1)S(1)} custom-call(s32[2]{0:T(128)S(1)} %get-tuple-element.42.refs_1_.table_ref, bf16[2048,4096]{1,0:T(8,128)(2,1)} %factor_ref.7, bf16[512,256]{1,0:T(8,128)(2,1)S(1)} %total.8.refs_3_.refs_2_.refs_0_, bf16[512,256]{1,0:T(8,128)(2,1)S(1)} %total.9.refs_3_.refs_2_.refs_1_, ...), custom_call_target="tpu_custom_call" | custom-call | flops 2147483648 | bytes 4194304 | tf_op jit(solution)/shard_map/whiten/pallas_call | solution.py:185
  118.6 5.0 %whiten.5 = bf16[2,512,512]{2,1,0:T(8,128)(2,1)S(1)} custom-call(s32[2]{0:T(128)S(1)} %get-tuple-element.44.refs_3_.table_ref, bf16[2048,4096]{1,0:T(8,128)(2,1)} %factor_ref.7, bf16[512,256]{1,0:T(8,128)(2,1)S(1)} %total.8.refs_3_.refs_2_.refs_0_, bf16[512,256]{1,0:T(8,128)(2,1)S(1)} %total.9.refs_3_.refs_2_.refs_1_, ...), custom_call_target="tpu_custom_call" | custom-call | flops 2147483648 | bytes 4194304 | tf_op jit(solution)/shard_map/whiten/pallas_call | solution.py:185
  124.1 5.0 %whiten.6.a_ref = bf16[2,512,512]{2,1,0:T(8,128)(2,1)S(1)} custom-call(s32[2]{0:T(128)S(1)} %get-tuple-element.43.refs_2_.table_ref, bf16[2048,4096]{1,0:T(8,128)(2,1)} %factor_ref.7, bf16[512,256]{1,0:T(8,128)(2,1)S(1)} %total.8.refs_3_.refs_2_.refs_0_, bf16[512,256]{1,0:T(8,128)(2,1)S(1)} %total.9.refs_3_.refs_2_.refs_1_, ...), custom_call_target="tpu_custom_call" | custom-call | flops 2147483648 | bytes 4194304 | tf_op jit(solution)/shard_map/whiten/pallas_call | solution.py:185
  130.9 5.0 %whiten.4.a_ref = bf16[2,512,512]{2,1,0:T(8,128)(2,1)S(1)} custom-call(s32[2]{0:T(128)S(1)} %get-tuple-element.39.refs_4_.table_ref, bf16[2048,4096]{1,0:T(8,128)(2,1)} %factor_ref.7, bf16[512,256]{1,0:T(8,128)(2,1)S(1)} %total.8.refs_3_.refs_2_.refs_0_, bf16[512,256]{1,0:T(8,128)(2,1)S(1)} %total.9.refs_3_.refs_2_.refs_1_, ...), custom_call_target="tpu_custom_call" | custom-call | flops 2147483648 | bytes 4194304 | tf_op jit(solution)/shard_map/whiten/pallas_call | solution.py:185
  136.2 8.1 %collective-permute-done.20.b_ref = bf16[2,512,512]{2,1,0:T(8,128)(2,1)S(1)} collective-permute-done((bf16[2,512,512]{2,1,0:T(8,128)(2,1)S(1)}, bf16[2,512,512]{2,1,0:T(8,128)(2,1)S(1)}, u32[]{:S(2)}, u32[]{:S(2)}) %collective-permute-start.20) | collective-permute-done | bytes 1048608 | tf_op jit(solution)/shard_map/ppermute | solution.py:403
  146.1 7.7 %collective-permute-done.21 = bf16[1,512,512]{2,1,0:T(8,128)(2,1)S(1)} collective-permute-done((bf16[1,512,512]{2,1,0:T(8,128)(2,1)S(1)}, bf16[1,512,512]{2,1,0:T(8,128)(2,1)S(1)}, u32[]{:S(2)}, u32[]{:S(2)}) %collective-permute-start.21) | collective-permute-done | bytes 524320 | tf_op jit(solution)/shard_map/ppermute | solution.py:408
  154.9 11.8 %all_to_all.11 = f32[32,4,128]{2,1,0:T(4,128)S(1)} all-to-all(f32[32,4,128]{2,1,0:T(4,128)S(1)} %get-tuple-element.75), channel_id=1, replica_groups=mesh['sample'=4,'landmark'=8] {'sample','landmark'}, dimensions={0} | all-to-all | bytes 131072 | tf_op jit(solution)/shard_map/all_to_all | solution.py:410
  (74 shorter events, 27.0 us)
Async XLA Ops:
  2.0 0.7 copy-start
  2.7 0.7 copy-start.1
  26.0 7.1 %collective-permute-start = (bf16[512,256]{1,0:T(8,128)(2,1)S(1)}, bf16[512,256]{1,0:T(8,128)(2,1)S(1)}, u32[]{:S(2)}, u32[]{:S(2)}) collective-permute-start(bf16[512,256]{1,0:T(8,128)(2,1)S(1)} %exchanged.18.rest_0_), channel_id=1, source_target_pairs={{0,8},{8,0},{16,24},{24,16},{1,9},{9,1},{17,25},{25,17},{2,10},{10... | collective-permute-start | bytes 786440 | tf_op jit(solution)/shard_map/ppermute | solution.py:324
  31.4 7.1 %collective-permute-start.3 = (bf16[512,256]{1,0:T(8,128)(2,1)S(1)}, bf16[512,256]{1,0:T(8,128)(2,1)S(1)}, u32[]{:S(2)}, u32[]{:S(2)}) collective-permute-start(bf16[512,256]{1,0:T(8,128)(2,1)S(1)} %exchanged.21), channel_id=1, source_target_pairs={{0,8},{8,0},{16,24},{24,16},{1,9},{9,1},{17,25},{25,17},{2,10},{10... | collective-permute-start | bytes 786440 | tf_op jit(solution)/shard_map/ppermute | solution.py:324
  33.2 6.1 %collective-permute-start.1 = (bf16[512,256]{1,0:T(8,128)(2,1)S(1)}, bf16[512,256]{1,0:T(8,128)(2,1)S(1)}, u32[]{:S(2)}, u32[]{:S(2)}) collective-permute-start(bf16[512,256]{1,0:T(8,128)(2,1)S(1)} %exchanged.19.rest_0_.refs_1_), channel_id=1, source_target_pairs={{8,16},{16,8},{9,17},{17,9},{10,18},{18,10},{11,19},{19,11},{12,20... | collective-permute-start | bytes 786440 | tf_op jit(solution)/shard_map/ppermute | solution.py:324
  38.6 10.3 %collective-permute-start.4 = (bf16[512,256]{1,0:T(8,128)(2,1)S(1)}, bf16[512,256]{1,0:T(8,128)(2,1)S(1)}, u32[]{:S(2)}, u32[]{:S(2)}) collective-permute-start(bf16[512,256]{1,0:T(8,128)(2,1)S(1)} %exchanged.22.rest_0_.refs_1_), channel_id=1, source_target_pairs={{8,16},{16,8},{9,17},{17,9},{10,18},{18,10},{11,19},{19,11},{12,20... | collective-permute-start | bytes 786440 | tf_op jit(solution)/shard_map/ppermute | solution.py:324
  39.3 10.7 %collective-permute-start.2 = (bf16[512,256]{1,0:T(8,128)(2,1)S(1)}, bf16[512,256]{1,0:T(8,128)(2,1)S(1)}, u32[]{:S(2)}, u32[]{:S(2)}) collective-permute-start(bf16[512,256]{1,0:T(8,128)(2,1)S(1)} %exchanged.20), channel_id=1, source_target_pairs={{0,8},{8,0},{16,24},{24,16},{1,9},{9,1},{17,25},{25,17},{2,10},{10... | collective-permute-start | bytes 786440 | tf_op jit(solution)/shard_map/ppermute | solution.py:324
  49.0 6.7 %collective-permute-start.5 = (bf16[512,256]{1,0:T(8,128)(2,1)S(1)}, bf16[512,256]{1,0:T(8,128)(2,1)S(1)}, u32[]{:S(2)}, u32[]{:S(2)}) collective-permute-start(bf16[512,256]{1,0:T(8,128)(2,1)S(1)} %exchanged.23), channel_id=1, source_target_pairs={{0,8},{8,0},{16,24},{24,16},{1,9},{9,1},{17,25},{25,17},{2,10},{10... | collective-permute-start | bytes 786440 | tf_op jit(solution)/shard_map/ppermute | solution.py:324
  50.1 6.3 %collective-permute-start.6 = (bf16[512,256]{1,0:T(8,128)(2,1)S(1)}, bf16[512,256]{1,0:T(8,128)(2,1)S(1)}, u32[]{:S(2)}, u32[]{:S(2)}) collective-permute-start(bf16[512,256]{1,0:T(8,128)(2,1)S(1)} %exchanged.24.rest_0_.refs_1_), channel_id=1, source_target_pairs={{8,16},{16,8},{9,17},{17,9},{10,18},{18,10},{11,19},{19,11},{12,20... | collective-permute-start | bytes 786440 | tf_op jit(solution)/shard_map/ppermute | solution.py:324
  55.7 12.5 %collective-permute-start.8 = (bf16[512,256]{1,0:T(8,128)(2,1)S(1)}, bf16[512,256]{1,0:T(8,128)(2,1)S(1)}, u32[]{:S(2)}, u32[]{:S(2)}) collective-permute-start(bf16[512,256]{1,0:T(8,128)(2,1)S(1)} %exchanged.26.rest_0_.refs_1_), channel_id=1, source_target_pairs={{8,16},{16,8},{9,17},{17,9},{10,18},{18,10},{11,19},{19,11},{12,20... | collective-permute-start | bytes 786440 | tf_op jit(solution)/shard_map/ppermute | solution.py:324
  56.5 14.0 %collective-permute-start.7 = (bf16[512,256]{1,0:T(8,128)(2,1)S(1)}, bf16[512,256]{1,0:T(8,128)(2,1)S(1)}, u32[]{:S(2)}, u32[]{:S(2)}) collective-permute-start(bf16[512,256]{1,0:T(8,128)(2,1)S(1)} %exchanged.25), channel_id=1, source_target_pairs={{0,8},{8,0},{16,24},{24,16},{1,9},{9,1},{17,25},{25,17},{2,10},{10... | collective-permute-start | bytes 786440 | tf_op jit(solution)/shard_map/ppermute | solution.py:324
  68.3 7.6 %collective-permute-start.9 = (bf16[512,256]{1,0:T(8,128)(2,1)S(1)}, bf16[512,256]{1,0:T(8,128)(2,1)S(1)}, u32[]{:S(2)}, u32[]{:S(2)}) collective-permute-start(bf16[512,256]{1,0:T(8,128)(2,1)S(1)} %exchanged.27), channel_id=1, source_target_pairs={{0,8},{8,0},{16,24},{24,16},{1,9},{9,1},{17,25},{25,17},{2,10},{10... | collective-permute-start | bytes 786440 | tf_op jit(solution)/shard_map/ppermute | solution.py:324
  70.6 10.7 %collective-permute-start.10 = (bf16[512,256]{1,0:T(8,128)(2,1)S(1)}, bf16[512,256]{1,0:T(8,128)(2,1)S(1)}, u32[]{:S(2)}, u32[]{:S(2)}) collective-permute-start(bf16[512,256]{1,0:T(8,128)(2,1)S(1)} %exchanged.28.rest_0_.refs_1_), channel_id=1, source_target_pairs={{8,16},{16,8},{9,17},{17,9},{10,18},{18,10},{11,19},{19,11},{12,20... | collective-permute-start | bytes 786440 | tf_op jit(solution)/shard_map/ppermute | solution.py:324
  76.0 11.3 %collective-permute-start.12 = (bf16[512,256]{1,0:T(8,128)(2,1)S(1)}, bf16[512,256]{1,0:T(8,128)(2,1)S(1)}, u32[]{:S(2)}, u32[]{:S(2)}) collective-permute-start(bf16[512,256]{1,0:T(8,128)(2,1)S(1)} %exchanged.30.rest_0_.refs_1_), channel_id=1, source_target_pairs={{8,16},{16,8},{9,17},{17,9},{10,18},{18,10},{11,19},{19,11},{12,20... | collective-permute-start | bytes 786440 | tf_op jit(solution)/shard_map/ppermute | solution.py:324
  81.4 10.3 %collective-permute-start.11 = (bf16[512,256]{1,0:T(8,128)(2,1)S(1)}, bf16[512,256]{1,0:T(8,128)(2,1)S(1)}, u32[]{:S(2)}, u32[]{:S(2)}) collective-permute-start(bf16[512,256]{1,0:T(8,128)(2,1)S(1)} %exchanged.29), channel_id=1, source_target_pairs={{0,8},{8,0},{16,24},{24,16},{1,9},{9,1},{17,25},{25,17},{2,10},{10... | collective-permute-start | bytes 786440 | tf_op jit(solution)/shard_map/ppermute | solution.py:324
  87.3 7.1 %collective-permute-start.13 = (bf16[512,256]{1,0:T(8,128)(2,1)S(1)}, bf16[512,256]{1,0:T(8,128)(2,1)S(1)}, u32[]{:S(2)}, u32[]{:S(2)}) collective-permute-start(bf16[512,256]{1,0:T(8,128)(2,1)S(1)} %exchanged.31), channel_id=1, source_target_pairs={{0,8},{8,0},{16,24},{24,16},{1,9},{9,1},{17,25},{25,17},{2,10},{10... | collective-permute-start | bytes 786440 | tf_op jit(solution)/shard_map/ppermute | solution.py:324
  94.5 1.5 collective-permute-start.16
  95.3 9.7 %collective-permute-start.14 = (bf16[512,256]{1,0:T(8,128)(2,1)S(1)}, bf16[512,256]{1,0:T(8,128)(2,1)S(1)}, u32[]{:S(2)}, u32[]{:S(2)}) collective-permute-start(bf16[512,256]{1,0:T(8,128)(2,1)S(1)} %exchanged.32.refs_0_.refs_1_), channel_id=1, source_target_pairs={{8,16},{16,8},{9,17},{17,9},{10,18},{18,10},{11,19},{19,11},{12,20... | collective-permute-start | bytes 786440 | tf_op jit(solution)/shard_map/ppermute | solution.py:324
  96.1 13.2 %collective-permute-start.17 = (bf16[512,256]{1,0:T(8,128)(2,1)S(1)}, bf16[512,256]{1,0:T(8,128)(2,1)S(1)}, u32[]{:S(2)}, u32[]{:S(2)}) collective-permute-start(bf16[512,256]{1,0:T(8,128)(2,1)S(1)} %exchanged.35), channel_id=1, source_target_pairs={{0,8},{8,0},{16,24},{24,16},{1,9},{9,1},{17,25},{25,17},{2,10},{10... | collective-permute-start | bytes 786440 | tf_op jit(solution)/shard_map/ppermute | solution.py:324
  105.0 8.3 %collective-permute-start.15 = (bf16[512,256]{1,0:T(8,128)(2,1)S(1)}, bf16[512,256]{1,0:T(8,128)(2,1)S(1)}, u32[]{:S(2)}, u32[]{:S(2)}) collective-permute-start(bf16[512,256]{1,0:T(8,128)(2,1)S(1)} %exchanged.33), channel_id=1, source_target_pairs={{0,8},{8,0},{16,24},{24,16},{1,9},{9,1},{17,25},{25,17},{2,10},{10... | collective-permute-start | bytes 786440 | tf_op jit(solution)/shard_map/ppermute | solution.py:324
  118.5 10.6 %collective-permute-start.19 = (bf16[2,512,512]{2,1,0:T(8,128)(2,1)S(1)}, bf16[2,512,512]{2,1,0:T(8,128)(2,1)S(1)}, u32[]{:S(2)}, u32[]{:S(2)}) collective-permute-start(bf16[2,512,512]{2,1,0:T(8,128)(2,1)S(1)} %whiten.7), channel_id=1, source_target_pairs={{0,1},{1,0},{2,3},{3,2},{4,5},{5,4},{6,7},{7,6},{8,9},{9,8},{10,11... | collective-permute-start | bytes 3145736 | tf_op jit(solution)/shard_map/ppermute | solution.py:399
  123.6 12.3 %collective-permute-start.18 = (bf16[2,512,512]{2,1,0:T(8,128)(2,1)S(1)}, bf16[2,512,512]{2,1,0:T(8,128)(2,1)S(1)}, u32[]{:S(2)}, u32[]{:S(2)}) collective-permute-start(bf16[2,512,512]{2,1,0:T(8,128)(2,1)S(1)} %whiten.5), channel_id=1, source_target_pairs={{0,1},{1,0},{2,3},{3,2},{4,5},{5,4},{6,7},{7,6},{8,9},{9,8},{10,11... | collective-permute-start | bytes 3145736 | tf_op jit(solution)/shard_map/ppermute | solution.py:399
  129.4 14.9 %collective-permute-start.20 = (bf16[2,512,512]{2,1,0:T(8,128)(2,1)S(1)}, bf16[2,512,512]{2,1,0:T(8,128)(2,1)S(1)}, u32[]{:S(2)}, u32[]{:S(2)}) collective-permute-start(bf16[2,512,512]{2,1,0:T(8,128)(2,1)S(1)} %add_blocks.4), channel_id=1, source_target_pairs={{0,2},{1,5},{2,0},{3,7},{4,6},{5,1},{6,4},{7,3},{8,10},{9,13},{10,... | collective-permute-start | bytes 3145736 | tf_op jit(solution)/shard_map/ppermute | solution.py:403
  144.5 9.2 %collective-permute-start.21 = (bf16[1,512,512]{2,1,0:T(8,128)(2,1)S(1)}, bf16[1,512,512]{2,1,0:T(8,128)(2,1)S(1)}, u32[]{:S(2)}, u32[]{:S(2)}) collective-permute-start(bf16[1,512,512]{2,1,0:T(8,128)(2,1)S(1)} %get-tuple-element.73), channel_id=1, source_target_pairs={{0,4},{1,3},{2,6},{3,1},{4,0},{5,7},{6,2},{7,5},{8,12},{9,11},{10,... | collective-permute-start | bytes 1572872 | tf_op jit(solution)/shard_map/ppermute | solution.py:408

commit v4 on v3

--- a/solution.py
+++ b/solution.py
@@ -8,7 +8,7 @@
 from jax.experimental.pallas import tpu as pltpu
 from jax.sharding import PartitionSpec as P
 
-VMEM_LIMIT = 14 * 1024 * 1024
+VMEM_LIMIT = 10 * 1024 * 1024
 TILE = 256
 NT = (((1,), (1,)), ((), ()))
 
@@ -49,59 +49,74 @@
     shape = labels_ref.shape
     slots = lax.broadcasted_iota(jnp.int32, shape, 0) * shape[1] + lax.broadcasted_iota(jnp.int32, shape, 1)
     mask_a, mask_b = slot_masks(labels_ref[...], own_count, slots)
-    first = lax.broadcasted_iota(jnp.int32, out_ref.shape[1:], 0) == 0
-    pair = jnp.where(first, jnp.sum(mask_a), jnp.sum(mask_b))
-    out_ref[...] = jnp.broadcast_to(pair[None], out_ref.shape)
-
-
-def own_counts(here, counts, labels, copies, after):
+    first = lax.broadcasted_iota(jnp.int32, out_ref.shape, 0) == 0
+    out_ref[...] = jnp.where(first, jnp.sum(mask_a), jnp.sum(mask_b))
+
+
+def own_counts(here, counts, labels, after):
     return call(
         counts_kernel,
         "own_counts",
-        jax.ShapeDtypeStruct((copies, 8, 128), jnp.float32),
+        jax.ShapeDtypeStruct((8, 128), jnp.float32),
         [SMEM, SMEM, VMEM] + [ANY] * len(after),
         (here, counts, labels.reshape(-1, 128), *after),
     )
 
 
-def rows_kernel(parts, here_ref, counts_ref, pair_ref, x_ref, z_ref, flips_ref, labels_ref,
-                held_ref, first_ref, scale_ref, signs_ref, weight_ref, flips_buf, x_sem, z_sem, f_sem):
+def weights_kernel(mask_a_ref, mask_b_ref, *refs):
+    out = refs[-1]
+    pair = refs[0][...]
+    for ref in refs[1:-1]:
+        pair = pair + ref[...]
+    count_a, count_b = pair[0:1, 0:1], pair[1:2, 0:1]
+    balance = jnp.sqrt(count_a * count_b / (count_a + count_b))
+    out[...] = mask_a_ref[...] * (balance / count_a) - mask_b_ref[...] * (balance / count_b)
+
+
+def row_weights(mask_a, mask_b, pairs):
+    out_shape = jax.ShapeDtypeStruct(mask_a.shape, jnp.float32)
+    return call(weights_kernel, "row_weights", out_shape, [VMEM] * (2 + len(pairs)), (mask_a, mask_b, *pairs))
+
+
+def rows_kernel(parts, here_ref, counts_ref, x_ref, z_ref, flips_ref, labels_ref,
+                held_x_ref, held_z_ref, scale_ref, signs_ref, mask_a_ref, mask_b_ref, flips_buf, x_sem, z_sem, f_sem):
     rows, width = x_ref.shape
     block = rows // parts
+    tile = z_ref.shape[0] // parts
 
     def x_copy(i):
         here = pl.ds(i * block, block)
-        return pltpu.make_async_copy(x_ref.at[here, :], held_ref.at[here, :], x_sem.at[i])
+        return pltpu.make_async_copy(x_ref.at[here, :], held_x_ref.at[here, :], x_sem.at[i])
+
+    def z_copy(i):
+        here = pl.ds(i * tile, tile)
+        return pltpu.make_async_copy(z_ref.at[here, :], held_z_ref.at[here, :], z_sem.at[i])
 
     flips_copy = pltpu.make_async_copy(flips_ref, flips_buf, f_sem)
-    z_copy = pltpu.make_async_copy(z_ref.at[pl.ds(0, first_ref.shape[0]), :], first_ref, z_sem)
     for i in range(parts):
         x_copy(i).start()
-    z_copy.start()
     flips_copy.start()
+    for i in range(parts):
+        z_copy(i).start()
     own_count = counts_ref[here_ref[0]]
-    pair = jnp.sum(pair_ref[...], axis=0)
-    count_a, count_b = pair[0:1, 0:1], pair[1:2, 0:1]
-    balance = jnp.sqrt(count_a * count_b / (count_a + count_b))
-    weight_a, weight_b = balance / count_a, balance / count_b
     for j in range(rows // 128):
         here = pl.ds(j * 128, 128)
         labels = jnp.transpose(jnp.broadcast_to(labels_ref[pl.ds(j, 1), :], (128, 128)))[:, 0:1]
         slots = j * 128 + lax.broadcasted_iota(jnp.int32, (128, 1), 0)
-        mask_a, mask_b = slot_masks(labels, own_count, slots)
-        weight_ref[here, :] = mask_a * weight_a - mask_b * weight_b
+        mask_a_ref[here, :], mask_b_ref[here, :] = slot_masks(labels, own_count, slots)
     for i in range(parts):
         x_copy(i).wait()
         here = pl.ds(i * block, block)
-        x = held_ref[here, :].astype(jnp.float32)
+        x = held_x_ref[here, :].astype(jnp.float32)
         mean = jnp.sum(x * x, axis=1, keepdims=True) * (1.0 / width)
         scale_ref[here, :] = lax.rsqrt(mean + 1e-06) * (0.5 / math.sqrt(width))
     flips_copy.wait()
     signs_ref[...] = (2 * flips_buf[...] - 1).astype(jnp.bfloat16)
-    z_copy.wait()
-
-
-def prepare_rows(here, counts, pair, x, z, flips, labels):
+    for i in range(parts):
+        z_copy(i).wait()
+
+
+def prepare_rows(here, counts, x, z, flips, labels):
     rows, width = x.shape
     perms = flips.shape[0]
     parts = 8
@@ -111,30 +126,28 @@
         "prepare_rows",
         [
             pltpu.VMEM((rows, width), x.dtype),
-            jax.ShapeDtypeStruct((TILE, width), z.dtype),
+            pltpu.VMEM(z.shape, z.dtype),
             column,
             jax.ShapeDtypeStruct((perms, rows), jnp.bfloat16),
             column,
+            column,
         ],
-        [SMEM, SMEM, VMEM, HBM, HBM, HBM, VMEM],
-        (here, counts, pair, in_hbm(x), in_hbm(z), in_hbm(flips), labels.reshape(-1, 128)),
+        [SMEM, SMEM, HBM, HBM, HBM, VMEM],
+        (here, counts, in_hbm(x), in_hbm(z), in_hbm(flips), labels.reshape(-1, 128)),
         flops=3 * rows * width,
-        bytes_accessed=(rows + TILE) * width * 2 + perms * rows * 4,
+        bytes_accessed=(rows + z.shape[0]) * width * 2 + perms * rows * 4,
         scratch=[
             pltpu.VMEM(flips.shape, flips.dtype),
             pltpu.SemaphoreType.DMA((parts,)),
-            pltpu.SemaphoreType.DMA,
+            pltpu.SemaphoreType.DMA((parts,)),
             pltpu.SemaphoreType.DMA,
         ],
     )
 
 
-def moments_kernel(after, next_at_ref, x_ref, z_ref, scale_ref, signs_ref, weight_ref, z_all_ref, *rest):
-    out_ref, next_ref, sem = rest[after:]
-    at = pl.multiple_of(next_at_ref[0], TILE)
-    next_copy = pltpu.make_async_copy(z_all_ref.at[pl.ds(at, TILE), :], next_ref, sem)
-    next_copy.start()
-    z = z_ref[...]
+def moments_kernel(first, x_ref, z_ref, scale_ref, signs_ref, weight_ref, *rest):
+    out_ref = rest[-1]
+    z = z_ref[pl.ds(first, TILE), :]
     z32 = z.astype(jnp.float32)
     mean = jnp.sum(z32 * z32, axis=1, keepdims=True) * (1.0 / z.shape[1])
     point = jnp.broadcast_to(lax.rsqrt(mean + 1e-06), (TILE, 128))
@@ -143,63 +156,72 @@
     kern = jnp.exp(cross * scale_ref[...] * point_row)
     weighted = (weight_ref[...] * kern).astype(jnp.bfloat16)
     out_ref[...] = jnp.dot(signs_ref[...], weighted, preferred_element_type=jnp.float32).astype(jnp.bfloat16)
-    next_copy.wait()
-
-
-def moments_part(next_at, x, z, scale, signs, weight, z_all, after):
+
+
+def moments_part(first, x, z, scale, signs, weight, after):
     rows, width = x.shape
     perms = signs.shape[0]
     return call(
-        functools.partial(moments_kernel, len(after)),
+        functools.partial(moments_kernel, first),
         "moments",
-        [
-            jax.ShapeDtypeStruct((perms, TILE), jnp.bfloat16),
-            jax.ShapeDtypeStruct((TILE, width), z.dtype),
-        ],
-        [SMEM] + [VMEM] * 5 + [HBM] + [ANY] * len(after),
-        (next_at, x, z, scale, signs, weight, in_hbm(z_all), *after),
+        jax.ShapeDtypeStruct((perms, TILE), jnp.bfloat16),
+        [VMEM] * 5 + [ANY] * len(after),
+        (x, z, scale, signs, weight, *after),
         flops=2 * rows * width * TILE + 2 * perms * rows * TILE,
         bytes_accessed=TILE * width * 2,
         transcendentals=rows * TILE,
-        scratch=[pltpu.SemaphoreType.DMA],
-    )
-
-
-def whiten_kernel(table_ref, factor_ref, *refs):
-    parts, (out, moments) = refs[:-2], refs[-2:]
-    piece = parts[0].shape[1]
-
-    @pl.when(pl.program_id(0) == 0)
-    def _():
-        for i, part in enumerate(parts):
-            moments[:, pl.ds(i * piece, piece)] = part[...]
-
-    out[0] = jnp.dot(moments[...], factor_ref[...], preferred_element_type=jnp.float32).astype(jnp.bfloat16)
-
-
-def whiten(table, factor, parts, blocks):
+    )
+
+
+def load_kernel(factor_ref, after_ref, held_ref, sem):
+    parts = sem.shape[0]
+    block = factor_ref.shape[0] // parts
+    copies = []
+    for i in range(parts):
+        here = pl.ds(i * block, block)
+        copies.append(pltpu.make_async_copy(factor_ref.at[here, :], held_ref.at[here, :], sem.at[i]))
+        copies[-1].start()
+    for copy in copies:
+        copy.wait()
+
+
+def load_factor(factor, after):
+    return call(
+        load_kernel,
+        "load_factor",
+        pltpu.VMEM(factor.shape, factor.dtype),
+        [HBM, ANY],
+        (in_hbm(factor), after),
+        bytes_accessed=factor.size * 2,
+        scratch=[pltpu.SemaphoreType.DMA((8,))],
+    )
+
+
+def whiten_kernel(table, count, spot_ref, factor_ref, *refs):
+    out = refs[-1]
+    moments = jnp.concatenate([part[...] for part in refs[:count]], axis=1)
+    wide = out.shape[2]
+    spot = spot_ref[0]
+    for i, (zero, one) in enumerate(table):
+        block = jnp.bitwise_xor(jnp.where(spot % 2 == 0, zero, one), spot)
+        here = pl.ds(pl.multiple_of(block * wide, wide), wide)
+        out[i] = jnp.dot(moments, factor_ref[:, here], preferred_element_type=jnp.float32).astype(jnp.bfloat16)
+
+
+def whiten(table, spot, factor, parts, blocks, after):
     depth, columns = factor.shape
     perms = parts[0].shape[0]
-    count = table.shape[0]
+    count = len(table)
     wide = columns // blocks
-    return pl.pallas_call(
-        whiten_kernel,
-        grid_spec=pltpu.PrefetchScalarGridSpec(
-            num_scalar_prefetch=1,
-            grid=(count,),
-            in_specs=[pl.BlockSpec((depth, wide), lambda i, t: (0, t[i]))] + [VMEM] * len(parts),
-            out_specs=pl.BlockSpec((1, perms, wide), lambda i, t: (i, 0, 0)),
-            scratch_shapes=[pltpu.VMEM((perms, depth), jnp.bfloat16)],
-        ),
-        out_shape=jax.ShapeDtypeStruct((count, perms, wide), jnp.bfloat16),
-        compiler_params=pltpu.CompilerParams(vmem_limit_bytes=VMEM_LIMIT),
-        cost_estimate=pl.CostEstimate(
-            flops=2 * perms * depth * wide * count,
-            bytes_accessed=depth * wide * count * 2,
-            transcendentals=0,
-        ),
-        name="whiten",
-    )(table, in_hbm(factor), *parts)
+    return call(
+        functools.partial(whiten_kernel, table, len(parts)),
+        "whiten",
+        jax.ShapeDtypeStruct((count, perms, wide), jnp.bfloat16),
+        [SMEM] + [VMEM] * (1 + len(parts)) + [ANY] * len(after),
+        (spot, factor, *parts, *after),
+        flops=2 * perms * depth * wide * count,
+        bytes_accessed=depth * wide * count * 2,
+    )
 
 
 def add_kernel(a_ref, b_ref, *outs):
@@ -345,9 +367,8 @@
     def local(embeddings, landmarks, factor, flips, labels, counts):
         here = lax.axis_index("sample").astype(jnp.int32)
         spot = lax.axis_index("landmark").astype(jnp.int32)
-        core = spot % 2
         depth = jnp.minimum(here, n_sample - 1 - here).reshape(1)
-        here = here.reshape(1)
+        here, spot = here.reshape(1), spot.reshape(1)
         points = landmarks.shape[0]
         perms = flips.shape[0]
         count = points // TILE
@@ -356,26 +377,20 @@
         kept_order = sorted(kept_places, key=lambda q: [-((q >> t) & 1) for t in range(1, bits)])
         sent_order = [q + 1 for q in kept_order]
 
-        def table_of(places, order_core):
-            zero = jnp.array([place_of(0, q) for q in places], jnp.int32)
-            one = jnp.array([place_of(1, q) for q in places], jnp.int32)
-            return jnp.bitwise_xor(jnp.where(order_core == 0, zero, one), spot)
+        def table_of(places, swapped):
+            cores = (1, 0) if swapped else (0, 1)
+            return [tuple(place_of(core, q) for core in cores) for q in places]
 
         def pairs_of(t):
             return [(m, m ^ (1 << order_of(m % 2)[t])) for m in range(n_landmark)]
 
-        middle = len(kept_order) // 2
-        tables = [
-            (table_of(sent_order[part], 1 - core), table_of(kept_order[part], core))
-            for part in (slice(0, middle), slice(middle, None))
-        ]
-        starts = [jnp.full((1,), (t + 1) % count * TILE, jnp.int32) for t in range(count)]
-        after = [depth, *starts, *tables[0], *tables[1]]
-        depth, *starts, first_sent, first_kept, second_sent, second_kept = lax.optimization_barrier(after)
-
-        pair = own_counts(here, counts, labels, n_sample, [depth, first_sent, first_kept, second_sent, second_kept])
-        pair = lax.all_to_all(pair, "sample", 0, 0, tiled=True)
-        held, z, scale, signs, weight = prepare_rows(here, counts, pair, embeddings, landmarks, flips, labels)
+        own_pair = own_counts(here, counts, labels, [depth, spot])
+        pairs = [own_pair]
+        for shift in range(1, n_sample):
+            to = [(i, (i + shift) % n_sample) for i in range(n_sample)]
+            pairs.append(lax.ppermute(own_pair, "sample", to))
+        x, z, scale, signs, mask_a, mask_b = prepare_rows(here, counts, embeddings, landmarks, flips, labels)
+        weight = row_weights(mask_a, mask_b, pairs)
 
         line = SampleSum(n_sample, depth)
         totals = []
@@ -383,21 +398,26 @@
         for t in range(count + n_sample - 2):
             if t < count:
                 after = [value] if t > 0 else []
-                piece, z = moments_part(starts[t], held, z, scale, signs, weight, landmarks, after)
-                line.pieces.append(piece)
+                line.pieces.append(moments_part(t * TILE, x, z, scale, signs, weight, after))
             after = totals[-1:] + line.pieces[-1:]
-            value = line.exchange(0, t, after)
-            odd = line.exchange(1, t, after)
-            value = value if odd is None else odd
+            if t == count:
+                held_factor = load_factor(factor, value)
+                after.append(held_factor)
+            for parity in (0, 1) if t < count else (1, 0):
+                sent = line.exchange(parity, t, after)
+                value = value if sent is None else sent
+                if t >= count:
+                    after = [value]
             if t >= n_sample - 1:
                 totals.append(line.total(t - (n_sample - 1)))
         totals.append(line.total(count - 1))
 
+        middle = len(kept_order) // 2
         sums = []
-        for sent_table, kept_table in ((first_sent, first_kept), (second_sent, second_kept)):
-            sent = whiten(sent_table, factor, totals, n_landmark)
+        for part in (slice(0, middle), slice(middle, None)):
+            sent = whiten(table_of(sent_order[part], True), spot, held_factor, totals, n_landmark, sums[-1:])
             recv = lax.ppermute(sent, "landmark", siblings)
-            kept = whiten(kept_table, factor, totals, n_landmark)
+            kept = whiten(table_of(kept_order[part], False), spot, held_factor, totals, n_landmark, [sent])
             (total,) = add_blocks(kept, recv, [kept.shape[0]])
             sums.append(total)
         recv = lax.ppermute(sums[0], "landmark", pairs_of(1))

time: 168 us -> 157 us (0.935)
  Pallas kernels: 66.4 us -> 54.5 us
  blocking collectives: 23.5 us -> 11.8 us
  starting transfers between devices: 47 us -> 54.6 us
  waiting for transfers between devices: 26 us -> 32.8 us
    pallas_call x4 -> x0, Pallas kernels: 19.8 us -> none  [whiten(): pl.pallas_call(whiten_kernel, grid_spec=pltpu.PrefetchScalarGridSpec(num_...]
    all_to_all x1 -> x0, blocking collectives: 11.7 us -> none  [local(): pair = lax.all_to_all(pair, 'sample', 0, 0, tiled=True)]
    pallas_call x40 -> x46, Pallas kernels: 46.5 us -> 54.5 us  [call(): pl.pallas_call(kernel, out_shape=out_shape, in_specs=in_specs, out_specs=...]
    ppermute x0 -> x3, starting transfers between devices: none -> 6.11 us  [local(): pairs.append(lax.ppermute(own_pair, 'sample', to))]
    ppermute x18, waiting for transfers between devices: 10.2 us -> 14 us  [exchange(): self.recv[parity, period] = lax.ppermute(value, 'sample', pairs)]
    ppermute x1, waiting for transfers between devices: 8.06 us -> 10.7 us  [local(): recv = lax.ppermute(sums[0], 'landmark', pairs_of(1))]
    ppermute x18, starting transfers between devices: 43.2 us -> 45.2 us  [exchange(): self.recv[parity, period] = lax.ppermute(value, 'sample', pairs)]
  transfers between devices with their start and end apart: 22 -> 25, of which waited for: 8 -> 8; matrix products, arithmetic and copies ran while one was open for 0% -> 0% of each run, Pallas kernels for 29% -> 28%
where the time goes in v4:
time: 157 us
  starting transfers between devices  54.6 us (35%)
  Pallas kernels  54.5 us (35%)
  waiting for transfers between devices  32.8 us (21%)
  blocking collectives  11.8 us (8%)
    pallas_call x46, Pallas kernels, call(): pl.pallas_call(kernel, out_shape=out_shape, in_specs=in_specs, out_specs=...  54.5 us
    ppermute x18, starting transfers between devices, exchange(): self.recv[parity, period] = lax.ppermute(value, 'sample', pairs)  45.2 us
    ppermute x18, waiting for transfers between devices, exchange(): self.recv[parity, period] = lax.ppermute(value, 'sample', pairs)  14 us
    all_to_all x1, blocking collectives, local(): share = lax.all_to_all(share, ('sample', 'landmark'), 0, 0, tiled=True)  11.8 us
    ppermute x1, waiting for transfers between devices, local(): recv = lax.ppermute(sums[0], 'landmark', pairs_of(1))  10.7 us
    ppermute x1, waiting for transfers between devices, local(): recv = lax.ppermute(sent, 'landmark', pairs_of(t))  7.7 us
    ppermute x3, starting transfers between devices, local(): pairs.append(lax.ppermute(own_pair, 'sample', to))  6.11 us
  transfers between devices with their start and end apart: 25, of which 8 were waited for; matrix products, arithmetic and copies ran while one was open for 0% of the time, Pallas kernels for 28%

profile of v4, /device:TPU:0, one launch (start us, length us, event | category | flops | bytes accessed | tf_op | source)
XLA Modules:
  0.0 156.8 jit_solution(14503302178294770989)
XLA Ops:
  2.7 5.1 %collective-permute-start.2 = (f32[8,128]{1,0:T(8,128)S(1)}, f32[8,128]{1,0:T(8,128)S(1)}, u32[]{:S(2)}, u32[]{:S(2)}) collective-permute-start(f32[8,128]{1,0:T(8,128)S(1)} %own_counts.1.refs_0_), channel_id=1, source_target_pairs={{0,24},{8,0},{16,8},{24,16},{1,25},{9,1},{17,9},{25,17},{2,26},{10... | collective-permute-start | bytes 12296 | tf_op jit(solution)/shard_map/ppermute | solution.py:391
  8.8 9.6 %prepare_rows.1 = (bf16[1024,4096]{1,0:T(8,128)(2,1)S(1)}, bf16[2048,4096]{1,0:T(8,128)(2,1)S(1)}, f32[1024,1]{1,0:T(8,128)S(1)}, bf16[512,1024]{1,0:T(8,128)(2,...) custom-call(s32[1]{0:T(128)} %bitcast.2.here_ref, s32[4]{0:T(128)S(1)} %copy-done.1, bf16[1024,4096]{1,0:T(8,128)(2,1)} %x_ref.1, ...), custom_call_target="tpu_custom_call" | custom-call | flops 12582912 | bytes 27262976 | tf_op jit(solution)/shard_map/prepare_rows/pallas_call | solution.py:27
  18.5 3.2 %moments.8.refs_0_.refs_1_ = bf16[512,256]{1,0:T(8,128)(2,1)S(1)} custom-call(bf16[1024,4096]{1,0:T(8,128)(2,1)S(1)} %get-tuple-element.12.x_ref, bf16[2048,4096]{1,0:T(8,128)(2,1)S(1)} %get-tuple-element.13.z_ref, f32[1024,1]{1,0:T(8,128)S(1)} %get-tuple-element.14.scale_ref, bf16[512,1024]{1,0:T(8,128)(2,1)S(1)} %get-tuple-element.15.signs_ref, ...), custom_call_target="tpu_custom_call" | custom-call | flops 2415919104 | bytes 2097152 | tf_op jit(solution)/shard_map/moments/pallas_call | solution.py:27
  21.7 2.5 %collective-permute-start.3 = (bf16[512,256]{1,0:T(8,128)(2,1)S(1)}, bf16[512,256]{1,0:T(8,128)(2,1)S(1)}, u32[]{:S(2)}, u32[]{:S(2)}) collective-permute-start(bf16[512,256]{1,0:T(8,128)(2,1)S(1)} %exchanged.18.rest_0_), channel_id=1, source_target_pairs={{0,8},{8,0},{16,24},{24,16},{1,9},{9,1},{17,25},{25,17},{2,10},{10... | collective-permute-start | bytes 786440 | tf_op jit(solution)/shard_map/ppermute | solution.py:346
  24.3 3.2 %moments.9.refs_2_.refs_0_.refs_1_ = bf16[512,256]{1,0:T(8,128)(2,1)S(1)} custom-call(bf16[1024,4096]{1,0:T(8,128)(2,1)S(1)} %get-tuple-element.12.x_ref, bf16[2048,4096]{1,0:T(8,128)(2,1)S(1)} %get-tuple-element.13.z_ref, f32[1024,1]{1,0:T(8,128)S(1)} %get-tuple-element.14.scale_ref, bf16[512,1024]{1,0:T(8,128)(2,1)S(1)} %get-tuple-element.15.signs_ref, ...), custom_call_target="tpu_custom_call" | custom-call | flops 2415919104 | bytes 2097152 | tf_op jit(solution)/shard_map/moments/pallas_call | solution.py:27
  27.6 3.4 %collective-permute-done.3.refs_1_ = bf16[512,256]{1,0:T(8,128)(2,1)S(1)} collective-permute-done((bf16[512,256]{1,0:T(8,128)(2,1)S(1)}, bf16[512,256]{1,0:T(8,128)(2,1)S(1)}, u32[]{:S(2)}, u32[]{:S(2)}) %collective-permute-start.3) | collective-permute-done | bytes 262176 | tf_op jit(solution)/shard_map/ppermute | solution.py:346
  31.8 3.2 %moments.10.refs_0_.refs_3_.refs_2_ = bf16[512,256]{1,0:T(8,128)(2,1)S(1)} custom-call(bf16[1024,4096]{1,0:T(8,128)(2,1)S(1)} %get-tuple-element.12.x_ref, bf16[2048,4096]{1,0:T(8,128)(2,1)S(1)} %get-tuple-element.13.z_ref, f32[1024,1]{1,0:T(8,128)S(1)} %get-tuple-element.14.scale_ref, bf16[512,1024]{1,0:T(8,128)(2,1)S(1)} %get-tuple-element.15.signs_ref, ...), custom_call_target="tpu_custom_call" | custom-call | flops 2415919104 | bytes 2097152 | tf_op jit(solution)/shard_map/moments/pallas_call | solution.py:27
  36.1 8.0 %collective-permute-start.5 = (bf16[512,256]{1,0:T(8,128)(2,1)S(1)}, bf16[512,256]{1,0:T(8,128)(2,1)S(1)}, u32[]{:S(2)}, u32[]{:S(2)}) collective-permute-start(bf16[512,256]{1,0:T(8,128)(2,1)S(1)} %exchanged.20), channel_id=1, source_target_pairs={{0,8},{8,0},{16,24},{24,16},{1,9},{9,1},{17,25},{25,17},{2,10},{10... | collective-permute-start | bytes 786440 | tf_op jit(solution)/shard_map/ppermute | solution.py:346
  44.2 3.2 %moments.11.refs_2_.refs_0_.refs_3_ = bf16[512,256]{1,0:T(8,128)(2,1)S(1)} custom-call(bf16[1024,4096]{1,0:T(8,128)(2,1)S(1)} %get-tuple-element.12.x_ref, bf16[2048,4096]{1,0:T(8,128)(2,1)S(1)} %get-tuple-element.13.z_ref, f32[1024,1]{1,0:T(8,128)S(1)} %get-tuple-element.14.scale_ref, bf16[512,1024]{1,0:T(8,128)(2,1)S(1)} %get-tuple-element.15.signs_ref, ...), custom_call_target="tpu_custom_call" | custom-call | flops 2415919104 | bytes 2097152 | tf_op jit(solution)/shard_map/moments/pallas_call | solution.py:27
  47.6 3.4 %collective-permute-done.5.refs_1_.refs_0_ = bf16[512,256]{1,0:T(8,128)(2,1)S(1)} collective-permute-done((bf16[512,256]{1,0:T(8,128)(2,1)S(1)}, bf16[512,256]{1,0:T(8,128)(2,1)S(1)}, u32[]{:S(2)}, u32[]{:S(2)}) %collective-permute-start.5) | collective-permute-done | bytes 262176 | tf_op jit(solution)/shard_map/ppermute | solution.py:346
  52.0 3.2 %moments.12.refs_0_.refs_4_.refs_3_ = bf16[512,256]{1,0:T(8,128)(2,1)S(1)} custom-call(bf16[1024,4096]{1,0:T(8,128)(2,1)S(1)} %get-tuple-element.12.x_ref, bf16[2048,4096]{1,0:T(8,128)(2,1)S(1)} %get-tuple-element.13.z_ref, f32[1024,1]{1,0:T(8,128)S(1)} %get-tuple-element.14.scale_ref, bf16[512,1024]{1,0:T(8,128)(2,1)S(1)} %get-tuple-element.15.signs_ref, ...), custom_call_target="tpu_custom_call" | custom-call | flops 2415919104 | bytes 2097152 | tf_op jit(solution)/shard_map/moments/pallas_call | solution.py:27
  56.0 7.8 %collective-permute-start.8 = (bf16[512,256]{1,0:T(8,128)(2,1)S(1)}, bf16[512,256]{1,0:T(8,128)(2,1)S(1)}, u32[]{:S(2)}, u32[]{:S(2)}) collective-permute-start(bf16[512,256]{1,0:T(8,128)(2,1)S(1)} %exchanged.24), channel_id=1, source_target_pairs={{0,8},{8,0},{16,24},{24,16},{1,9},{9,1},{17,25},{25,17},{2,10},{10... | collective-permute-start | bytes 786440 | tf_op jit(solution)/shard_map/ppermute | solution.py:346
  63.9 3.2 %moments.13.refs_3_.refs_0_.refs_4_ = bf16[512,256]{1,0:T(8,128)(2,1)S(1)} custom-call(bf16[1024,4096]{1,0:T(8,128)(2,1)S(1)} %get-tuple-element.12.x_ref, bf16[2048,4096]{1,0:T(8,128)(2,1)S(1)} %get-tuple-element.13.z_ref, f32[1024,1]{1,0:T(8,128)S(1)} %get-tuple-element.14.scale_ref, bf16[512,1024]{1,0:T(8,128)(2,1)S(1)} %get-tuple-element.15.signs_ref, ...), custom_call_target="tpu_custom_call" | custom-call | flops 2415919104 | bytes 2097152 | tf_op jit(solution)/shard_map/moments/pallas_call | solution.py:27
  70.6 3.2 %moments.14.refs_0_.refs_4_.refs_3_ = bf16[512,256]{1,0:T(8,128)(2,1)S(1)} custom-call(bf16[1024,4096]{1,0:T(8,128)(2,1)S(1)} %get-tuple-element.12.x_ref, bf16[2048,4096]{1,0:T(8,128)(2,1)S(1)} %get-tuple-element.13.z_ref, f32[1024,1]{1,0:T(8,128)S(1)} %get-tuple-element.14.scale_ref, bf16[512,1024]{1,0:T(8,128)(2,1)S(1)} %get-tuple-element.15.signs_ref, ...), custom_call_target="tpu_custom_call" | custom-call | flops 2415919104 | bytes 2097152 | tf_op jit(solution)/shard_map/moments/pallas_call | solution.py:27
  74.6 6.4 %collective-permute-start.12 = (bf16[512,256]{1,0:T(8,128)(2,1)S(1)}, bf16[512,256]{1,0:T(8,128)(2,1)S(1)}, u32[]{:S(2)}, u32[]{:S(2)}) collective-permute-start(bf16[512,256]{1,0:T(8,128)(2,1)S(1)} %exchanged.28), channel_id=1, source_target_pairs={{0,8},{8,0},{16,24},{24,16},{1,9},{9,1},{17,25},{25,17},{2,10},{10... | collective-permute-start | bytes 786440 | tf_op jit(solution)/shard_map/ppermute | solution.py:346
  81.0 3.2 %moments.15.refs_3_.refs_0_.refs_4_ = bf16[512,256]{1,0:T(8,128)(2,1)S(1)} custom-call(bf16[1024,4096]{1,0:T(8,128)(2,1)S(1)} %get-tuple-element.12.x_ref, bf16[2048,4096]{1,0:T(8,128)(2,1)S(1)} %get-tuple-element.13.z_ref, f32[1024,1]{1,0:T(8,128)S(1)} %get-tuple-element.14.scale_ref, bf16[512,1024]{1,0:T(8,128)(2,1)S(1)} %get-tuple-element.15.signs_ref, ...), custom_call_target="tpu_custom_call" | custom-call | flops 2415919104 | bytes 2097152 | tf_op jit(solution)/shard_map/moments/pallas_call | solution.py:27
  84.3 4.4 %collective-permute-start.16 = (bf16[512,256]{1,0:T(8,128)(2,1)S(1)}, bf16[512,256]{1,0:T(8,128)(2,1)S(1)}, u32[]{:S(2)}, u32[]{:S(2)}) collective-permute-start(bf16[512,256]{1,0:T(8,128)(2,1)S(1)} %exchanged.32), channel_id=1, source_target_pairs={{0,8},{8,0},{16,24},{24,16},{1,9},{9,1},{17,25},{25,17},{2,10},{10... | collective-permute-start | bytes 786440 | tf_op jit(solution)/shard_map/ppermute | solution.py:346
  89.5 5.9 %load_factor.1.refs_4_.factor_ref = bf16[2048,4096]{1,0:T(8,128)(2,1)S(1)} custom-call(bf16[2048,4096]{1,0:T(8,128)(2,1)} %factor_ref.1, bf16[512,256]{1,0:T(8,128)(2,1)S(1)} %exchanged.31.after_ref.refs_0_.refs_1_), custom_call_target="tpu_custom_call" | custom-call | bytes 16777216 | tf_op jit(solution)/shard_map/load_factor/pallas_call | solution.py:27
  96.3 4.6 %collective-permute-start.18 = (bf16[512,256]{1,0:T(8,128)(2,1)S(1)}, bf16[512,256]{1,0:T(8,128)(2,1)S(1)}, u32[]{:S(2)}, u32[]{:S(2)}) collective-permute-start(bf16[512,256]{1,0:T(8,128)(2,1)S(1)} %exchanged.34.refs_2_), channel_id=1, source_target_pairs={{0,8},{8,0},{16,24},{24,16},{1,9},{9,1},{17,25},{25,17},{2,10},{10... | collective-permute-start | bytes 786440 | tf_op jit(solution)/shard_map/ppermute | solution.py:346
  101.0 5.4 %collective-permute-start.20 = (bf16[512,256]{1,0:T(8,128)(2,1)S(1)}, bf16[512,256]{1,0:T(8,128)(2,1)S(1)}, u32[]{:S(2)}, u32[]{:S(2)}) collective-permute-start(bf16[512,256]{1,0:T(8,128)(2,1)S(1)} %exchanged.35), channel_id=1, source_target_pairs={{0,8},{8,0},{16,24},{24,16},{1,9},{9,1},{17,25},{25,17},{2,10},{10... | collective-permute-start | bytes 786440 | tf_op jit(solution)/shard_map/ppermute | solution.py:346
  106.4 4.3 %collective-permute-done.20.refs_0_ = bf16[512,256]{1,0:T(8,128)(2,1)S(1)} collective-permute-done((bf16[512,256]{1,0:T(8,128)(2,1)S(1)}, bf16[512,256]{1,0:T(8,128)(2,1)S(1)}, u32[]{:S(2)}, u32[]{:S(2)}) %collective-permute-start.20) | collective-permute-done | bytes 262176 | tf_op jit(solution)/shard_map/ppermute | solution.py:346
  123.0 10.7 %collective-permute-done.23.b_ref = bf16[2,512,512]{2,1,0:T(8,128)(2,1)S(1)} collective-permute-done((bf16[2,512,512]{2,1,0:T(8,128)(2,1)S(1)}, bf16[2,512,512]{2,1,0:T(8,128)(2,1)S(1)}, u32[]{:S(2)}, u32[]{:S(2)}) %collective-permute-start.23) | collective-permute-done | bytes 1048608 | tf_op jit(solution)/shard_map/ppermute | solution.py:423
  135.5 7.7 %collective-permute-done.24 = bf16[1,512,512]{2,1,0:T(8,128)(2,1)S(1)} collective-permute-done((bf16[1,512,512]{2,1,0:T(8,128)(2,1)S(1)}, bf16[1,512,512]{2,1,0:T(8,128)(2,1)S(1)}, u32[]{:S(2)}, u32[]{:S(2)}) %collective-permute-start.24) | collective-permute-done | bytes 524320 | tf_op jit(solution)/shard_map/ppermute | solution.py:428
  144.3 11.8 %all_to_all.5 = f32[32,4,128]{2,1,0:T(4,128)S(1)} all-to-all(f32[32,4,128]{2,1,0:T(4,128)S(1)} %get-tuple-element.21), channel_id=1, replica_groups=mesh['sample'=4,'landmark'=8] {'sample','landmark'}, dimensions={0} | all-to-all | bytes 131072 | tf_op jit(solution)/shard_map/all_to_all | solution.py:430
  (79 shorter events, 28.8 us)
Async XLA Ops:
  2.7 15.7 %collective-permute-start.2 = (f32[8,128]{1,0:T(8,128)S(1)}, f32[8,128]{1,0:T(8,128)S(1)}, u32[]{:S(2)}, u32[]{:S(2)}) collective-permute-start(f32[8,128]{1,0:T(8,128)S(1)} %own_counts.1.refs_0_), channel_id=1, source_target_pairs={{0,24},{8,0},{16,8},{24,16},{1,25},{9,1},{17,9},{25,17},{2,26},{10... | collective-permute-start | bytes 12296 | tf_op jit(solution)/shard_map/ppermute | solution.py:391
  7.8 10.6 %collective-permute-start.1 = (f32[8,128]{1,0:T(8,128)S(1)}, f32[8,128]{1,0:T(8,128)S(1)}, u32[]{:S(2)}, u32[]{:S(2)}) collective-permute-start(f32[8,128]{1,0:T(8,128)S(1)} %own_counts.1.refs_0_), channel_id=1, source_target_pairs={{0,16},{8,24},{16,0},{24,8},{1,17},{9,25},{17,1},{25,9},{2,18},{10... | collective-permute-start | bytes 12296 | tf_op jit(solution)/shard_map/ppermute | solution.py:391
  7.8 10.6 %collective-permute-start = (f32[8,128]{1,0:T(8,128)S(1)}, f32[8,128]{1,0:T(8,128)S(1)}, u32[]{:S(2)}, u32[]{:S(2)}) collective-permute-start(f32[8,128]{1,0:T(8,128)S(1)} %own_counts.1.refs_0_), channel_id=1, source_target_pairs={{0,8},{8,16},{16,24},{24,0},{1,9},{9,17},{17,25},{25,1},{2,10},{10... | collective-permute-start | bytes 12296 | tf_op jit(solution)/shard_map/ppermute | solution.py:391
  21.7 9.3 %collective-permute-start.3 = (bf16[512,256]{1,0:T(8,128)(2,1)S(1)}, bf16[512,256]{1,0:T(8,128)(2,1)S(1)}, u32[]{:S(2)}, u32[]{:S(2)}) collective-permute-start(bf16[512,256]{1,0:T(8,128)(2,1)S(1)} %exchanged.18.rest_0_), channel_id=1, source_target_pairs={{0,8},{8,0},{16,24},{24,16},{1,9},{9,1},{17,25},{25,17},{2,10},{10... | collective-permute-start | bytes 786440 | tf_op jit(solution)/shard_map/ppermute | solution.py:346
  27.5 7.8 %collective-permute-start.6 = (bf16[512,256]{1,0:T(8,128)(2,1)S(1)}, bf16[512,256]{1,0:T(8,128)(2,1)S(1)}, u32[]{:S(2)}, u32[]{:S(2)}) collective-permute-start(bf16[512,256]{1,0:T(8,128)(2,1)S(1)} %exchanged.21), channel_id=1, source_target_pairs={{0,8},{8,0},{16,24},{24,16},{1,9},{9,1},{17,25},{25,17},{2,10},{10... | collective-permute-start | bytes 786440 | tf_op jit(solution)/shard_map/ppermute | solution.py:346
  31.1 5.0 %collective-permute-start.4 = (bf16[512,256]{1,0:T(8,128)(2,1)S(1)}, bf16[512,256]{1,0:T(8,128)(2,1)S(1)}, u32[]{:S(2)}, u32[]{:S(2)}) collective-permute-start(bf16[512,256]{1,0:T(8,128)(2,1)S(1)} %exchanged.19.rest_0_.refs_1_), channel_id=1, source_target_pairs={{8,16},{16,8},{9,17},{17,9},{10,18},{18,10},{11,19},{19,11},{12,20... | collective-permute-start | bytes 786440 | tf_op jit(solution)/shard_map/ppermute | solution.py:346
  35.4 12.0 %collective-permute-start.9 = (bf16[512,256]{1,0:T(8,128)(2,1)S(1)}, bf16[512,256]{1,0:T(8,128)(2,1)S(1)}, u32[]{:S(2)}, u32[]{:S(2)}) collective-permute-start(bf16[512,256]{1,0:T(8,128)(2,1)S(1)} %exchanged.22.rest_0_.refs_1_), channel_id=1, source_target_pairs={{8,16},{16,8},{9,17},{17,9},{10,18},{18,10},{11,19},{19,11},{12,20... | collective-permute-start | bytes 786440 | tf_op jit(solution)/shard_map/ppermute | solution.py:346
  36.1 14.9 %collective-permute-start.5 = (bf16[512,256]{1,0:T(8,128)(2,1)S(1)}, bf16[512,256]{1,0:T(8,128)(2,1)S(1)}, u32[]{:S(2)}, u32[]{:S(2)}) collective-permute-start(bf16[512,256]{1,0:T(8,128)(2,1)S(1)} %exchanged.20), channel_id=1, source_target_pairs={{0,8},{8,0},{16,24},{24,16},{1,9},{9,1},{17,25},{25,17},{2,10},{10... | collective-permute-start | bytes 786440 | tf_op jit(solution)/shard_map/ppermute | solution.py:346
  47.4 7.8 %collective-permute-start.10 = (bf16[512,256]{1,0:T(8,128)(2,1)S(1)}, bf16[512,256]{1,0:T(8,128)(2,1)S(1)}, u32[]{:S(2)}, u32[]{:S(2)}) collective-permute-start(bf16[512,256]{1,0:T(8,128)(2,1)S(1)} %exchanged.25), channel_id=1, source_target_pairs={{0,8},{8,0},{16,24},{24,16},{1,9},{9,1},{17,25},{25,17},{2,10},{10... | collective-permute-start | bytes 786440 | tf_op jit(solution)/shard_map/ppermute | solution.py:346
  51.1 4.9 %collective-permute-start.7 = (bf16[512,256]{1,0:T(8,128)(2,1)S(1)}, bf16[512,256]{1,0:T(8,128)(2,1)S(1)}, u32[]{:S(2)}, u32[]{:S(2)}) collective-permute-start(bf16[512,256]{1,0:T(8,128)(2,1)S(1)} %exchanged.23.rest_0_.refs_1_), channel_id=1, source_target_pairs={{8,16},{16,8},{9,17},{17,9},{10,18},{18,10},{11,19},{19,11},{12,20... | collective-permute-start | bytes 786440 | tf_op jit(solution)/shard_map/ppermute | solution.py:346
  55.3 11.8 %collective-permute-start.13 = (bf16[512,256]{1,0:T(8,128)(2,1)S(1)}, bf16[512,256]{1,0:T(8,128)(2,1)S(1)}, u32[]{:S(2)}, u32[]{:S(2)}) collective-permute-start(bf16[512,256]{1,0:T(8,128)(2,1)S(1)} %exchanged.26.rest_0_.refs_1_), channel_id=1, source_target_pairs={{8,16},{16,8},{9,17},{17,9},{10,18},{18,10},{11,19},{19,11},{12,20... | collective-permute-start | bytes 786440 | tf_op jit(solution)/shard_map/ppermute | solution.py:346
  56.0 13.8 %collective-permute-start.8 = (bf16[512,256]{1,0:T(8,128)(2,1)S(1)}, bf16[512,256]{1,0:T(8,128)(2,1)S(1)}, u32[]{:S(2)}, u32[]{:S(2)}) collective-permute-start(bf16[512,256]{1,0:T(8,128)(2,1)S(1)} %exchanged.24), channel_id=1, source_target_pairs={{0,8},{8,0},{16,24},{24,16},{1,9},{9,1},{17,25},{25,17},{2,10},{10... | collective-permute-start | bytes 786440 | tf_op jit(solution)/shard_map/ppermute | solution.py:346
  67.1 6.7 %collective-permute-start.14 = (bf16[512,256]{1,0:T(8,128)(2,1)S(1)}, bf16[512,256]{1,0:T(8,128)(2,1)S(1)}, u32[]{:S(2)}, u32[]{:S(2)}) collective-permute-start(bf16[512,256]{1,0:T(8,128)(2,1)S(1)} %exchanged.29), channel_id=1, source_target_pairs={{0,8},{8,0},{16,24},{24,16},{1,9},{9,1},{17,25},{25,17},{2,10},{10... | collective-permute-start | bytes 786440 | tf_op jit(solution)/shard_map/ppermute | solution.py:346
  69.9 4.7 %collective-permute-start.11 = (bf16[512,256]{1,0:T(8,128)(2,1)S(1)}, bf16[512,256]{1,0:T(8,128)(2,1)S(1)}, u32[]{:S(2)}, u32[]{:S(2)}) collective-permute-start(bf16[512,256]{1,0:T(8,128)(2,1)S(1)} %exchanged.27.rest_0_.refs_1_), channel_id=1, source_target_pairs={{8,16},{16,8},{9,17},{17,9},{10,18},{18,10},{11,19},{19,11},{12,20... | collective-permute-start | bytes 786440 | tf_op jit(solution)/shard_map/ppermute | solution.py:346
  73.9 10.4 %collective-permute-start.15 = (bf16[512,256]{1,0:T(8,128)(2,1)S(1)}, bf16[512,256]{1,0:T(8,128)(2,1)S(1)}, u32[]{:S(2)}, u32[]{:S(2)}) collective-permute-start(bf16[512,256]{1,0:T(8,128)(2,1)S(1)} %exchanged.30.rest_0_.refs_1_), channel_id=1, source_target_pairs={{8,16},{16,8},{9,17},{17,9},{10,18},{18,10},{11,19},{19,11},{12,20... | collective-permute-start | bytes 786440 | tf_op jit(solution)/shard_map/ppermute | solution.py:346
  74.6 14.1 %collective-permute-start.12 = (bf16[512,256]{1,0:T(8,128)(2,1)S(1)}, bf16[512,256]{1,0:T(8,128)(2,1)S(1)}, u32[]{:S(2)}, u32[]{:S(2)}) collective-permute-start(bf16[512,256]{1,0:T(8,128)(2,1)S(1)} %exchanged.28), channel_id=1, source_target_pairs={{0,8},{8,0},{16,24},{24,16},{1,9},{9,1},{17,25},{25,17},{2,10},{10... | collective-permute-start | bytes 786440 | tf_op jit(solution)/shard_map/ppermute | solution.py:346
  84.3 11.1 %collective-permute-start.16 = (bf16[512,256]{1,0:T(8,128)(2,1)S(1)}, bf16[512,256]{1,0:T(8,128)(2,1)S(1)}, u32[]{:S(2)}, u32[]{:S(2)}) collective-permute-start(bf16[512,256]{1,0:T(8,128)(2,1)S(1)} %exchanged.32), channel_id=1, source_target_pairs={{0,8},{8,0},{16,24},{24,16},{1,9},{9,1},{17,25},{25,17},{2,10},{10... | collective-permute-start | bytes 786440 | tf_op jit(solution)/shard_map/ppermute | solution.py:346
  88.8 7.4 %collective-permute-start.17 = (bf16[512,256]{1,0:T(8,128)(2,1)S(1)}, bf16[512,256]{1,0:T(8,128)(2,1)S(1)}, u32[]{:S(2)}, u32[]{:S(2)}) collective-permute-start(bf16[512,256]{1,0:T(8,128)(2,1)S(1)} %exchanged.31.after_ref.refs_0_.refs_1_), channel_id=1, source_target_pairs={{8,16},{16,8},{9,17},{17,9},{10,18},{18,10},{11,19},{19,11},{12,20... | collective-permute-start | bytes 786440 | tf_op jit(solution)/shard_map/ppermute | solution.py:346
  95.5 5.4 %collective-permute-start.19 = (bf16[512,256]{1,0:T(8,128)(2,1)S(1)}, bf16[512,256]{1,0:T(8,128)(2,1)S(1)}, u32[]{:S(2)}, u32[]{:S(2)}) collective-permute-start(bf16[512,256]{1,0:T(8,128)(2,1)S(1)} %exchanged.33.refs_2_.refs_0_.refs_1_), channel_id=1, source_target_pairs={{8,16},{16,8},{9,17},{17,9},{10,18},{18,10},{11,19},{19,11},{12,20... | collective-permute-start | bytes 786440 | tf_op jit(solution)/shard_map/ppermute | solution.py:346
  96.3 10.1 %collective-permute-start.18 = (bf16[512,256]{1,0:T(8,128)(2,1)S(1)}, bf16[512,256]{1,0:T(8,128)(2,1)S(1)}, u32[]{:S(2)}, u32[]{:S(2)}) collective-permute-start(bf16[512,256]{1,0:T(8,128)(2,1)S(1)} %exchanged.34.refs_2_), channel_id=1, source_target_pairs={{0,8},{8,0},{16,24},{24,16},{1,9},{9,1},{17,25},{25,17},{2,10},{10... | collective-permute-start | bytes 786440 | tf_op jit(solution)/shard_map/ppermute | solution.py:346
  101.0 9.7 %collective-permute-start.20 = (bf16[512,256]{1,0:T(8,128)(2,1)S(1)}, bf16[512,256]{1,0:T(8,128)(2,1)S(1)}, u32[]{:S(2)}, u32[]{:S(2)}) collective-permute-start(bf16[512,256]{1,0:T(8,128)(2,1)S(1)} %exchanged.35), channel_id=1, source_target_pairs={{0,8},{8,0},{16,24},{24,16},{1,9},{9,1},{17,25},{25,17},{2,10},{10... | collective-permute-start | bytes 786440 | tf_op jit(solution)/shard_map/ppermute | solution.py:346
  118.6 4.1 %collective-permute-start.22 = (bf16[2,512,512]{2,1,0:T(8,128)(2,1)S(1)}, bf16[2,512,512]{2,1,0:T(8,128)(2,1)S(1)}, u32[]{:S(2)}, u32[]{:S(2)}) collective-permute-start(bf16[2,512,512]{2,1,0:T(8,128)(2,1)S(1)} %whiten.6.refs_8_), channel_id=1, source_target_pairs={{0,1},{1,0},{2,3},{3,2},{4,5},{5,4},{6,7},{7,6},{8,9},{9,8},{10,11... | collective-permute-start | bytes 3145736 | tf_op jit(solution)/shard_map/ppermute | solution.py:419
  118.9 14.8 %collective-permute-start.23 = (bf16[2,512,512]{2,1,0:T(8,128)(2,1)S(1)}, bf16[2,512,512]{2,1,0:T(8,128)(2,1)S(1)}, u32[]{:S(2)}, u32[]{:S(2)}) collective-permute-start(bf16[2,512,512]{2,1,0:T(8,128)(2,1)S(1)} %add_blocks.3.refs_8_), channel_id=1, source_target_pairs={{0,2},{1,5},{2,0},{3,7},{4,6},{5,1},{6,4},{7,3},{8,10},{9,13},{10,... | collective-permute-start | bytes 3145736 | tf_op jit(solution)/shard_map/ppermute | solution.py:423
  133.9 9.2 %collective-permute-start.24 = (bf16[1,512,512]{2,1,0:T(8,128)(2,1)S(1)}, bf16[1,512,512]{2,1,0:T(8,128)(2,1)S(1)}, u32[]{:S(2)}, u32[]{:S(2)}) collective-permute-start(bf16[1,512,512]{2,1,0:T(8,128)(2,1)S(1)} %get-tuple-element.19), channel_id=1, source_target_pairs={{0,4},{1,3},{2,6},{3,1},{4,0},{5,7},{6,2},{7,5},{8,12},{9,11},{10,... | collective-permute-start | bytes 1572872 | tf_op jit(solution)/shard_map/ppermute | solution.py:428
  (3 other events, 4.1 us)

commit v5 on v4

--- a/solution.py
+++ b/solution.py
@@ -173,7 +173,8 @@
     )
 
 
-def load_kernel(factor_ref, after_ref, held_ref, sem):
+def load_kernel(factor_ref, *refs):
+    held_ref, sem = refs[-2:]
     parts = sem.shape[0]
     block = factor_ref.shape[0] // parts
     copies = []
@@ -190,8 +191,8 @@
         load_kernel,
         "load_factor",
         pltpu.VMEM(factor.shape, factor.dtype),
-        [HBM, ANY],
-        (in_hbm(factor), after),
+        [HBM] + [ANY] * len(after),
+        (in_hbm(factor), *after),
         bytes_accessed=factor.size * 2,
         scratch=[pltpu.SemaphoreType.DMA((8,))],
     )
@@ -326,7 +327,7 @@
         if d == self.last:
             key = (d % 2, c + d)
             return [self.sent[key], self.recv[key]]
-        return [self.recv[d % 2, c + self.n - 2 - d]]
+        return [self.recv[d % 2, c + self.n - 1 - d]]
 
     def exchange(self, parity, period, after=()):
         options = {}
@@ -334,8 +335,8 @@
             if d % 2 == parity:
                 if self.has(period - d):
                     options[d] = self.inner(d, period - d)
-            elif d > 0 and self.has(period - (self.n - 1 - d)):
-                options[d] = self.whole(d, period - (self.n - 1 - d))
+            elif d > 0 and self.has(period - (self.n - d)):
+                options[d] = self.whole(d, period - (self.n - d))
         if not options:
             return None
         value = sum_at("exchanged", self.depth, options, after)
@@ -395,21 +396,21 @@
         line = SampleSum(n_sample, depth)
         totals = []
         value = None
-        for t in range(count + n_sample - 2):
+        for t in range(count + n_sample - 1):
             if t < count:
                 after = [value] if t > 0 else []
+                after += [line.recv[1, t - 2]] if (1, t - 2) in line.recv else []
                 line.pieces.append(moments_part(t * TILE, x, z, scale, signs, weight, after))
             after = totals[-1:] + line.pieces[-1:]
             if t == count:
-                held_factor = load_factor(factor, value)
+                held_factor = load_factor(factor, [value, line.recv[1, t - 2]])
                 after.append(held_factor)
-            for parity in (0, 1) if t < count else (1, 0):
+            for parity in (1, 0):
                 sent = line.exchange(parity, t, after)
-                value = value if sent is None else sent
-                if t >= count:
-                    after = [value]
-            if t >= n_sample - 1:
-                totals.append(line.total(t - (n_sample - 1)))
+                if sent is not None:
+                    value, after = sent, [sent]
+            if t >= n_sample:
+                totals.append(line.total(t - n_sample))
         totals.append(line.total(count - 1))
 
         middle = len(kept_order) // 2

time: 157 us -> 148 us (0.943)
  starting transfers between devices: 54.6 us -> 39.5 us
  waiting for transfers between devices: 32.8 us -> 38.3 us
    ppermute x18 -> x19, starting transfers between devices: 45.2 us -> 29.9 us  [exchange(): self.recv[parity, period] = lax.ppermute(value, 'sample', pairs)]
    ppermute x18 -> x19, waiting for transfers between devices: 14 us -> 19.7 us  [exchange(): self.recv[parity, period] = lax.ppermute(value, 'sample', pairs)]
    pallas_call x46 -> x47, Pallas kernels: 54.5 us -> 54.1 us  [call(): pl.pallas_call(kernel, out_shape=out_shape, in_specs=in_specs, out_specs=...]
  transfers between devices with their start and end apart: 25 -> 26, of which waited for: 8 -> 14; matrix products, arithmetic and copies ran while one was open for 0% -> 0% of each run, Pallas kernels for 28% -> 29%
where the time goes in v5:
time: 148 us
  Pallas kernels  54.1 us (37%)
  starting transfers between devices  39.5 us (27%)
  waiting for transfers between devices  38.3 us (26%)
  blocking collectives  12.6 us (9%)
    pallas_call x47, Pallas kernels, call(): pl.pallas_call(kernel, out_shape=out_shape, in_specs=in_specs, out_specs=...  54.1 us
    ppermute x19, starting transfers between devices, exchange(): self.recv[parity, period] = lax.ppermute(value, 'sample', pairs)  29.9 us
    ppermute x19, waiting for transfers between devices, exchange(): self.recv[parity, period] = lax.ppermute(value, 'sample', pairs)  19.7 us
    all_to_all x1, blocking collectives, local(): share = lax.all_to_all(share, ('sample', 'landmark'), 0, 0, tiled=True)  12.6 us
    ppermute x1, waiting for transfers between devices, local(): recv = lax.ppermute(sums[0], 'landmark', pairs_of(1))  10.7 us
    ppermute x1, waiting for transfers between devices, local(): recv = lax.ppermute(sent, 'landmark', pairs_of(t))  7.6 us
    ppermute x3, starting transfers between devices, local(): pairs.append(lax.ppermute(own_pair, 'sample', to))  6.11 us
  transfers between devices with their start and end apart: 26, of which 14 were waited for; matrix products, arithmetic and copies ran while one was open for 0% of the time, Pallas kernels for 29%

profile of v5, /device:TPU:0, one launch (start us, length us, event | category | flops | bytes accessed | tf_op | source)
XLA Modules:
  0.0 147.6 jit_solution(12795805579420061922)
XLA Ops:
  2.7 5.1 %collective-permute-start.2 = (f32[8,128]{1,0:T(8,128)S(1)}, f32[8,128]{1,0:T(8,128)S(1)}, u32[]{:S(2)}, u32[]{:S(2)}) collective-permute-start(f32[8,128]{1,0:T(8,128)S(1)} %own_counts.1.refs_0_), channel_id=1, source_target_pairs={{0,24},{8,0},{16,8},{24,16},{1,25},{9,1},{17,9},{25,17},{2,26},{10... | collective-permute-start | bytes 12296 | tf_op jit(solution)/shard_map/ppermute | solution.py:392
  8.8 9.6 %prepare_rows.1 = (bf16[1024,4096]{1,0:T(8,128)(2,1)S(1)}, bf16[2048,4096]{1,0:T(8,128)(2,1)S(1)}, f32[1024,1]{1,0:T(8,128)S(1)}, bf16[512,1024]{1,0:T(8,128)(2,...) custom-call(s32[1]{0:T(128)} %bitcast.2.here_ref, s32[4]{0:T(128)S(1)} %copy-done.1, bf16[1024,4096]{1,0:T(8,128)(2,1)} %x_ref.1, ...), custom_call_target="tpu_custom_call" | custom-call | flops 12582912 | bytes 27262976 | tf_op jit(solution)/shard_map/prepare_rows/pallas_call | solution.py:27
  18.5 3.1 %moments.8.refs_0_.refs_1_ = bf16[512,256]{1,0:T(8,128)(2,1)S(1)} custom-call(bf16[1024,4096]{1,0:T(8,128)(2,1)S(1)} %get-tuple-element.12.x_ref, bf16[2048,4096]{1,0:T(8,128)(2,1)S(1)} %get-tuple-element.13.z_ref, f32[1024,1]{1,0:T(8,128)S(1)} %get-tuple-element.14.scale_ref, bf16[512,1024]{1,0:T(8,128)(2,1)S(1)} %get-tuple-element.15.signs_ref, ...), custom_call_target="tpu_custom_call" | custom-call | flops 2415919104 | bytes 2097152 | tf_op jit(solution)/shard_map/moments/pallas_call | solution.py:27
  21.6 2.5 %collective-permute-start.3 = (bf16[512,256]{1,0:T(8,128)(2,1)S(1)}, bf16[512,256]{1,0:T(8,128)(2,1)S(1)}, u32[]{:S(2)}, u32[]{:S(2)}) collective-permute-start(bf16[512,256]{1,0:T(8,128)(2,1)S(1)} %exchanged.19.rest_0_), channel_id=1, source_target_pairs={{0,8},{8,0},{16,24},{24,16},{1,9},{9,1},{17,25},{25,17},{2,10},{10... | collective-permute-start | bytes 786440 | tf_op jit(solution)/shard_map/ppermute | solution.py:347
  24.2 3.2 %moments.9.refs_2_.refs_0_ = bf16[512,256]{1,0:T(8,128)(2,1)S(1)} custom-call(bf16[1024,4096]{1,0:T(8,128)(2,1)S(1)} %get-tuple-element.12.x_ref, bf16[2048,4096]{1,0:T(8,128)(2,1)S(1)} %get-tuple-element.13.z_ref, f32[1024,1]{1,0:T(8,128)S(1)} %get-tuple-element.14.scale_ref, bf16[512,1024]{1,0:T(8,128)(2,1)S(1)} %get-tuple-element.15.signs_ref, ...), custom_call_target="tpu_custom_call" | custom-call | flops 2415919104 | bytes 2097152 | tf_op jit(solution)/shard_map/moments/pallas_call | solution.py:27
  32.2 3.1 %moments.10.refs_2_.refs_0_ = bf16[512,256]{1,0:T(8,128)(2,1)S(1)} custom-call(bf16[1024,4096]{1,0:T(8,128)(2,1)S(1)} %get-tuple-element.12.x_ref, bf16[2048,4096]{1,0:T(8,128)(2,1)S(1)} %get-tuple-element.13.z_ref, f32[1024,1]{1,0:T(8,128)S(1)} %get-tuple-element.14.scale_ref, bf16[512,1024]{1,0:T(8,128)(2,1)S(1)} %get-tuple-element.15.signs_ref, ...), custom_call_target="tpu_custom_call" | custom-call | flops 2415919104 | bytes 2097152 | tf_op jit(solution)/shard_map/moments/pallas_call | solution.py:27
  39.2 3.2 %moments.11.refs_2_.refs_0_ = bf16[512,256]{1,0:T(8,128)(2,1)S(1)} custom-call(bf16[1024,4096]{1,0:T(8,128)(2,1)S(1)} %get-tuple-element.12.x_ref, bf16[2048,4096]{1,0:T(8,128)(2,1)S(1)} %get-tuple-element.13.z_ref, f32[1024,1]{1,0:T(8,128)S(1)} %get-tuple-element.14.scale_ref, bf16[512,1024]{1,0:T(8,128)(2,1)S(1)} %get-tuple-element.15.signs_ref, ...), custom_call_target="tpu_custom_call" | custom-call | flops 2415919104 | bytes 2097152 | tf_op jit(solution)/shard_map/moments/pallas_call | solution.py:27
  46.2 3.2 %moments.12.refs_2_.refs_0_ = bf16[512,256]{1,0:T(8,128)(2,1)S(1)} custom-call(bf16[1024,4096]{1,0:T(8,128)(2,1)S(1)} %get-tuple-element.12.x_ref, bf16[2048,4096]{1,0:T(8,128)(2,1)S(1)} %get-tuple-element.13.z_ref, f32[1024,1]{1,0:T(8,128)S(1)} %get-tuple-element.14.scale_ref, bf16[512,1024]{1,0:T(8,128)(2,1)S(1)} %get-tuple-element.15.signs_ref, ...), custom_call_target="tpu_custom_call" | custom-call | flops 2415919104 | bytes 2097152 | tf_op jit(solution)/shard_map/moments/pallas_call | solution.py:27
  49.9 2.4 %collective-permute-start.10 = (bf16[512,256]{1,0:T(8,128)(2,1)S(1)}, bf16[512,256]{1,0:T(8,128)(2,1)S(1)}, u32[]{:S(2)}, u32[]{:S(2)}) collective-permute-start(bf16[512,256]{1,0:T(8,128)(2,1)S(1)} %exchanged.27.rest_0_), channel_id=1, source_target_pairs={{0,8},{8,0},{16,24},{24,16},{1,9},{9,1},{17,25},{25,17},{2,10},{10... | collective-permute-start | bytes 786440 | tf_op jit(solution)/shard_map/ppermute | solution.py:347
  53.0 3.2 %moments.13.refs_3_.refs_0_ = bf16[512,256]{1,0:T(8,128)(2,1)S(1)} custom-call(bf16[1024,4096]{1,0:T(8,128)(2,1)S(1)} %get-tuple-element.12.x_ref, bf16[2048,4096]{1,0:T(8,128)(2,1)S(1)} %get-tuple-element.13.z_ref, f32[1024,1]{1,0:T(8,128)S(1)} %get-tuple-element.14.scale_ref, bf16[512,1024]{1,0:T(8,128)(2,1)S(1)} %get-tuple-element.15.signs_ref, ...), custom_call_target="tpu_custom_call" | custom-call | flops 2415919104 | bytes 2097152 | tf_op jit(solution)/shard_map/moments/pallas_call | solution.py:27
  57.9 2.4 %collective-permute-start.12 = (bf16[512,256]{1,0:T(8,128)(2,1)S(1)}, bf16[512,256]{1,0:T(8,128)(2,1)S(1)}, u32[]{:S(2)}, u32[]{:S(2)}) collective-permute-start(bf16[512,256]{1,0:T(8,128)(2,1)S(1)} %exchanged.29.rest_0_), channel_id=1, source_target_pairs={{0,8},{8,0},{16,24},{24,16},{1,9},{9,1},{17,25},{25,17},{2,10},{10... | collective-permute-start | bytes 786440 | tf_op jit(solution)/shard_map/ppermute | solution.py:347
  61.1 3.2 %moments.14.refs_3_.refs_0_ = bf16[512,256]{1,0:T(8,128)(2,1)S(1)} custom-call(bf16[1024,4096]{1,0:T(8,128)(2,1)S(1)} %get-tuple-element.12.x_ref, bf16[2048,4096]{1,0:T(8,128)(2,1)S(1)} %get-tuple-element.13.z_ref, f32[1024,1]{1,0:T(8,128)S(1)} %get-tuple-element.14.scale_ref, bf16[512,1024]{1,0:T(8,128)(2,1)S(1)} %get-tuple-element.15.signs_ref, ...), custom_call_target="tpu_custom_call" | custom-call | flops 2415919104 | bytes 2097152 | tf_op jit(solution)/shard_map/moments/pallas_call | solution.py:27
  64.3 2.5 %collective-permute-done.12.refs_1_.refs_0_ = bf16[512,256]{1,0:T(8,128)(2,1)S(1)} collective-permute-done((bf16[512,256]{1,0:T(8,128)(2,1)S(1)}, bf16[512,256]{1,0:T(8,128)(2,1)S(1)}, u32[]{:S(2)}, u32[]{:S(2)}) %collective-permute-start.12) | collective-permute-done | bytes 262176 | tf_op jit(solution)/shard_map/ppermute | solution.py:347
  66.9 2.5 %collective-permute-start.14 = (bf16[512,256]{1,0:T(8,128)(2,1)S(1)}, bf16[512,256]{1,0:T(8,128)(2,1)S(1)}, u32[]{:S(2)}, u32[]{:S(2)}) collective-permute-start(bf16[512,256]{1,0:T(8,128)(2,1)S(1)} %exchanged.31.rest_0_), channel_id=1, source_target_pairs={{0,8},{8,0},{16,24},{24,16},{1,9},{9,1},{17,25},{25,17},{2,10},{10... | collective-permute-start | bytes 786440 | tf_op jit(solution)/shard_map/ppermute | solution.py:347
  70.1 3.2 %moments.15.refs_3_.refs_0_ = bf16[512,256]{1,0:T(8,128)(2,1)S(1)} custom-call(bf16[1024,4096]{1,0:T(8,128)(2,1)S(1)} %get-tuple-element.12.x_ref, bf16[2048,4096]{1,0:T(8,128)(2,1)S(1)} %get-tuple-element.13.z_ref, f32[1024,1]{1,0:T(8,128)S(1)} %get-tuple-element.14.scale_ref, bf16[512,1024]{1,0:T(8,128)(2,1)S(1)} %get-tuple-element.15.signs_ref, ...), custom_call_target="tpu_custom_call" | custom-call | flops 2415919104 | bytes 2097152 | tf_op jit(solution)/shard_map/moments/pallas_call | solution.py:27
  73.2 3.1 %collective-permute-done.14.refs_1_.refs_0_ = bf16[512,256]{1,0:T(8,128)(2,1)S(1)} collective-permute-done((bf16[512,256]{1,0:T(8,128)(2,1)S(1)}, bf16[512,256]{1,0:T(8,128)(2,1)S(1)}, u32[]{:S(2)}, u32[]{:S(2)}) %collective-permute-start.14) | collective-permute-done | bytes 262176 | tf_op jit(solution)/shard_map/ppermute | solution.py:347
  79.0 5.9 %load_factor.1.refs_4_.factor_ref = bf16[2048,4096]{1,0:T(8,128)(2,1)S(1)} custom-call(bf16[2048,4096]{1,0:T(8,128)(2,1)} %factor_ref.1, bf16[512,256]{1,0:T(8,128)(2,1)S(1)} %exchanged.33.refs_0_, bf16[512,256]{1,0:T(8,128)(2,1)S(1)} %collective-permute-done.15.refs_1_.refs_2_), custom_call_target="tpu_custom_call" | custom-call | bytes 16777216 | tf_op jit(solution)/shard_map/load_factor/pallas_call | solution.py:27
  88.5 2.4 %collective-permute-start.19 = (bf16[512,256]{1,0:T(8,128)(2,1)S(1)}, bf16[512,256]{1,0:T(8,128)(2,1)S(1)}, u32[]{:S(2)}, u32[]{:S(2)}) collective-permute-start(bf16[512,256]{1,0:T(8,128)(2,1)S(1)} %exchanged.36), channel_id=1, source_target_pairs={{0,8},{8,0},{16,24},{24,16},{1,9},{9,1},{17,25},{25,17},{2,10},{10... | collective-permute-start | bytes 786440 | tf_op jit(solution)/shard_map/ppermute | solution.py:347
  90.9 3.1 %collective-permute-done.17.refs_0_ = bf16[512,256]{1,0:T(8,128)(2,1)S(1)} collective-permute-done((bf16[512,256]{1,0:T(8,128)(2,1)S(1)}, bf16[512,256]{1,0:T(8,128)(2,1)S(1)}, u32[]{:S(2)}, u32[]{:S(2)}) %collective-permute-start.17) | collective-permute-done | bytes 262176 | tf_op jit(solution)/shard_map/ppermute | solution.py:347
  96.8 3.9 %collective-permute-done.21.refs_0_ = bf16[512,256]{1,0:T(8,128)(2,1)S(1)} collective-permute-done((bf16[512,256]{1,0:T(8,128)(2,1)S(1)}, bf16[512,256]{1,0:T(8,128)(2,1)S(1)}, u32[]{:S(2)}, u32[]{:S(2)}) %collective-permute-start.21) | collective-permute-done | bytes 262176 | tf_op jit(solution)/shard_map/ppermute | solution.py:347
  106.3 2.4 %whiten.6.refs_8_ = bf16[2,512,512]{2,1,0:T(8,128)(2,1)S(1)} custom-call(s32[1]{0:T(128)} %bitcast.refs_1_.spot_ref, bf16[2048,4096]{1,0:T(8,128)(2,1)S(1)} %load_factor.1.refs_4_.factor_ref, bf16[512,256]{1,0:T(8,128)(2,1)S(1)} %total.8.refs_2_.refs_0_, bf16[512,256]{1,0:T(8,128)(2,1)S(1)} %total.9.refs_2_.refs_1_, bf16[512,256]{1,0:T(8,128)(2,1)S(1)} %total.10.refs_2_, ...), custom_call_target="tpu_custom_call" | custom-call | flops 2147483648 | bytes 4194304 | tf_op jit(solution)/shard_map/whiten/pallas_call | solution.py:27
  113.0 10.7 %collective-permute-done.24.b_ref = bf16[2,512,512]{2,1,0:T(8,128)(2,1)S(1)} collective-permute-done((bf16[2,512,512]{2,1,0:T(8,128)(2,1)S(1)}, bf16[2,512,512]{2,1,0:T(8,128)(2,1)S(1)}, u32[]{:S(2)}, u32[]{:S(2)}) %collective-permute-start.24) | collective-permute-done | bytes 1048608 | tf_op jit(solution)/shard_map/ppermute | solution.py:424
  125.6 7.6 %collective-permute-done.25 = bf16[1,512,512]{2,1,0:T(8,128)(2,1)S(1)} collective-permute-done((bf16[1,512,512]{2,1,0:T(8,128)(2,1)S(1)}, bf16[1,512,512]{2,1,0:T(8,128)(2,1)S(1)}, u32[]{:S(2)}, u32[]{:S(2)}) %collective-permute-start.25) | collective-permute-done | bytes 524320 | tf_op jit(solution)/shard_map/ppermute | solution.py:429
  134.4 12.6 %all_to_all.5 = f32[32,4,128]{2,1,0:T(4,128)S(1)} all-to-all(f32[32,4,128]{2,1,0:T(4,128)S(1)} %get-tuple-element.21), channel_id=1, replica_groups=mesh['sample'=4,'landmark'=8] {'sample','landmark'}, dimensions={0} | all-to-all | bytes 131072 | tf_op jit(solution)/shard_map/all_to_all | solution.py:431
  (82 shorter events, 42.5 us)
Async XLA Ops:
  2.7 15.7 %collective-permute-start.2 = (f32[8,128]{1,0:T(8,128)S(1)}, f32[8,128]{1,0:T(8,128)S(1)}, u32[]{:S(2)}, u32[]{:S(2)}) collective-permute-start(f32[8,128]{1,0:T(8,128)S(1)} %own_counts.1.refs_0_), channel_id=1, source_target_pairs={{0,24},{8,0},{16,8},{24,16},{1,25},{9,1},{17,9},{25,17},{2,26},{10... | collective-permute-start | bytes 12296 | tf_op jit(solution)/shard_map/ppermute | solution.py:392
  7.8 10.6 %collective-permute-start.1 = (f32[8,128]{1,0:T(8,128)S(1)}, f32[8,128]{1,0:T(8,128)S(1)}, u32[]{:S(2)}, u32[]{:S(2)}) collective-permute-start(f32[8,128]{1,0:T(8,128)S(1)} %own_counts.1.refs_0_), channel_id=1, source_target_pairs={{0,16},{8,24},{16,0},{24,8},{1,17},{9,25},{17,1},{25,9},{2,18},{10... | collective-permute-start | bytes 12296 | tf_op jit(solution)/shard_map/ppermute | solution.py:392
  7.8 10.6 %collective-permute-start = (f32[8,128]{1,0:T(8,128)S(1)}, f32[8,128]{1,0:T(8,128)S(1)}, u32[]{:S(2)}, u32[]{:S(2)}) collective-permute-start(f32[8,128]{1,0:T(8,128)S(1)} %own_counts.1.refs_0_), channel_id=1, source_target_pairs={{0,8},{8,16},{16,24},{24,0},{1,9},{9,17},{17,25},{25,1},{2,10},{10... | collective-permute-start | bytes 12296 | tf_op jit(solution)/shard_map/ppermute | solution.py:392
  21.6 8.0 %collective-permute-start.3 = (bf16[512,256]{1,0:T(8,128)(2,1)S(1)}, bf16[512,256]{1,0:T(8,128)(2,1)S(1)}, u32[]{:S(2)}, u32[]{:S(2)}) collective-permute-start(bf16[512,256]{1,0:T(8,128)(2,1)S(1)} %exchanged.19.rest_0_), channel_id=1, source_target_pairs={{0,8},{8,0},{16,24},{24,16},{1,9},{9,1},{17,25},{25,17},{2,10},{10... | collective-permute-start | bytes 786440 | tf_op jit(solution)/shard_map/ppermute | solution.py:347
  29.8 6.6 %collective-permute-start.4 = (bf16[512,256]{1,0:T(8,128)(2,1)S(1)}, bf16[512,256]{1,0:T(8,128)(2,1)S(1)}, u32[]{:S(2)}, u32[]{:S(2)}) collective-permute-start(bf16[512,256]{1,0:T(8,128)(2,1)S(1)} %exchanged.21.rest_0_), channel_id=1, source_target_pairs={{0,8},{8,0},{16,24},{24,16},{1,9},{9,1},{17,25},{25,17},{2,10},{10... | collective-permute-start | bytes 786440 | tf_op jit(solution)/shard_map/ppermute | solution.py:347
  31.6 7.7 %collective-permute-start.5 = (bf16[512,256]{1,0:T(8,128)(2,1)S(1)}, bf16[512,256]{1,0:T(8,128)(2,1)S(1)}, u32[]{:S(2)}, u32[]{:S(2)}) collective-permute-start(bf16[512,256]{1,0:T(8,128)(2,1)S(1)} %exchanged.20.refs_1_), channel_id=1, source_target_pairs={{8,16},{16,8},{9,17},{17,9},{10,18},{18,10},{11,19},{19,11},{12,20... | collective-permute-start | bytes 786440 | tf_op jit(solution)/shard_map/ppermute | solution.py:347
  36.5 6.4 %collective-permute-start.6 = (bf16[512,256]{1,0:T(8,128)(2,1)S(1)}, bf16[512,256]{1,0:T(8,128)(2,1)S(1)}, u32[]{:S(2)}, u32[]{:S(2)}) collective-permute-start(bf16[512,256]{1,0:T(8,128)(2,1)S(1)} %exchanged.23.rest_0_), channel_id=1, source_target_pairs={{0,8},{8,0},{16,24},{24,16},{1,9},{9,1},{17,25},{25,17},{2,10},{10... | collective-permute-start | bytes 786440 | tf_op jit(solution)/shard_map/ppermute | solution.py:347
  38.5 7.7 %collective-permute-start.7 = (bf16[512,256]{1,0:T(8,128)(2,1)S(1)}, bf16[512,256]{1,0:T(8,128)(2,1)S(1)}, u32[]{:S(2)}, u32[]{:S(2)}) collective-permute-start(bf16[512,256]{1,0:T(8,128)(2,1)S(1)} %exchanged.22.refs_1_), channel_id=1, source_target_pairs={{8,16},{16,8},{9,17},{17,9},{10,18},{18,10},{11,19},{19,11},{12,20... | collective-permute-start | bytes 786440 | tf_op jit(solution)/shard_map/ppermute | solution.py:347
  43.0 6.8 %collective-permute-start.8 = (bf16[512,256]{1,0:T(8,128)(2,1)S(1)}, bf16[512,256]{1,0:T(8,128)(2,1)S(1)}, u32[]{:S(2)}, u32[]{:S(2)}) collective-permute-start(bf16[512,256]{1,0:T(8,128)(2,1)S(1)} %exchanged.25.rest_0_), channel_id=1, source_target_pairs={{0,8},{8,0},{16,24},{24,16},{1,9},{9,1},{17,25},{25,17},{2,10},{10... | collective-permute-start | bytes 786440 | tf_op jit(solution)/shard_map/ppermute | solution.py:347
  45.3 7.7 %collective-permute-start.9 = (bf16[512,256]{1,0:T(8,128)(2,1)S(1)}, bf16[512,256]{1,0:T(8,128)(2,1)S(1)}, u32[]{:S(2)}, u32[]{:S(2)}) collective-permute-start(bf16[512,256]{1,0:T(8,128)(2,1)S(1)} %exchanged.24.refs_3_.refs_1_), channel_id=1, source_target_pairs={{8,16},{16,8},{9,17},{17,9},{10,18},{18,10},{11,19},{19,11},{12,20... | collective-permute-start | bytes 786440 | tf_op jit(solution)/shard_map/ppermute | solution.py:347
  49.9 7.9 %collective-permute-start.10 = (bf16[512,256]{1,0:T(8,128)(2,1)S(1)}, bf16[512,256]{1,0:T(8,128)(2,1)S(1)}, u32[]{:S(2)}, u32[]{:S(2)}) collective-permute-start(bf16[512,256]{1,0:T(8,128)(2,1)S(1)} %exchanged.27.rest_0_), channel_id=1, source_target_pairs={{0,8},{8,0},{16,24},{24,16},{1,9},{9,1},{17,25},{25,17},{2,10},{10... | collective-permute-start | bytes 786440 | tf_op jit(solution)/shard_map/ppermute | solution.py:347
  52.3 8.8 %collective-permute-start.11 = (bf16[512,256]{1,0:T(8,128)(2,1)S(1)}, bf16[512,256]{1,0:T(8,128)(2,1)S(1)}, u32[]{:S(2)}, u32[]{:S(2)}) collective-permute-start(bf16[512,256]{1,0:T(8,128)(2,1)S(1)} %exchanged.26.refs_3_.refs_1_), channel_id=1, source_target_pairs={{8,16},{16,8},{9,17},{17,9},{10,18},{18,10},{11,19},{19,11},{12,20... | collective-permute-start | bytes 786440 | tf_op jit(solution)/shard_map/ppermute | solution.py:347
  57.9 8.9 %collective-permute-start.12 = (bf16[512,256]{1,0:T(8,128)(2,1)S(1)}, bf16[512,256]{1,0:T(8,128)(2,1)S(1)}, u32[]{:S(2)}, u32[]{:S(2)}) collective-permute-start(bf16[512,256]{1,0:T(8,128)(2,1)S(1)} %exchanged.29.rest_0_), channel_id=1, source_target_pairs={{0,8},{8,0},{16,24},{24,16},{1,9},{9,1},{17,25},{25,17},{2,10},{10... | collective-permute-start | bytes 786440 | tf_op jit(solution)/shard_map/ppermute | solution.py:347
  60.4 9.7 %collective-permute-start.13 = (bf16[512,256]{1,0:T(8,128)(2,1)S(1)}, bf16[512,256]{1,0:T(8,128)(2,1)S(1)}, u32[]{:S(2)}, u32[]{:S(2)}) collective-permute-start(bf16[512,256]{1,0:T(8,128)(2,1)S(1)} %exchanged.28.refs_3_.refs_1_), channel_id=1, source_target_pairs={{8,16},{16,8},{9,17},{17,9},{10,18},{18,10},{11,19},{19,11},{12,20... | collective-permute-start | bytes 786440 | tf_op jit(solution)/shard_map/ppermute | solution.py:347
  66.9 9.5 %collective-permute-start.14 = (bf16[512,256]{1,0:T(8,128)(2,1)S(1)}, bf16[512,256]{1,0:T(8,128)(2,1)S(1)}, u32[]{:S(2)}, u32[]{:S(2)}) collective-permute-start(bf16[512,256]{1,0:T(8,128)(2,1)S(1)} %exchanged.31.rest_0_), channel_id=1, source_target_pairs={{0,8},{8,0},{16,24},{24,16},{1,9},{9,1},{17,25},{25,17},{2,10},{10... | collective-permute-start | bytes 786440 | tf_op jit(solution)/shard_map/ppermute | solution.py:347
  69.4 9.7 %collective-permute-start.15 = (bf16[512,256]{1,0:T(8,128)(2,1)S(1)}, bf16[512,256]{1,0:T(8,128)(2,1)S(1)}, u32[]{:S(2)}, u32[]{:S(2)}) collective-permute-start(bf16[512,256]{1,0:T(8,128)(2,1)S(1)} %exchanged.30.refs_3_.refs_0_.refs_1_), channel_id=1, source_target_pairs={{8,16},{16,8},{9,17},{17,9},{10,18},{18,10},{11,19},{19,11},{12,20... | collective-permute-start | bytes 786440 | tf_op jit(solution)/shard_map/ppermute | solution.py:347
  76.5 9.2 %collective-permute-start.16 = (bf16[512,256]{1,0:T(8,128)(2,1)S(1)}, bf16[512,256]{1,0:T(8,128)(2,1)S(1)}, u32[]{:S(2)}, u32[]{:S(2)}) collective-permute-start(bf16[512,256]{1,0:T(8,128)(2,1)S(1)} %exchanged.33.refs_0_), channel_id=1, source_target_pairs={{0,8},{8,0},{16,24},{24,16},{1,9},{9,1},{17,25},{25,17},{2,10},{10... | collective-permute-start | bytes 786440 | tf_op jit(solution)/shard_map/ppermute | solution.py:347
  78.3 10.1 %collective-permute-start.18 = (bf16[512,256]{1,0:T(8,128)(2,1)S(1)}, bf16[512,256]{1,0:T(8,128)(2,1)S(1)}, u32[]{:S(2)}, u32[]{:S(2)}) collective-permute-start(bf16[512,256]{1,0:T(8,128)(2,1)S(1)} %exchanged.32.refs_3_.refs_0_.refs_1_), channel_id=1, source_target_pairs={{8,16},{16,8},{9,17},{17,9},{10,18},{18,10},{11,19},{19,11},{12,20... | collective-permute-start | bytes 786440 | tf_op jit(solution)/shard_map/ppermute | solution.py:347
  85.8 8.1 %collective-permute-start.17 = (bf16[512,256]{1,0:T(8,128)(2,1)S(1)}, bf16[512,256]{1,0:T(8,128)(2,1)S(1)}, u32[]{:S(2)}, u32[]{:S(2)}) collective-permute-start(bf16[512,256]{1,0:T(8,128)(2,1)S(1)} %exchanged.35), channel_id=1, source_target_pairs={{0,8},{8,0},{16,24},{24,16},{1,9},{9,1},{17,25},{25,17},{2,10},{10... | collective-permute-start | bytes 786440 | tf_op jit(solution)/shard_map/ppermute | solution.py:347
  87.7 6.3 %collective-permute-start.20 = (bf16[512,256]{1,0:T(8,128)(2,1)S(1)}, bf16[512,256]{1,0:T(8,128)(2,1)S(1)}, u32[]{:S(2)}, u32[]{:S(2)}) collective-permute-start(bf16[512,256]{1,0:T(8,128)(2,1)S(1)} %exchanged.34.refs_2_.refs_0_.refs_1_), channel_id=1, source_target_pairs={{8,16},{16,8},{9,17},{17,9},{10,18},{18,10},{11,19},{19,11},{12,20... | collective-permute-start | bytes 786440 | tf_op jit(solution)/shard_map/ppermute | solution.py:347
  88.5 8.3 %collective-permute-start.19 = (bf16[512,256]{1,0:T(8,128)(2,1)S(1)}, bf16[512,256]{1,0:T(8,128)(2,1)S(1)}, u32[]{:S(2)}, u32[]{:S(2)}) collective-permute-start(bf16[512,256]{1,0:T(8,128)(2,1)S(1)} %exchanged.36), channel_id=1, source_target_pairs={{0,8},{8,0},{16,24},{24,16},{1,9},{9,1},{17,25},{25,17},{2,10},{10... | collective-permute-start | bytes 786440 | tf_op jit(solution)/shard_map/ppermute | solution.py:347
  94.1 6.6 %collective-permute-start.21 = (bf16[512,256]{1,0:T(8,128)(2,1)S(1)}, bf16[512,256]{1,0:T(8,128)(2,1)S(1)}, u32[]{:S(2)}, u32[]{:S(2)}) collective-permute-start(bf16[512,256]{1,0:T(8,128)(2,1)S(1)} %exchanged.37), channel_id=1, source_target_pairs={{0,8},{8,0},{16,24},{24,16},{1,9},{9,1},{17,25},{25,17},{2,10},{10... | collective-permute-start | bytes 786440 | tf_op jit(solution)/shard_map/ppermute | solution.py:347
  108.9 14.8 %collective-permute-start.24 = (bf16[2,512,512]{2,1,0:T(8,128)(2,1)S(1)}, bf16[2,512,512]{2,1,0:T(8,128)(2,1)S(1)}, u32[]{:S(2)}, u32[]{:S(2)}) collective-permute-start(bf16[2,512,512]{2,1,0:T(8,128)(2,1)S(1)} %add_blocks.3.refs_8_), channel_id=1, source_target_pairs={{0,2},{1,5},{2,0},{3,7},{4,6},{5,1},{6,4},{7,3},{8,10},{9,13},{10,... | collective-permute-start | bytes 3145736 | tf_op jit(solution)/shard_map/ppermute | solution.py:424
  124.0 9.2 %collective-permute-start.25 = (bf16[1,512,512]{2,1,0:T(8,128)(2,1)S(1)}, bf16[1,512,512]{2,1,0:T(8,128)(2,1)S(1)}, u32[]{:S(2)}, u32[]{:S(2)}) collective-permute-start(bf16[1,512,512]{2,1,0:T(8,128)(2,1)S(1)} %get-tuple-element.19), channel_id=1, source_target_pairs={{0,4},{1,3},{2,6},{3,1},{4,0},{5,7},{6,2},{7,5},{8,12},{9,11},{10,... | collective-permute-start | bytes 1572872 | tf_op jit(solution)/shard_map/ppermute | solution.py:429
  (4 other events, 8.2 us)

commit v6 on v5

--- a/solution.py
+++ b/solution.py
@@ -82,22 +82,17 @@
                 held_x_ref, held_z_ref, scale_ref, signs_ref, mask_a_ref, mask_b_ref, flips_buf, x_sem, z_sem, f_sem):
     rows, width = x_ref.shape
     block = rows // parts
-    tile = z_ref.shape[0] // parts
 
     def x_copy(i):
         here = pl.ds(i * block, block)
         return pltpu.make_async_copy(x_ref.at[here, :], held_x_ref.at[here, :], x_sem.at[i])
 
-    def z_copy(i):
-        here = pl.ds(i * tile, tile)
-        return pltpu.make_async_copy(z_ref.at[here, :], held_z_ref.at[here, :], z_sem.at[i])
-
+    z_copy = pltpu.make_async_copy(z_ref.at[pl.ds(0, TILE), :], held_z_ref, z_sem)
     flips_copy = pltpu.make_async_copy(flips_ref, flips_buf, f_sem)
     for i in range(parts):
         x_copy(i).start()
     flips_copy.start()
-    for i in range(parts):
-        z_copy(i).start()
+    z_copy.start()
     own_count = counts_ref[here_ref[0]]
     for j in range(rows // 128):
         here = pl.ds(j * 128, 128)
@@ -112,8 +107,7 @@
         scale_ref[here, :] = lax.rsqrt(mean + 1e-06) * (0.5 / math.sqrt(width))
     flips_copy.wait()
     signs_ref[...] = (2 * flips_buf[...] - 1).astype(jnp.bfloat16)
-    for i in range(parts):
-        z_copy(i).wait()
+    z_copy.wait()
 
 
 def prepare_rows(here, counts, x, z, flips, labels):
@@ -126,7 +120,7 @@
         "prepare_rows",
         [
             pltpu.VMEM((rows, width), x.dtype),
-            pltpu.VMEM(z.shape, z.dtype),
+            pltpu.VMEM((TILE, width), z.dtype),
             column,
             jax.ShapeDtypeStruct((perms, rows), jnp.bfloat16),
             column,
@@ -135,18 +129,35 @@
         [SMEM, SMEM, HBM, HBM, HBM, VMEM],
         (here, counts, in_hbm(x), in_hbm(z), in_hbm(flips), labels.reshape(-1, 128)),
         flops=3 * rows * width,
-        bytes_accessed=(rows + z.shape[0]) * width * 2 + perms * rows * 4,
+        bytes_accessed=(rows + TILE) * width * 2 + perms * rows * 4,
         scratch=[
             pltpu.VMEM(flips.shape, flips.dtype),
             pltpu.SemaphoreType.DMA((parts,)),
-            pltpu.SemaphoreType.DMA((parts,)),
+            pltpu.SemaphoreType.DMA,
             pltpu.SemaphoreType.DMA,
         ],
     )
 
 
-def moments_kernel(first, x_ref, z_ref, scale_ref, signs_ref, weight_ref, *rest):
-    out_ref = rest[-1]
+def row_copies(source, at, target, sem):
+    parts = sem.shape[0]
+    block = target.shape[0] // parts
+    copies = []
+    for i in range(parts):
+        rows = source.at[pl.ds(at + i * block, block), :]
+        copies.append(pltpu.make_async_copy(rows, target.at[pl.ds(i * block, block), :], sem.at[i]))
+    return copies
+
+
+def moments_kernel(first, loads, x_ref, z_ref, scale_ref, signs_ref, weight_ref, *rest):
+    copies = []
+    if loads:
+        z_all_ref, out_ref, held_ref, sem = rest
+        copies = row_copies(z_all_ref, TILE, held_ref, sem)
+    else:
+        out_ref = rest[-1]
+    for copy in copies:
+        copy.start()
     z = z_ref[pl.ds(first, TILE), :]
     z32 = z.astype(jnp.float32)
     mean = jnp.sum(z32 * z32, axis=1, keepdims=True) * (1.0 / z.shape[1])
@@ -156,32 +167,38 @@
     kern = jnp.exp(cross * scale_ref[...] * point_row)
     weighted = (weight_ref[...] * kern).astype(jnp.bfloat16)
     out_ref[...] = jnp.dot(signs_ref[...], weighted, preferred_element_type=jnp.float32).astype(jnp.bfloat16)
-
-
-def moments_part(first, x, z, scale, signs, weight, after):
+    for copy in copies:
+        copy.wait()
+
+
+def moments_part(first, x, z, scale, signs, weight, after=(), z_all=None):
     rows, width = x.shape
     perms = signs.shape[0]
-    return call(
-        functools.partial(moments_kernel, first),
+    out_shape = [jax.ShapeDtypeStruct((perms, TILE), jnp.bfloat16)]
+    in_specs, args, scratch = [VMEM] * 5, [x, z, scale, signs, weight], []
+    if z_all is not None:
+        others = z_all.shape[0] - TILE
+        out_shape.append(pltpu.VMEM((others, width), z.dtype))
+        in_specs, args = in_specs + [HBM], args + [in_hbm(z_all)]
+        scratch = [pltpu.SemaphoreType.DMA((others // TILE,))]
+    return call(
+        functools.partial(moments_kernel, first, z_all is not None),
         "moments",
-        jax.ShapeDtypeStruct((perms, TILE), jnp.bfloat16),
-        [VMEM] * 5 + [ANY] * len(after),
-        (x, z, scale, signs, weight, *after),
+        out_shape,
+        in_specs + [ANY] * len(after),
+        (*args, *after),
         flops=2 * rows * width * TILE + 2 * perms * rows * TILE,
         bytes_accessed=TILE * width * 2,
         transcendentals=rows * TILE,
+        scratch=scratch,
     )
 
 
 def load_kernel(factor_ref, *refs):
     held_ref, sem = refs[-2:]
-    parts = sem.shape[0]
-    block = factor_ref.shape[0] // parts
-    copies = []
-    for i in range(parts):
-        here = pl.ds(i * block, block)
-        copies.append(pltpu.make_async_copy(factor_ref.at[here, :], held_ref.at[here, :], sem.at[i]))
-        copies[-1].start()
+    copies = row_copies(factor_ref, 0, held_ref, sem)
+    for copy in copies:
+        copy.start()
     for copy in copies:
         copy.wait()
 
@@ -397,18 +414,23 @@
         totals = []
         value = None
         for t in range(count + n_sample - 1):
-            if t < count:
-                after = [value] if t > 0 else []
-                after += [line.recv[1, t - 2]] if (1, t - 2) in line.recv else []
-                line.pieces.append(moments_part(t * TILE, x, z, scale, signs, weight, after))
+            if t == 0:
+                piece, z = moments_part(0, x, z, scale, signs, weight, z_all=landmarks)
+                line.pieces.append(piece)
+            elif t < count:
+                after = [value] + ([line.recv[1, t - 2]] if (1, t - 2) in line.recv else [])
+                line.pieces += moments_part((t - 1) * TILE, x, z, scale, signs, weight, after)
             after = totals[-1:] + line.pieces[-1:]
+            if t == count + n_sample - 2:
+                after.append(held_factor)
             if t == count:
-                held_factor = load_factor(factor, [value, line.recv[1, t - 2]])
-                after.append(held_factor)
+                after.append(line.recv[1, t - 2])
             for parity in (1, 0):
                 sent = line.exchange(parity, t, after)
                 if sent is not None:
                     value, after = sent, [sent]
+            if t == count:
+                held_factor = load_factor(factor, [value, line.recv[1, t - 1]])
             if t >= n_sample:
                 totals.append(line.total(t - n_sample))
         totals.append(line.total(count - 1))

time: 148 us -> 149 us (level)
  waiting for transfers between devices: 38.3 us -> 42 us
  starting transfers between devices: 39.5 us -> 37.4 us
    ppermute x19, waiting for transfers between devices: 19.7 us -> 23.4 us  [exchange(): self.recv[parity, period] = lax.ppermute(value, 'sample', pairs)]
    ppermute x19, starting transfers between devices: 29.9 us -> 27.9 us  [exchange(): self.recv[parity, period] = lax.ppermute(value, 'sample', pairs)]
  transfers between devices with their start and end apart: 26 -> 26, of which waited for: 14 -> 13; matrix products, arithmetic and copies ran while one was open for 0% -> 0% of each run, Pallas kernels for 29% -> 27%
where the time goes in v6:
time: 149 us
  Pallas kernels  54.8 us (37%)
  waiting for transfers between devices  42 us (28%)
  starting transfers between devices  37.4 us (25%)
  blocking collectives  11.8 us (8%)
    pallas_call x47, Pallas kernels, call(): pl.pallas_call(kernel, out_shape=out_shape, in_specs=in_specs, out_specs=...  54.8 us
    ppermute x19, starting transfers between devices, exchange(): self.recv[parity, period] = lax.ppermute(value, 'sample', pairs)  27.9 us
    ppermute x19, waiting for transfers between devices, exchange(): self.recv[parity, period] = lax.ppermute(value, 'sample', pairs)  23.4 us
    all_to_all x1, blocking collectives, local(): share = lax.all_to_all(share, ('sample', 'landmark'), 0, 0, tiled=True)  11.8 us
    ppermute x1, waiting for transfers between devices, local(): recv = lax.ppermute(sums[0], 'landmark', pairs_of(1))  10.7 us
    ppermute x1, waiting for transfers between devices, local(): recv = lax.ppermute(sent, 'landmark', pairs_of(t))  7.63 us
    ppermute x3, starting transfers between devices, local(): pairs.append(lax.ppermute(own_pair, 'sample', to))  6.11 us
  transfers between devices with their start and end apart: 26, of which 13 were waited for; matrix products, arithmetic and copies ran while one was open for 0% of the time, Pallas kernels for 27%

profile of v6, /device:TPU:0, one launch (start us, length us, event | category | flops | bytes accessed | tf_op | source)
XLA Modules:
  0.0 149.1 jit_solution(9326607225492947236)
XLA Ops:
  2.7 5.1 %collective-permute-start.2 = (f32[8,128]{1,0:T(8,128)S(1)}, f32[8,128]{1,0:T(8,128)S(1)}, u32[]{:S(2)}, u32[]{:S(2)}) collective-permute-start(f32[8,128]{1,0:T(8,128)S(1)} %own_counts.1.refs_0_), channel_id=1, source_target_pairs={{0,24},{8,0},{16,8},{24,16},{1,25},{9,1},{17,9},{25,17},{2,26},{10... | collective-permute-start | bytes 12296 | tf_op jit(solution)/shard_map/ppermute | solution.py:409
  8.8 5.3 %prepare_rows.1 = (bf16[1024,4096]{1,0:T(8,128)(2,1)S(1)}, bf16[256,4096]{1,0:T(8,128)(2,1)S(1)}, f32[1024,1]{1,0:T(8,128)S(1)}, bf16[512,1024]{1,0:T(8,128)(2,1...) custom-call(s32[1]{0:T(128)} %bitcast.2.here_ref, s32[4]{0:T(128)S(1)} %copy-done.1, bf16[1024,4096]{1,0:T(8,128)(2,1)} %x_ref.1, ...), custom_call_target="tpu_custom_call" | custom-call | flops 12582912 | bytes 12582912 | tf_op jit(solution)/shard_map/prepare_rows/pallas_call | solution.py:27
  14.2 7.8 %moments.8 = (bf16[512,256]{1,0:T(8,128)(2,1)S(1)}, bf16[1792,4096]{1,0:T(8,128)(2,1)S(1)}) custom-call(bf16[1024,4096]{1,0:T(8,128)(2,1)S(1)} %get-tuple-element.14.x_ref, bf16[256,4096]{1,0:T(8,128)(2,1)S(1)} %get-tuple-element.15.z_ref, f32[1024,1]{1,0:T(8,128)S(1)} %get-tuple-element.16.scale_ref, bf16[512,1024]{1,0:T(8,128)(2,1)S(1)} %get-tuple-element.17.signs_ref, ...), custom_call_target="tpu_custom_call" | custom-call | flops 2415919104 | bytes 2097152 | tf_op jit(solution)/shard_map/moments/pallas_call | solution.py:27
  22.0 2.5 %collective-permute-start.3 = (bf16[512,256]{1,0:T(8,128)(2,1)S(1)}, bf16[512,256]{1,0:T(8,128)(2,1)S(1)}, u32[]{:S(2)}, u32[]{:S(2)}) collective-permute-start(bf16[512,256]{1,0:T(8,128)(2,1)S(1)} %exchanged.19.rest_0_), channel_id=1, source_target_pairs={{0,8},{8,0},{16,24},{24,16},{1,9},{9,1},{17,25},{25,17},{2,10},{10... | collective-permute-start | bytes 786440 | tf_op jit(solution)/shard_map/ppermute | solution.py:364
  24.6 3.2 %moments.9.refs_2_.refs_0_ = bf16[512,256]{1,0:T(8,128)(2,1)S(1)} custom-call(bf16[1024,4096]{1,0:T(8,128)(2,1)S(1)} %get-tuple-element.14.x_ref, bf16[1792,4096]{1,0:T(8,128)(2,1)S(1)} %get-tuple-element.20.z_ref, f32[1024,1]{1,0:T(8,128)S(1)} %get-tuple-element.16.scale_ref, bf16[512,1024]{1,0:T(8,128)(2,1)S(1)} %get-tuple-element.17.signs_ref, ...), custom_call_target="tpu_custom_call" | custom-call | flops 2415919104 | bytes 2097152 | tf_op jit(solution)/shard_map/moments/pallas_call | solution.py:27
  32.6 3.2 %moments.10.refs_2_.refs_0_ = bf16[512,256]{1,0:T(8,128)(2,1)S(1)} custom-call(bf16[1024,4096]{1,0:T(8,128)(2,1)S(1)} %get-tuple-element.14.x_ref, bf16[1792,4096]{1,0:T(8,128)(2,1)S(1)} %get-tuple-element.20.z_ref, f32[1024,1]{1,0:T(8,128)S(1)} %get-tuple-element.16.scale_ref, bf16[512,1024]{1,0:T(8,128)(2,1)S(1)} %get-tuple-element.17.signs_ref, ...), custom_call_target="tpu_custom_call" | custom-call | flops 2415919104 | bytes 2097152 | tf_op jit(solution)/shard_map/moments/pallas_call | solution.py:27
  39.6 3.2 %moments.11.refs_2_.refs_0_ = bf16[512,256]{1,0:T(8,128)(2,1)S(1)} custom-call(bf16[1024,4096]{1,0:T(8,128)(2,1)S(1)} %get-tuple-element.14.x_ref, bf16[1792,4096]{1,0:T(8,128)(2,1)S(1)} %get-tuple-element.20.z_ref, f32[1024,1]{1,0:T(8,128)S(1)} %get-tuple-element.16.scale_ref, bf16[512,1024]{1,0:T(8,128)(2,1)S(1)} %get-tuple-element.17.signs_ref, ...), custom_call_target="tpu_custom_call" | custom-call | flops 2415919104 | bytes 2097152 | tf_op jit(solution)/shard_map/moments/pallas_call | solution.py:27
  46.6 3.2 %moments.12.refs_2_.refs_0_ = bf16[512,256]{1,0:T(8,128)(2,1)S(1)} custom-call(bf16[1024,4096]{1,0:T(8,128)(2,1)S(1)} %get-tuple-element.14.x_ref, bf16[1792,4096]{1,0:T(8,128)(2,1)S(1)} %get-tuple-element.20.z_ref, f32[1024,1]{1,0:T(8,128)S(1)} %get-tuple-element.16.scale_ref, bf16[512,1024]{1,0:T(8,128)(2,1)S(1)} %get-tuple-element.17.signs_ref, ...), custom_call_target="tpu_custom_call" | custom-call | flops 2415919104 | bytes 2097152 | tf_op jit(solution)/shard_map/moments/pallas_call | solution.py:27
  50.2 2.4 %collective-permute-start.10 = (bf16[512,256]{1,0:T(8,128)(2,1)S(1)}, bf16[512,256]{1,0:T(8,128)(2,1)S(1)}, u32[]{:S(2)}, u32[]{:S(2)}) collective-permute-start(bf16[512,256]{1,0:T(8,128)(2,1)S(1)} %exchanged.27.rest_0_), channel_id=1, source_target_pairs={{0,8},{8,0},{16,24},{24,16},{1,9},{9,1},{17,25},{25,17},{2,10},{10... | collective-permute-start | bytes 786440 | tf_op jit(solution)/shard_map/ppermute | solution.py:364
  53.4 3.2 %moments.13.refs_3_.refs_0_ = bf16[512,256]{1,0:T(8,128)(2,1)S(1)} custom-call(bf16[1024,4096]{1,0:T(8,128)(2,1)S(1)} %get-tuple-element.14.x_ref, bf16[1792,4096]{1,0:T(8,128)(2,1)S(1)} %get-tuple-element.20.z_ref, f32[1024,1]{1,0:T(8,128)S(1)} %get-tuple-element.16.scale_ref, bf16[512,1024]{1,0:T(8,128)(2,1)S(1)} %get-tuple-element.17.signs_ref, ...), custom_call_target="tpu_custom_call" | custom-call | flops 2415919104 | bytes 2097152 | tf_op jit(solution)/shard_map/moments/pallas_call | solution.py:27
  58.1 2.4 %collective-permute-start.11 = (bf16[512,256]{1,0:T(8,128)(2,1)S(1)}, bf16[512,256]{1,0:T(8,128)(2,1)S(1)}, u32[]{:S(2)}, u32[]{:S(2)}) collective-permute-start(bf16[512,256]{1,0:T(8,128)(2,1)S(1)} %exchanged.29.rest_0_), channel_id=1, source_target_pairs={{0,8},{8,0},{16,24},{24,16},{1,9},{9,1},{17,25},{25,17},{2,10},{10... | collective-permute-start | bytes 786440 | tf_op jit(solution)/shard_map/ppermute | solution.py:364
  61.2 3.2 %moments.14.refs_3_.refs_0_ = bf16[512,256]{1,0:T(8,128)(2,1)S(1)} custom-call(bf16[1024,4096]{1,0:T(8,128)(2,1)S(1)} %get-tuple-element.14.x_ref, bf16[1792,4096]{1,0:T(8,128)(2,1)S(1)} %get-tuple-element.20.z_ref, f32[1024,1]{1,0:T(8,128)S(1)} %get-tuple-element.16.scale_ref, bf16[512,1024]{1,0:T(8,128)(2,1)S(1)} %get-tuple-element.17.signs_ref, ...), custom_call_target="tpu_custom_call" | custom-call | flops 2415919104 | bytes 2097152 | tf_op jit(solution)/shard_map/moments/pallas_call | solution.py:27
  66.7 2.4 %collective-permute-start.15 = (bf16[512,256]{1,0:T(8,128)(2,1)S(1)}, bf16[512,256]{1,0:T(8,128)(2,1)S(1)}, u32[]{:S(2)}, u32[]{:S(2)}) collective-permute-start(bf16[512,256]{1,0:T(8,128)(2,1)S(1)} %exchanged.31.rest_0_), channel_id=1, source_target_pairs={{0,8},{8,0},{16,24},{24,16},{1,9},{9,1},{17,25},{25,17},{2,10},{10... | collective-permute-start | bytes 786440 | tf_op jit(solution)/shard_map/ppermute | solution.py:364
  69.9 3.2 %moments.15.refs_3_.refs_0_ = bf16[512,256]{1,0:T(8,128)(2,1)S(1)} custom-call(bf16[1024,4096]{1,0:T(8,128)(2,1)S(1)} %get-tuple-element.14.x_ref, bf16[1792,4096]{1,0:T(8,128)(2,1)S(1)} %get-tuple-element.20.z_ref, f32[1024,1]{1,0:T(8,128)S(1)} %get-tuple-element.16.scale_ref, bf16[512,1024]{1,0:T(8,128)(2,1)S(1)} %get-tuple-element.17.signs_ref, ...), custom_call_target="tpu_custom_call" | custom-call | flops 2415919104 | bytes 2097152 | tf_op jit(solution)/shard_map/moments/pallas_call | solution.py:27
  73.1 3.1 %collective-permute-done.15.refs_1_.refs_0_ = bf16[512,256]{1,0:T(8,128)(2,1)S(1)} collective-permute-done((bf16[512,256]{1,0:T(8,128)(2,1)S(1)}, bf16[512,256]{1,0:T(8,128)(2,1)S(1)}, u32[]{:S(2)}, u32[]{:S(2)}) %collective-permute-start.15) | collective-permute-done | bytes 262176 | tf_op jit(solution)/shard_map/ppermute | solution.py:364
  79.1 6.5 %collective-permute-done.16.refs_1_.refs_0_ = bf16[512,256]{1,0:T(8,128)(2,1)S(1)} collective-permute-done((bf16[512,256]{1,0:T(8,128)(2,1)S(1)}, bf16[512,256]{1,0:T(8,128)(2,1)S(1)}, u32[]{:S(2)}, u32[]{:S(2)}) %collective-permute-start.16) | collective-permute-done | bytes 262176 | tf_op jit(solution)/shard_map/ppermute | solution.py:364
  90.5 5.9 %load_factor.1.refs_4_.factor_ref = bf16[2048,4096]{1,0:T(8,128)(2,1)S(1)} custom-call(bf16[2048,4096]{1,0:T(8,128)(2,1)} %factor_ref.1, bf16[512,256]{1,0:T(8,128)(2,1)S(1)} %exchanged.35.refs_0_, bf16[512,256]{1,0:T(8,128)(2,1)S(1)} %collective-permute-done.17.refs_1_.refs_2_), custom_call_target="tpu_custom_call" | custom-call | bytes 16777216 | tf_op jit(solution)/shard_map/load_factor/pallas_call | solution.py:27
  97.4 5.6 %collective-permute-done.21.refs_0_ = bf16[512,256]{1,0:T(8,128)(2,1)S(1)} collective-permute-done((bf16[512,256]{1,0:T(8,128)(2,1)S(1)}, bf16[512,256]{1,0:T(8,128)(2,1)S(1)}, u32[]{:S(2)}, u32[]{:S(2)}) %collective-permute-start.21) | collective-permute-done | bytes 262176 | tf_op jit(solution)/shard_map/ppermute | solution.py:364
  103.3 2.3 %whiten.4.refs_8_ = bf16[2,512,512]{2,1,0:T(8,128)(2,1)S(1)} custom-call(s32[1]{0:T(128)} %bitcast.refs_1_.spot_ref, bf16[2048,4096]{1,0:T(8,128)(2,1)S(1)} %load_factor.1.refs_4_.factor_ref, bf16[512,256]{1,0:T(8,128)(2,1)S(1)} %total.8.refs_2_.refs_0_, bf16[512,256]{1,0:T(8,128)(2,1)S(1)} %total.9.refs_2_.refs_1_, bf16[512,256]{1,0:T(8,128)(2,1)S(1)} %total.10.refs_2_, ...), custom_call_target="tpu_custom_call" | custom-call | flops 2147483648 | bytes 4194304 | tf_op jit(solution)/shard_map/whiten/pallas_call | solution.py:27
  105.7 2.4 %whiten.5.a_ref = bf16[2,512,512]{2,1,0:T(8,128)(2,1)S(1)} custom-call(s32[1]{0:T(128)} %bitcast.refs_1_.spot_ref, bf16[2048,4096]{1,0:T(8,128)(2,1)S(1)} %load_factor.1.refs_4_.factor_ref, bf16[512,256]{1,0:T(8,128)(2,1)S(1)} %total.8.refs_2_.refs_0_, bf16[512,256]{1,0:T(8,128)(2,1)S(1)} %total.9.refs_2_.refs_1_, bf16[512,256]{1,0:T(8,128)(2,1)S(1)} %total.10.refs_2_, ...), custom_call_target="tpu_custom_call" | custom-call | flops 2147483648 | bytes 4194304 | tf_op jit(solution)/shard_map/whiten/pallas_call | solution.py:27
  108.6 2.4 %whiten.6.refs_8_ = bf16[2,512,512]{2,1,0:T(8,128)(2,1)S(1)} custom-call(s32[1]{0:T(128)} %bitcast.refs_1_.spot_ref, bf16[2048,4096]{1,0:T(8,128)(2,1)S(1)} %load_factor.1.refs_4_.factor_ref, bf16[512,256]{1,0:T(8,128)(2,1)S(1)} %total.8.refs_2_.refs_0_, bf16[512,256]{1,0:T(8,128)(2,1)S(1)} %total.9.refs_2_.refs_1_, bf16[512,256]{1,0:T(8,128)(2,1)S(1)} %total.10.refs_2_, ...), custom_call_target="tpu_custom_call" | custom-call | flops 2147483648 | bytes 4194304 | tf_op jit(solution)/shard_map/whiten/pallas_call | solution.py:27
  115.3 10.7 %collective-permute-done.24.b_ref = bf16[2,512,512]{2,1,0:T(8,128)(2,1)S(1)} collective-permute-done((bf16[2,512,512]{2,1,0:T(8,128)(2,1)S(1)}, bf16[2,512,512]{2,1,0:T(8,128)(2,1)S(1)}, u32[]{:S(2)}, u32[]{:S(2)}) %collective-permute-start.24) | collective-permute-done | bytes 1048608 | tf_op jit(solution)/shard_map/ppermute | solution.py:446
  127.9 7.6 %collective-permute-done.25 = bf16[1,512,512]{2,1,0:T(8,128)(2,1)S(1)} collective-permute-done((bf16[1,512,512]{2,1,0:T(8,128)(2,1)S(1)}, bf16[1,512,512]{2,1,0:T(8,128)(2,1)S(1)}, u32[]{:S(2)}, u32[]{:S(2)}) %collective-permute-start.25) | collective-permute-done | bytes 524320 | tf_op jit(solution)/shard_map/ppermute | solution.py:451
  136.7 11.8 %all_to_all.5 = f32[32,4,128]{2,1,0:T(4,128)S(1)} all-to-all(f32[32,4,128]{2,1,0:T(4,128)S(1)} %get-tuple-element.25), channel_id=1, replica_groups=mesh['sample'=4,'landmark'=8] {'sample','landmark'}, dimensions={0} | all-to-all | bytes 131072 | tf_op jit(solution)/shard_map/all_to_all | solution.py:453
  (82 shorter events, 39.2 us)
Async XLA Ops:
  2.7 11.4 %collective-permute-start.2 = (f32[8,128]{1,0:T(8,128)S(1)}, f32[8,128]{1,0:T(8,128)S(1)}, u32[]{:S(2)}, u32[]{:S(2)}) collective-permute-start(f32[8,128]{1,0:T(8,128)S(1)} %own_counts.1.refs_0_), channel_id=1, source_target_pairs={{0,24},{8,0},{16,8},{24,16},{1,25},{9,1},{17,9},{25,17},{2,26},{10... | collective-permute-start | bytes 12296 | tf_op jit(solution)/shard_map/ppermute | solution.py:409
  7.8 6.3 %collective-permute-start.1 = (f32[8,128]{1,0:T(8,128)S(1)}, f32[8,128]{1,0:T(8,128)S(1)}, u32[]{:S(2)}, u32[]{:S(2)}) collective-permute-start(f32[8,128]{1,0:T(8,128)S(1)} %own_counts.1.refs_0_), channel_id=1, source_target_pairs={{0,16},{8,24},{16,0},{24,8},{1,17},{9,25},{17,1},{25,9},{2,18},{10... | collective-permute-start | bytes 12296 | tf_op jit(solution)/shard_map/ppermute | solution.py:409
  7.8 6.4 %collective-permute-start = (f32[8,128]{1,0:T(8,128)S(1)}, f32[8,128]{1,0:T(8,128)S(1)}, u32[]{:S(2)}, u32[]{:S(2)}) collective-permute-start(f32[8,128]{1,0:T(8,128)S(1)} %own_counts.1.refs_0_), channel_id=1, source_target_pairs={{0,8},{8,16},{16,24},{24,0},{1,9},{9,17},{17,25},{25,1},{2,10},{10... | collective-permute-start | bytes 12296 | tf_op jit(solution)/shard_map/ppermute | solution.py:409
  22.0 8.0 %collective-permute-start.3 = (bf16[512,256]{1,0:T(8,128)(2,1)S(1)}, bf16[512,256]{1,0:T(8,128)(2,1)S(1)}, u32[]{:S(2)}, u32[]{:S(2)}) collective-permute-start(bf16[512,256]{1,0:T(8,128)(2,1)S(1)} %exchanged.19.rest_0_), channel_id=1, source_target_pairs={{0,8},{8,0},{16,24},{24,16},{1,9},{9,1},{17,25},{25,17},{2,10},{10... | collective-permute-start | bytes 786440 | tf_op jit(solution)/shard_map/ppermute | solution.py:364
  30.1 6.6 %collective-permute-start.4 = (bf16[512,256]{1,0:T(8,128)(2,1)S(1)}, bf16[512,256]{1,0:T(8,128)(2,1)S(1)}, u32[]{:S(2)}, u32[]{:S(2)}) collective-permute-start(bf16[512,256]{1,0:T(8,128)(2,1)S(1)} %exchanged.21.rest_0_), channel_id=1, source_target_pairs={{0,8},{8,0},{16,24},{24,16},{1,9},{9,1},{17,25},{25,17},{2,10},{10... | collective-permute-start | bytes 786440 | tf_op jit(solution)/shard_map/ppermute | solution.py:364
  31.9 7.7 %collective-permute-start.5 = (bf16[512,256]{1,0:T(8,128)(2,1)S(1)}, bf16[512,256]{1,0:T(8,128)(2,1)S(1)}, u32[]{:S(2)}, u32[]{:S(2)}) collective-permute-start(bf16[512,256]{1,0:T(8,128)(2,1)S(1)} %exchanged.20.refs_1_), channel_id=1, source_target_pairs={{8,16},{16,8},{9,17},{17,9},{10,18},{18,10},{11,19},{19,11},{12,20... | collective-permute-start | bytes 786440 | tf_op jit(solution)/shard_map/ppermute | solution.py:364
  36.9 6.5 %collective-permute-start.6 = (bf16[512,256]{1,0:T(8,128)(2,1)S(1)}, bf16[512,256]{1,0:T(8,128)(2,1)S(1)}, u32[]{:S(2)}, u32[]{:S(2)}) collective-permute-start(bf16[512,256]{1,0:T(8,128)(2,1)S(1)} %exchanged.23.rest_0_), channel_id=1, source_target_pairs={{0,8},{8,0},{16,24},{24,16},{1,9},{9,1},{17,25},{25,17},{2,10},{10... | collective-permute-start | bytes 786440 | tf_op jit(solution)/shard_map/ppermute | solution.py:364
  39.0 7.6 %collective-permute-start.7 = (bf16[512,256]{1,0:T(8,128)(2,1)S(1)}, bf16[512,256]{1,0:T(8,128)(2,1)S(1)}, u32[]{:S(2)}, u32[]{:S(2)}) collective-permute-start(bf16[512,256]{1,0:T(8,128)(2,1)S(1)} %exchanged.22.refs_1_), channel_id=1, source_target_pairs={{8,16},{16,8},{9,17},{17,9},{10,18},{18,10},{11,19},{19,11},{12,20... | collective-permute-start | bytes 786440 | tf_op jit(solution)/shard_map/ppermute | solution.py:364
  43.4 6.7 %collective-permute-start.8 = (bf16[512,256]{1,0:T(8,128)(2,1)S(1)}, bf16[512,256]{1,0:T(8,128)(2,1)S(1)}, u32[]{:S(2)}, u32[]{:S(2)}) collective-permute-start(bf16[512,256]{1,0:T(8,128)(2,1)S(1)} %exchanged.25.rest_0_), channel_id=1, source_target_pairs={{0,8},{8,0},{16,24},{24,16},{1,9},{9,1},{17,25},{25,17},{2,10},{10... | collective-permute-start | bytes 786440 | tf_op jit(solution)/shard_map/ppermute | solution.py:364
  45.7 7.6 %collective-permute-start.9 = (bf16[512,256]{1,0:T(8,128)(2,1)S(1)}, bf16[512,256]{1,0:T(8,128)(2,1)S(1)}, u32[]{:S(2)}, u32[]{:S(2)}) collective-permute-start(bf16[512,256]{1,0:T(8,128)(2,1)S(1)} %exchanged.24.refs_3_.refs_1_), channel_id=1, source_target_pairs={{8,16},{16,8},{9,17},{17,9},{10,18},{18,10},{11,19},{19,11},{12,20... | collective-permute-start | bytes 786440 | tf_op jit(solution)/shard_map/ppermute | solution.py:364
  50.2 7.7 %collective-permute-start.10 = (bf16[512,256]{1,0:T(8,128)(2,1)S(1)}, bf16[512,256]{1,0:T(8,128)(2,1)S(1)}, u32[]{:S(2)}, u32[]{:S(2)}) collective-permute-start(bf16[512,256]{1,0:T(8,128)(2,1)S(1)} %exchanged.27.rest_0_), channel_id=1, source_target_pairs={{0,8},{8,0},{16,24},{24,16},{1,9},{9,1},{17,25},{25,17},{2,10},{10... | collective-permute-start | bytes 786440 | tf_op jit(solution)/shard_map/ppermute | solution.py:364
  52.6 8.5 %collective-permute-start.12 = (bf16[512,256]{1,0:T(8,128)(2,1)S(1)}, bf16[512,256]{1,0:T(8,128)(2,1)S(1)}, u32[]{:S(2)}, u32[]{:S(2)}) collective-permute-start(bf16[512,256]{1,0:T(8,128)(2,1)S(1)} %exchanged.26.refs_3_.refs_1_), channel_id=1, source_target_pairs={{8,16},{16,8},{9,17},{17,9},{10,18},{18,10},{11,19},{19,11},{12,20... | collective-permute-start | bytes 786440 | tf_op jit(solution)/shard_map/ppermute | solution.py:364
  58.1 8.6 %collective-permute-start.11 = (bf16[512,256]{1,0:T(8,128)(2,1)S(1)}, bf16[512,256]{1,0:T(8,128)(2,1)S(1)}, u32[]{:S(2)}, u32[]{:S(2)}) collective-permute-start(bf16[512,256]{1,0:T(8,128)(2,1)S(1)} %exchanged.29.rest_0_), channel_id=1, source_target_pairs={{0,8},{8,0},{16,24},{24,16},{1,9},{9,1},{17,25},{25,17},{2,10},{10... | collective-permute-start | bytes 786440 | tf_op jit(solution)/shard_map/ppermute | solution.py:364
  60.5 9.4 %collective-permute-start.14 = (bf16[512,256]{1,0:T(8,128)(2,1)S(1)}, bf16[512,256]{1,0:T(8,128)(2,1)S(1)}, u32[]{:S(2)}, u32[]{:S(2)}) collective-permute-start(bf16[512,256]{1,0:T(8,128)(2,1)S(1)} %exchanged.28.refs_3_.refs_1_), channel_id=1, source_target_pairs={{8,16},{16,8},{9,17},{17,9},{10,18},{18,10},{11,19},{19,11},{12,20... | collective-permute-start | bytes 786440 | tf_op jit(solution)/shard_map/ppermute | solution.py:364
  66.7 9.5 %collective-permute-start.15 = (bf16[512,256]{1,0:T(8,128)(2,1)S(1)}, bf16[512,256]{1,0:T(8,128)(2,1)S(1)}, u32[]{:S(2)}, u32[]{:S(2)}) collective-permute-start(bf16[512,256]{1,0:T(8,128)(2,1)S(1)} %exchanged.31.rest_0_), channel_id=1, source_target_pairs={{0,8},{8,0},{16,24},{24,16},{1,9},{9,1},{17,25},{25,17},{2,10},{10... | collective-permute-start | bytes 786440 | tf_op jit(solution)/shard_map/ppermute | solution.py:364
  69.2 9.9 %collective-permute-start.13 = (bf16[512,256]{1,0:T(8,128)(2,1)S(1)}, bf16[512,256]{1,0:T(8,128)(2,1)S(1)}, u32[]{:S(2)}, u32[]{:S(2)}) collective-permute-start(bf16[512,256]{1,0:T(8,128)(2,1)S(1)} %exchanged.30.refs_3_.refs_0_.refs_1_), channel_id=1, source_target_pairs={{8,16},{16,8},{9,17},{17,9},{10,18},{18,10},{11,19},{19,11},{12,20... | collective-permute-start | bytes 786440 | tf_op jit(solution)/shard_map/ppermute | solution.py:364
  76.4 9.2 %collective-permute-start.16 = (bf16[512,256]{1,0:T(8,128)(2,1)S(1)}, bf16[512,256]{1,0:T(8,128)(2,1)S(1)}, u32[]{:S(2)}, u32[]{:S(2)}) collective-permute-start(bf16[512,256]{1,0:T(8,128)(2,1)S(1)} %exchanged.33), channel_id=1, source_target_pairs={{0,8},{8,0},{16,24},{24,16},{1,9},{9,1},{17,25},{25,17},{2,10},{10... | collective-permute-start | bytes 786440 | tf_op jit(solution)/shard_map/ppermute | solution.py:364
  78.4 10.1 %collective-permute-start.17 = (bf16[512,256]{1,0:T(8,128)(2,1)S(1)}, bf16[512,256]{1,0:T(8,128)(2,1)S(1)}, u32[]{:S(2)}, u32[]{:S(2)}) collective-permute-start(bf16[512,256]{1,0:T(8,128)(2,1)S(1)} %exchanged.32.refs_3_.refs_0_.refs_1_), channel_id=1, source_target_pairs={{8,16},{16,8},{9,17},{17,9},{10,18},{18,10},{11,19},{19,11},{12,20... | collective-permute-start | bytes 786440 | tf_op jit(solution)/shard_map/ppermute | solution.py:364
  85.7 10.7 %collective-permute-start.18 = (bf16[512,256]{1,0:T(8,128)(2,1)S(1)}, bf16[512,256]{1,0:T(8,128)(2,1)S(1)}, u32[]{:S(2)}, u32[]{:S(2)}) collective-permute-start(bf16[512,256]{1,0:T(8,128)(2,1)S(1)} %exchanged.35.refs_0_), channel_id=1, source_target_pairs={{0,8},{8,0},{16,24},{24,16},{1,9},{9,1},{17,25},{25,17},{2,10},{10... | collective-permute-start | bytes 786440 | tf_op jit(solution)/shard_map/ppermute | solution.py:364
  87.8 8.7 %collective-permute-start.20 = (bf16[512,256]{1,0:T(8,128)(2,1)S(1)}, bf16[512,256]{1,0:T(8,128)(2,1)S(1)}, u32[]{:S(2)}, u32[]{:S(2)}) collective-permute-start(bf16[512,256]{1,0:T(8,128)(2,1)S(1)} %exchanged.34.refs_2_.refs_0_.refs_1_), channel_id=1, source_target_pairs={{8,16},{16,8},{9,17},{17,9},{10,18},{18,10},{11,19},{19,11},{12,20... | collective-permute-start | bytes 786440 | tf_op jit(solution)/shard_map/ppermute | solution.py:364
  88.6 8.8 %collective-permute-start.19 = (bf16[512,256]{1,0:T(8,128)(2,1)S(1)}, bf16[512,256]{1,0:T(8,128)(2,1)S(1)}, u32[]{:S(2)}, u32[]{:S(2)}) collective-permute-start(bf16[512,256]{1,0:T(8,128)(2,1)S(1)} %exchanged.36), channel_id=1, source_target_pairs={{0,8},{8,0},{16,24},{24,16},{1,9},{9,1},{17,25},{25,17},{2,10},{10... | collective-permute-start | bytes 786440 | tf_op jit(solution)/shard_map/ppermute | solution.py:364
  96.6 6.4 %collective-permute-start.21 = (bf16[512,256]{1,0:T(8,128)(2,1)S(1)}, bf16[512,256]{1,0:T(8,128)(2,1)S(1)}, u32[]{:S(2)}, u32[]{:S(2)}) collective-permute-start(bf16[512,256]{1,0:T(8,128)(2,1)S(1)} %exchanged.37), channel_id=1, source_target_pairs={{0,8},{8,0},{16,24},{24,16},{1,9},{9,1},{17,25},{25,17},{2,10},{10... | collective-permute-start | bytes 786440 | tf_op jit(solution)/shard_map/ppermute | solution.py:364
  111.2 14.8 %collective-permute-start.24 = (bf16[2,512,512]{2,1,0:T(8,128)(2,1)S(1)}, bf16[2,512,512]{2,1,0:T(8,128)(2,1)S(1)}, u32[]{:S(2)}, u32[]{:S(2)}) collective-permute-start(bf16[2,512,512]{2,1,0:T(8,128)(2,1)S(1)} %add_blocks.3.refs_8_), channel_id=1, source_target_pairs={{0,2},{1,5},{2,0},{3,7},{4,6},{5,1},{6,4},{7,3},{8,10},{9,13},{10,... | collective-permute-start | bytes 3145736 | tf_op jit(solution)/shard_map/ppermute | solution.py:446
  126.3 9.2 %collective-permute-start.25 = (bf16[1,512,512]{2,1,0:T(8,128)(2,1)S(1)}, bf16[1,512,512]{2,1,0:T(8,128)(2,1)S(1)}, u32[]{:S(2)}, u32[]{:S(2)}) collective-permute-start(bf16[1,512,512]{2,1,0:T(8,128)(2,1)S(1)} %get-tuple-element.23), channel_id=1, source_target_pairs={{0,4},{1,3},{2,6},{3,1},{4,0},{5,7},{6,2},{7,5},{8,12},{9,11},{10,... | collective-permute-start | bytes 1572872 | tf_op jit(solution)/shard_map/ppermute | solution.py:451
  (4 other events, 8.2 us)

commit v7 on v5

--- a/solution.py
+++ b/solution.py
@@ -198,30 +198,35 @@
     )
 
 
-def whiten_kernel(table, count, spot_ref, factor_ref, *refs):
-    out = refs[-1]
-    moments = jnp.concatenate([part[...] for part in refs[:count]], axis=1)
+def whiten_kernel(table, count, first, spot_ref, factor_ref, *refs):
+    out, parts = refs[-1], refs[:count]
+    moments = jnp.concatenate([part[...] for part in parts], axis=1)
+    rows = pl.ds(first, moments.shape[1])
     wide = out.shape[2]
     spot = spot_ref[0]
     for i, (zero, one) in enumerate(table):
         block = jnp.bitwise_xor(jnp.where(spot % 2 == 0, zero, one), spot)
         here = pl.ds(pl.multiple_of(block * wide, wide), wide)
-        out[i] = jnp.dot(moments, factor_ref[:, here], preferred_element_type=jnp.float32).astype(jnp.bfloat16)
-
-
-def whiten(table, spot, factor, parts, blocks, after):
+        value = jnp.dot(moments, factor_ref[rows, here], preferred_element_type=jnp.float32)
+        if first > 0:
+            value = value + refs[count][i]
+        out[i] = value.astype(out.dtype)
+
+
+def whiten(table, spot, factor, parts, blocks, after=(), partial=None):
     depth, columns = factor.shape
-    perms = parts[0].shape[0]
-    count = len(table)
+    perms, piece = parts[0].shape
     wide = columns // blocks
-    return call(
-        functools.partial(whiten_kernel, table, len(parts)),
-        "whiten",
-        jax.ShapeDtypeStruct((count, perms, wide), jnp.bfloat16),
-        [SMEM] + [VMEM] * (1 + len(parts)) + [ANY] * len(after),
-        (spot, factor, *parts, *after),
-        flops=2 * perms * depth * wide * count,
-        bytes_accessed=depth * wide * count * 2,
+    given = [] if partial is None else [partial]
+    first = 0 if partial is None else depth - len(parts) * piece
+    return call(
+        functools.partial(whiten_kernel, table, len(parts), first),
+        "whiten_first" if partial is None else "whiten",
+        jax.ShapeDtypeStruct((len(table), perms, wide), jnp.float32 if partial is None else jnp.bfloat16),
+        [SMEM] + [VMEM] * (1 + len(parts) + len(given)) + [ANY] * len(after),
+        (spot, factor, *parts, *given, *after),
+        flops=2 * perms * len(parts) * piece * wide * len(table),
+        bytes_accessed=len(parts) * piece * wide * len(table) * 2,
     )
 
 
@@ -347,8 +352,8 @@
         self.recv[parity, period] = lax.ppermute(value, "sample", pairs)
         return value
 
-    def total(self, c):
-        return sum_at("total", self.depth, {d: self.whole(d, c) for d in range(self.last + 1)})
+    def total(self, c, after=()):
+        return sum_at("total", self.depth, {d: self.whole(d, c) for d in range(self.last + 1)}, after)
 
 
 def make_local(mesh):
@@ -411,14 +416,18 @@
                     value, after = sent, [sent]
             if t >= n_sample:
                 totals.append(line.total(t - n_sample))
-        totals.append(line.total(count - 1))
-
         middle = len(kept_order) // 2
+        tables = []
+        for part in (slice(0, middle), slice(middle, None)):
+            tables += [table_of(sent_order[part], True), table_of(kept_order[part], False)]
+        firsts = [whiten(table, spot, held_factor, totals[:count // 2], n_landmark) for table in tables]
+        totals.append(line.total(count - 1, firsts[:3]))
+        late = totals[count // 2:]
         sums = []
-        for part in (slice(0, middle), slice(middle, None)):
-            sent = whiten(table_of(sent_order[part], True), spot, held_factor, totals, n_landmark, sums[-1:])
+        for i in (0, 2):
+            sent = whiten(tables[i], spot, held_factor, late, n_landmark, sums[-1:], firsts[i])
             recv = lax.ppermute(sent, "landmark", siblings)
-            kept = whiten(table_of(kept_order[part], False), spot, held_factor, totals, n_landmark, [sent])
+            kept = whiten(tables[i + 1], spot, held_factor, late, n_landmark, [sent], firsts[i + 1])
             (total,) = add_blocks(kept, recv, [kept.shape[0]])
             sums.append(total)
         recv = lax.ppermute(sums[0], "landmark", pairs_of(1))

time: 148 us -> 146 us (0.986)
  waiting for transfers between devices: 38.3 us -> 35.4 us
    ppermute x19, waiting for transfers between devices: 19.7 us -> 16 us  [exchange(): self.recv[parity, period] = lax.ppermute(value, 'sample', pairs)]
    pallas_call x47 -> x51, Pallas kernels: 54.1 us -> 54.8 us  [call(): pl.pallas_call(kernel, out_shape=out_shape, in_specs=in_specs, out_specs=...]
  transfers between devices with their start and end apart: 26 -> 26, of which waited for: 14 -> 13; matrix products, arithmetic and copies ran while one was open for 0% -> 0% of each run, Pallas kernels for 29% -> 32%
where the time goes in v7:
time: 146 us; the launch traced here: 145 us
  Pallas kernels  54.8 us (38%)
  starting transfers between devices  39.3 us (27%)
  waiting for transfers between devices  35.4 us (24%)
  blocking collectives  12.7 us (9%)
    pallas_call x51, Pallas kernels, call(): pl.pallas_call(kernel, out_shape=out_shape, in_specs=in_specs, out_specs=...  54.8 us
    ppermute x19, starting transfers between devices, exchange(): self.recv[parity, period] = lax.ppermute(value, 'sample', pairs)  29.6 us
    ppermute x19, waiting for transfers between devices, exchange(): self.recv[parity, period] = lax.ppermute(value, 'sample', pairs)  16 us
    all_to_all x1, blocking collectives, local(): share = lax.all_to_all(share, ('sample', 'landmark'), 0, 0, tiled=True)  12.7 us
    ppermute x1, waiting for transfers between devices, local(): recv = lax.ppermute(sums[0], 'landmark', pairs_of(1))  10.5 us
    ppermute x1, waiting for transfers between devices, local(): recv = lax.ppermute(sent, 'landmark', pairs_of(t))  7.49 us
    ppermute x3, starting transfers between devices, local(): pairs.append(lax.ppermute(own_pair, 'sample', to))  6.11 us
  transfers between devices with their start and end apart: 26, of which 13 were waited for; matrix products, arithmetic and copies ran while one was open for 0% of the time, Pallas kernels for 32%

profile of v7, /device:TPU:0, one launch (start us, length us, event | category | flops | bytes accessed | tf_op | source)
XLA Modules:
  0.0 145.3 jit_solution(9613480435218340561)
XLA Ops:
  2.7 5.1 %collective-permute-start.2 = (f32[8,128]{1,0:T(8,128)S(1)}, f32[8,128]{1,0:T(8,128)S(1)}, u32[]{:S(2)}, u32[]{:S(2)}) collective-permute-start(f32[8,128]{1,0:T(8,128)S(1)} %own_counts.1.refs_0_), channel_id=1, source_target_pairs={{0,24},{8,0},{16,8},{24,16},{1,25},{9,1},{17,9},{25,17},{2,26},{10... | collective-permute-start | bytes 12296 | tf_op jit(solution)/shard_map/ppermute | solution.py:397
  8.8 9.6 %prepare_rows.1 = (bf16[1024,4096]{1,0:T(8,128)(2,1)S(1)}, bf16[2048,4096]{1,0:T(8,128)(2,1)S(1)}, f32[1024,1]{1,0:T(8,128)S(1)}, bf16[512,1024]{1,0:T(8,128)(2,...) custom-call(s32[1]{0:T(128)} %bitcast.2.here_ref, s32[4]{0:T(128)S(1)} %copy-done.1, bf16[1024,4096]{1,0:T(8,128)(2,1)} %x_ref.1, ...), custom_call_target="tpu_custom_call" | custom-call | flops 12582912 | bytes 27262976 | tf_op jit(solution)/shard_map/prepare_rows/pallas_call | solution.py:27
  18.5 3.1 %moments.8.refs_0_.refs_1_ = bf16[512,256]{1,0:T(8,128)(2,1)S(1)} custom-call(bf16[1024,4096]{1,0:T(8,128)(2,1)S(1)} %get-tuple-element.12.x_ref, bf16[2048,4096]{1,0:T(8,128)(2,1)S(1)} %get-tuple-element.13.z_ref, f32[1024,1]{1,0:T(8,128)S(1)} %get-tuple-element.14.scale_ref, bf16[512,1024]{1,0:T(8,128)(2,1)S(1)} %get-tuple-element.15.signs_ref, ...), custom_call_target="tpu_custom_call" | custom-call | flops 2415919104 | bytes 2097152 | tf_op jit(solution)/shard_map/moments/pallas_call | solution.py:27
  21.6 2.5 %collective-permute-start.3 = (bf16[512,256]{1,0:T(8,128)(2,1)S(1)}, bf16[512,256]{1,0:T(8,128)(2,1)S(1)}, u32[]{:S(2)}, u32[]{:S(2)}) collective-permute-start(bf16[512,256]{1,0:T(8,128)(2,1)S(1)} %exchanged.19.rest_0_), channel_id=1, source_target_pairs={{0,8},{8,0},{16,24},{24,16},{1,9},{9,1},{17,25},{25,17},{2,10},{10... | collective-permute-start | bytes 786440 | tf_op jit(solution)/shard_map/ppermute | solution.py:352
  24.2 3.2 %moments.9.refs_2_.refs_0_ = bf16[512,256]{1,0:T(8,128)(2,1)S(1)} custom-call(bf16[1024,4096]{1,0:T(8,128)(2,1)S(1)} %get-tuple-element.12.x_ref, bf16[2048,4096]{1,0:T(8,128)(2,1)S(1)} %get-tuple-element.13.z_ref, f32[1024,1]{1,0:T(8,128)S(1)} %get-tuple-element.14.scale_ref, bf16[512,1024]{1,0:T(8,128)(2,1)S(1)} %get-tuple-element.15.signs_ref, ...), custom_call_target="tpu_custom_call" | custom-call | flops 2415919104 | bytes 2097152 | tf_op jit(solution)/shard_map/moments/pallas_call | solution.py:27
  27.4 2.3 %collective-permute-done.3.refs_1_ = bf16[512,256]{1,0:T(8,128)(2,1)S(1)} collective-permute-done((bf16[512,256]{1,0:T(8,128)(2,1)S(1)}, bf16[512,256]{1,0:T(8,128)(2,1)S(1)}, u32[]{:S(2)}, u32[]{:S(2)}) %collective-permute-start.3) | collective-permute-done | bytes 262176 | tf_op jit(solution)/shard_map/ppermute | solution.py:352
  32.2 3.1 %moments.10.refs_2_.refs_0_ = bf16[512,256]{1,0:T(8,128)(2,1)S(1)} custom-call(bf16[1024,4096]{1,0:T(8,128)(2,1)S(1)} %get-tuple-element.12.x_ref, bf16[2048,4096]{1,0:T(8,128)(2,1)S(1)} %get-tuple-element.13.z_ref, f32[1024,1]{1,0:T(8,128)S(1)} %get-tuple-element.14.scale_ref, bf16[512,1024]{1,0:T(8,128)(2,1)S(1)} %get-tuple-element.15.signs_ref, ...), custom_call_target="tpu_custom_call" | custom-call | flops 2415919104 | bytes 2097152 | tf_op jit(solution)/shard_map/moments/pallas_call | solution.py:27
  39.2 3.2 %moments.11.refs_2_.refs_0_ = bf16[512,256]{1,0:T(8,128)(2,1)S(1)} custom-call(bf16[1024,4096]{1,0:T(8,128)(2,1)S(1)} %get-tuple-element.12.x_ref, bf16[2048,4096]{1,0:T(8,128)(2,1)S(1)} %get-tuple-element.13.z_ref, f32[1024,1]{1,0:T(8,128)S(1)} %get-tuple-element.14.scale_ref, bf16[512,1024]{1,0:T(8,128)(2,1)S(1)} %get-tuple-element.15.signs_ref, ...), custom_call_target="tpu_custom_call" | custom-call | flops 2415919104 | bytes 2097152 | tf_op jit(solution)/shard_map/moments/pallas_call | solution.py:27
  43.0 2.3 %collective-permute-start.8 = (bf16[512,256]{1,0:T(8,128)(2,1)S(1)}, bf16[512,256]{1,0:T(8,128)(2,1)S(1)}, u32[]{:S(2)}, u32[]{:S(2)}) collective-permute-start(bf16[512,256]{1,0:T(8,128)(2,1)S(1)} %exchanged.25.rest_0_), channel_id=1, source_target_pairs={{0,8},{8,0},{16,24},{24,16},{1,9},{9,1},{17,25},{25,17},{2,10},{10... | collective-permute-start | bytes 786440 | tf_op jit(solution)/shard_map/ppermute | solution.py:352
  46.2 3.2 %moments.12.refs_2_.refs_0_ = bf16[512,256]{1,0:T(8,128)(2,1)S(1)} custom-call(bf16[1024,4096]{1,0:T(8,128)(2,1)S(1)} %get-tuple-element.12.x_ref, bf16[2048,4096]{1,0:T(8,128)(2,1)S(1)} %get-tuple-element.13.z_ref, f32[1024,1]{1,0:T(8,128)S(1)} %get-tuple-element.14.scale_ref, bf16[512,1024]{1,0:T(8,128)(2,1)S(1)} %get-tuple-element.15.signs_ref, ...), custom_call_target="tpu_custom_call" | custom-call | flops 2415919104 | bytes 2097152 | tf_op jit(solution)/shard_map/moments/pallas_call | solution.py:27
  49.9 2.4 %collective-permute-start.10 = (bf16[512,256]{1,0:T(8,128)(2,1)S(1)}, bf16[512,256]{1,0:T(8,128)(2,1)S(1)}, u32[]{:S(2)}, u32[]{:S(2)}) collective-permute-start(bf16[512,256]{1,0:T(8,128)(2,1)S(1)} %exchanged.27.rest_0_), channel_id=1, source_target_pairs={{0,8},{8,0},{16,24},{24,16},{1,9},{9,1},{17,25},{25,17},{2,10},{10... | collective-permute-start | bytes 786440 | tf_op jit(solution)/shard_map/ppermute | solution.py:352
  53.0 3.2 %moments.13.refs_3_.refs_0_ = bf16[512,256]{1,0:T(8,128)(2,1)S(1)} custom-call(bf16[1024,4096]{1,0:T(8,128)(2,1)S(1)} %get-tuple-element.12.x_ref, bf16[2048,4096]{1,0:T(8,128)(2,1)S(1)} %get-tuple-element.13.z_ref, f32[1024,1]{1,0:T(8,128)S(1)} %get-tuple-element.14.scale_ref, bf16[512,1024]{1,0:T(8,128)(2,1)S(1)} %get-tuple-element.15.signs_ref, ...), custom_call_target="tpu_custom_call" | custom-call | flops 2415919104 | bytes 2097152 | tf_op jit(solution)/shard_map/moments/pallas_call | solution.py:27
  57.9 2.4 %collective-permute-start.12 = (bf16[512,256]{1,0:T(8,128)(2,1)S(1)}, bf16[512,256]{1,0:T(8,128)(2,1)S(1)}, u32[]{:S(2)}, u32[]{:S(2)}) collective-permute-start(bf16[512,256]{1,0:T(8,128)(2,1)S(1)} %exchanged.29.rest_0_), channel_id=1, source_target_pairs={{0,8},{8,0},{16,24},{24,16},{1,9},{9,1},{17,25},{25,17},{2,10},{10... | collective-permute-start | bytes 786440 | tf_op jit(solution)/shard_map/ppermute | solution.py:352
  61.1 3.2 %moments.14.refs_3_.refs_0_ = bf16[512,256]{1,0:T(8,128)(2,1)S(1)} custom-call(bf16[1024,4096]{1,0:T(8,128)(2,1)S(1)} %get-tuple-element.12.x_ref, bf16[2048,4096]{1,0:T(8,128)(2,1)S(1)} %get-tuple-element.13.z_ref, f32[1024,1]{1,0:T(8,128)S(1)} %get-tuple-element.14.scale_ref, bf16[512,1024]{1,0:T(8,128)(2,1)S(1)} %get-tuple-element.15.signs_ref, ...), custom_call_target="tpu_custom_call" | custom-call | flops 2415919104 | bytes 2097152 | tf_op jit(solution)/shard_map/moments/pallas_call | solution.py:27
  64.3 2.5 %collective-permute-done.12.refs_1_.refs_0_ = bf16[512,256]{1,0:T(8,128)(2,1)S(1)} collective-permute-done((bf16[512,256]{1,0:T(8,128)(2,1)S(1)}, bf16[512,256]{1,0:T(8,128)(2,1)S(1)}, u32[]{:S(2)}, u32[]{:S(2)}) %collective-permute-start.12) | collective-permute-done | bytes 262176 | tf_op jit(solution)/shard_map/ppermute | solution.py:352
  66.9 2.5 %collective-permute-start.14 = (bf16[512,256]{1,0:T(8,128)(2,1)S(1)}, bf16[512,256]{1,0:T(8,128)(2,1)S(1)}, u32[]{:S(2)}, u32[]{:S(2)}) collective-permute-start(bf16[512,256]{1,0:T(8,128)(2,1)S(1)} %exchanged.31.rest_0_), channel_id=1, source_target_pairs={{0,8},{8,0},{16,24},{24,16},{1,9},{9,1},{17,25},{25,17},{2,10},{10... | collective-permute-start | bytes 786440 | tf_op jit(solution)/shard_map/ppermute | solution.py:352
  70.1 3.2 %moments.15.refs_3_.refs_0_ = bf16[512,256]{1,0:T(8,128)(2,1)S(1)} custom-call(bf16[1024,4096]{1,0:T(8,128)(2,1)S(1)} %get-tuple-element.12.x_ref, bf16[2048,4096]{1,0:T(8,128)(2,1)S(1)} %get-tuple-element.13.z_ref, f32[1024,1]{1,0:T(8,128)S(1)} %get-tuple-element.14.scale_ref, bf16[512,1024]{1,0:T(8,128)(2,1)S(1)} %get-tuple-element.15.signs_ref, ...), custom_call_target="tpu_custom_call" | custom-call | flops 2415919104 | bytes 2097152 | tf_op jit(solution)/shard_map/moments/pallas_call | solution.py:27
  73.2 3.1 %collective-permute-done.14.refs_1_.refs_0_ = bf16[512,256]{1,0:T(8,128)(2,1)S(1)} collective-permute-done((bf16[512,256]{1,0:T(8,128)(2,1)S(1)}, bf16[512,256]{1,0:T(8,128)(2,1)S(1)}, u32[]{:S(2)}, u32[]{:S(2)}) %collective-permute-start.14) | collective-permute-done | bytes 262176 | tf_op jit(solution)/shard_map/ppermute | solution.py:352
  79.0 5.9 %load_factor.1.refs_4_.factor_ref = bf16[2048,4096]{1,0:T(8,128)(2,1)S(1)} custom-call(bf16[2048,4096]{1,0:T(8,128)(2,1)} %factor_ref.1, bf16[512,256]{1,0:T(8,128)(2,1)S(1)} %exchanged.33.refs_0_, bf16[512,256]{1,0:T(8,128)(2,1)S(1)} %collective-permute-done.15.refs_1_.refs_2_), custom_call_target="tpu_custom_call" | custom-call | bytes 16777216 | tf_op jit(solution)/shard_map/load_factor/pallas_call | solution.py:27
  88.5 2.4 %collective-permute-start.19 = (bf16[512,256]{1,0:T(8,128)(2,1)S(1)}, bf16[512,256]{1,0:T(8,128)(2,1)S(1)}, u32[]{:S(2)}, u32[]{:S(2)}) collective-permute-start(bf16[512,256]{1,0:T(8,128)(2,1)S(1)} %exchanged.36), channel_id=1, source_target_pairs={{0,8},{8,0},{16,24},{24,16},{1,9},{9,1},{17,25},{25,17},{2,10},{10... | collective-permute-start | bytes 786440 | tf_op jit(solution)/shard_map/ppermute | solution.py:352
  90.9 3.1 %collective-permute-done.17.refs_0_ = bf16[512,256]{1,0:T(8,128)(2,1)S(1)} collective-permute-done((bf16[512,256]{1,0:T(8,128)(2,1)S(1)}, bf16[512,256]{1,0:T(8,128)(2,1)S(1)}, u32[]{:S(2)}, u32[]{:S(2)}) %collective-permute-start.17) | collective-permute-done | bytes 262176 | tf_op jit(solution)/shard_map/ppermute | solution.py:352
  110.8 10.5 %collective-permute-done.24.b_ref = bf16[2,512,512]{2,1,0:T(8,128)(2,1)S(1)} collective-permute-done((bf16[2,512,512]{2,1,0:T(8,128)(2,1)S(1)}, bf16[2,512,512]{2,1,0:T(8,128)(2,1)S(1)}, u32[]{:S(2)}, u32[]{:S(2)}) %collective-permute-start.24) | collective-permute-done | bytes 1048608 | tf_op jit(solution)/shard_map/ppermute | solution.py:433
  123.4 7.5 %collective-permute-done.25 = bf16[1,512,512]{2,1,0:T(8,128)(2,1)S(1)} collective-permute-done((bf16[1,512,512]{2,1,0:T(8,128)(2,1)S(1)}, bf16[1,512,512]{2,1,0:T(8,128)(2,1)S(1)}, u32[]{:S(2)}, u32[]{:S(2)}) %collective-permute-start.25) | collective-permute-done | bytes 524320 | tf_op jit(solution)/shard_map/ppermute | solution.py:438
  132.0 12.7 %all_to_all.5 = f32[32,4,128]{2,1,0:T(4,128)S(1)} all-to-all(f32[32,4,128]{2,1,0:T(4,128)S(1)} %get-tuple-element.21), channel_id=1, replica_groups=mesh['sample'=4,'landmark'=8] {'sample','landmark'}, dimensions={0} | all-to-all | bytes 131072 | tf_op jit(solution)/shard_map/all_to_all | solution.py:440
  (86 shorter events, 42.0 us)
Async XLA Ops:
  2.7 15.7 %collective-permute-start.2 = (f32[8,128]{1,0:T(8,128)S(1)}, f32[8,128]{1,0:T(8,128)S(1)}, u32[]{:S(2)}, u32[]{:S(2)}) collective-permute-start(f32[8,128]{1,0:T(8,128)S(1)} %own_counts.1.refs_0_), channel_id=1, source_target_pairs={{0,24},{8,0},{16,8},{24,16},{1,25},{9,1},{17,9},{25,17},{2,26},{10... | collective-permute-start | bytes 12296 | tf_op jit(solution)/shard_map/ppermute | solution.py:397
  7.8 10.6 %collective-permute-start.1 = (f32[8,128]{1,0:T(8,128)S(1)}, f32[8,128]{1,0:T(8,128)S(1)}, u32[]{:S(2)}, u32[]{:S(2)}) collective-permute-start(f32[8,128]{1,0:T(8,128)S(1)} %own_counts.1.refs_0_), channel_id=1, source_target_pairs={{0,16},{8,24},{16,0},{24,8},{1,17},{9,25},{17,1},{25,9},{2,18},{10... | collective-permute-start | bytes 12296 | tf_op jit(solution)/shard_map/ppermute | solution.py:397
  7.8 10.6 %collective-permute-start = (f32[8,128]{1,0:T(8,128)S(1)}, f32[8,128]{1,0:T(8,128)S(1)}, u32[]{:S(2)}, u32[]{:S(2)}) collective-permute-start(f32[8,128]{1,0:T(8,128)S(1)} %own_counts.1.refs_0_), channel_id=1, source_target_pairs={{0,8},{8,16},{16,24},{24,0},{1,9},{9,17},{17,25},{25,1},{2,10},{10... | collective-permute-start | bytes 12296 | tf_op jit(solution)/shard_map/ppermute | solution.py:397
  21.6 8.0 %collective-permute-start.3 = (bf16[512,256]{1,0:T(8,128)(2,1)S(1)}, bf16[512,256]{1,0:T(8,128)(2,1)S(1)}, u32[]{:S(2)}, u32[]{:S(2)}) collective-permute-start(bf16[512,256]{1,0:T(8,128)(2,1)S(1)} %exchanged.19.rest_0_), channel_id=1, source_target_pairs={{0,8},{8,0},{16,24},{24,16},{1,9},{9,1},{17,25},{25,17},{2,10},{10... | collective-permute-start | bytes 786440 | tf_op jit(solution)/shard_map/ppermute | solution.py:352
  29.8 6.6 %collective-permute-start.4 = (bf16[512,256]{1,0:T(8,128)(2,1)S(1)}, bf16[512,256]{1,0:T(8,128)(2,1)S(1)}, u32[]{:S(2)}, u32[]{:S(2)}) collective-permute-start(bf16[512,256]{1,0:T(8,128)(2,1)S(1)} %exchanged.21.rest_0_), channel_id=1, source_target_pairs={{0,8},{8,0},{16,24},{24,16},{1,9},{9,1},{17,25},{25,17},{2,10},{10... | collective-permute-start | bytes 786440 | tf_op jit(solution)/shard_map/ppermute | solution.py:352
  31.6 7.7 %collective-permute-start.5 = (bf16[512,256]{1,0:T(8,128)(2,1)S(1)}, bf16[512,256]{1,0:T(8,128)(2,1)S(1)}, u32[]{:S(2)}, u32[]{:S(2)}) collective-permute-start(bf16[512,256]{1,0:T(8,128)(2,1)S(1)} %exchanged.20.refs_1_), channel_id=1, source_target_pairs={{8,16},{16,8},{9,17},{17,9},{10,18},{18,10},{11,19},{19,11},{12,20... | collective-permute-start | bytes 786440 | tf_op jit(solution)/shard_map/ppermute | solution.py:352
  36.5 6.4 %collective-permute-start.6 = (bf16[512,256]{1,0:T(8,128)(2,1)S(1)}, bf16[512,256]{1,0:T(8,128)(2,1)S(1)}, u32[]{:S(2)}, u32[]{:S(2)}) collective-permute-start(bf16[512,256]{1,0:T(8,128)(2,1)S(1)} %exchanged.23.rest_0_), channel_id=1, source_target_pairs={{0,8},{8,0},{16,24},{24,16},{1,9},{9,1},{17,25},{25,17},{2,10},{10... | collective-permute-start | bytes 786440 | tf_op jit(solution)/shard_map/ppermute | solution.py:352
  38.5 7.7 %collective-permute-start.7 = (bf16[512,256]{1,0:T(8,128)(2,1)S(1)}, bf16[512,256]{1,0:T(8,128)(2,1)S(1)}, u32[]{:S(2)}, u32[]{:S(2)}) collective-permute-start(bf16[512,256]{1,0:T(8,128)(2,1)S(1)} %exchanged.22.refs_1_), channel_id=1, source_target_pairs={{8,16},{16,8},{9,17},{17,9},{10,18},{18,10},{11,19},{19,11},{12,20... | collective-permute-start | bytes 786440 | tf_op jit(solution)/shard_map/ppermute | solution.py:352
  43.0 6.8 %collective-permute-start.8 = (bf16[512,256]{1,0:T(8,128)(2,1)S(1)}, bf16[512,256]{1,0:T(8,128)(2,1)S(1)}, u32[]{:S(2)}, u32[]{:S(2)}) collective-permute-start(bf16[512,256]{1,0:T(8,128)(2,1)S(1)} %exchanged.25.rest_0_), channel_id=1, source_target_pairs={{0,8},{8,0},{16,24},{24,16},{1,9},{9,1},{17,25},{25,17},{2,10},{10... | collective-permute-start | bytes 786440 | tf_op jit(solution)/shard_map/ppermute | solution.py:352
  45.3 7.7 %collective-permute-start.9 = (bf16[512,256]{1,0:T(8,128)(2,1)S(1)}, bf16[512,256]{1,0:T(8,128)(2,1)S(1)}, u32[]{:S(2)}, u32[]{:S(2)}) collective-permute-start(bf16[512,256]{1,0:T(8,128)(2,1)S(1)} %exchanged.24.refs_3_.refs_1_), channel_id=1, source_target_pairs={{8,16},{16,8},{9,17},{17,9},{10,18},{18,10},{11,19},{19,11},{12,20... | collective-permute-start | bytes 786440 | tf_op jit(solution)/shard_map/ppermute | solution.py:352
  49.9 7.9 %collective-permute-start.10 = (bf16[512,256]{1,0:T(8,128)(2,1)S(1)}, bf16[512,256]{1,0:T(8,128)(2,1)S(1)}, u32[]{:S(2)}, u32[]{:S(2)}) collective-permute-start(bf16[512,256]{1,0:T(8,128)(2,1)S(1)} %exchanged.27.rest_0_), channel_id=1, source_target_pairs={{0,8},{8,0},{16,24},{24,16},{1,9},{9,1},{17,25},{25,17},{2,10},{10... | collective-permute-start | bytes 786440 | tf_op jit(solution)/shard_map/ppermute | solution.py:352
  52.3 8.8 %collective-permute-start.11 = (bf16[512,256]{1,0:T(8,128)(2,1)S(1)}, bf16[512,256]{1,0:T(8,128)(2,1)S(1)}, u32[]{:S(2)}, u32[]{:S(2)}) collective-permute-start(bf16[512,256]{1,0:T(8,128)(2,1)S(1)} %exchanged.26.refs_3_.refs_1_), channel_id=1, source_target_pairs={{8,16},{16,8},{9,17},{17,9},{10,18},{18,10},{11,19},{19,11},{12,20... | collective-permute-start | bytes 786440 | tf_op jit(solution)/shard_map/ppermute | solution.py:352
  57.9 8.9 %collective-permute-start.12 = (bf16[512,256]{1,0:T(8,128)(2,1)S(1)}, bf16[512,256]{1,0:T(8,128)(2,1)S(1)}, u32[]{:S(2)}, u32[]{:S(2)}) collective-permute-start(bf16[512,256]{1,0:T(8,128)(2,1)S(1)} %exchanged.29.rest_0_), channel_id=1, source_target_pairs={{0,8},{8,0},{16,24},{24,16},{1,9},{9,1},{17,25},{25,17},{2,10},{10... | collective-permute-start | bytes 786440 | tf_op jit(solution)/shard_map/ppermute | solution.py:352
  60.4 9.7 %collective-permute-start.13 = (bf16[512,256]{1,0:T(8,128)(2,1)S(1)}, bf16[512,256]{1,0:T(8,128)(2,1)S(1)}, u32[]{:S(2)}, u32[]{:S(2)}) collective-permute-start(bf16[512,256]{1,0:T(8,128)(2,1)S(1)} %exchanged.28.refs_3_.refs_1_), channel_id=1, source_target_pairs={{8,16},{16,8},{9,17},{17,9},{10,18},{18,10},{11,19},{19,11},{12,20... | collective-permute-start | bytes 786440 | tf_op jit(solution)/shard_map/ppermute | solution.py:352
  66.9 9.5 %collective-permute-start.14 = (bf16[512,256]{1,0:T(8,128)(2,1)S(1)}, bf16[512,256]{1,0:T(8,128)(2,1)S(1)}, u32[]{:S(2)}, u32[]{:S(2)}) collective-permute-start(bf16[512,256]{1,0:T(8,128)(2,1)S(1)} %exchanged.31.rest_0_), channel_id=1, source_target_pairs={{0,8},{8,0},{16,24},{24,16},{1,9},{9,1},{17,25},{25,17},{2,10},{10... | collective-permute-start | bytes 786440 | tf_op jit(solution)/shard_map/ppermute | solution.py:352
  69.3 9.7 %collective-permute-start.15 = (bf16[512,256]{1,0:T(8,128)(2,1)S(1)}, bf16[512,256]{1,0:T(8,128)(2,1)S(1)}, u32[]{:S(2)}, u32[]{:S(2)}) collective-permute-start(bf16[512,256]{1,0:T(8,128)(2,1)S(1)} %exchanged.30.refs_3_.refs_0_.refs_1_), channel_id=1, source_target_pairs={{8,16},{16,8},{9,17},{17,9},{10,18},{18,10},{11,19},{19,11},{12,20... | collective-permute-start | bytes 786440 | tf_op jit(solution)/shard_map/ppermute | solution.py:352
  76.5 9.2 %collective-permute-start.16 = (bf16[512,256]{1,0:T(8,128)(2,1)S(1)}, bf16[512,256]{1,0:T(8,128)(2,1)S(1)}, u32[]{:S(2)}, u32[]{:S(2)}) collective-permute-start(bf16[512,256]{1,0:T(8,128)(2,1)S(1)} %exchanged.33.refs_0_), channel_id=1, source_target_pairs={{0,8},{8,0},{16,24},{24,16},{1,9},{9,1},{17,25},{25,17},{2,10},{10... | collective-permute-start | bytes 786440 | tf_op jit(solution)/shard_map/ppermute | solution.py:352
  78.3 10.1 %collective-permute-start.18 = (bf16[512,256]{1,0:T(8,128)(2,1)S(1)}, bf16[512,256]{1,0:T(8,128)(2,1)S(1)}, u32[]{:S(2)}, u32[]{:S(2)}) collective-permute-start(bf16[512,256]{1,0:T(8,128)(2,1)S(1)} %exchanged.32.refs_3_.refs_0_.refs_1_), channel_id=1, source_target_pairs={{8,16},{16,8},{9,17},{17,9},{10,18},{18,10},{11,19},{19,11},{12,20... | collective-permute-start | bytes 786440 | tf_op jit(solution)/shard_map/ppermute | solution.py:352
  85.8 8.2 %collective-permute-start.17 = (bf16[512,256]{1,0:T(8,128)(2,1)S(1)}, bf16[512,256]{1,0:T(8,128)(2,1)S(1)}, u32[]{:S(2)}, u32[]{:S(2)}) collective-permute-start(bf16[512,256]{1,0:T(8,128)(2,1)S(1)} %exchanged.35), channel_id=1, source_target_pairs={{0,8},{8,0},{16,24},{24,16},{1,9},{9,1},{17,25},{25,17},{2,10},{10... | collective-permute-start | bytes 786440 | tf_op jit(solution)/shard_map/ppermute | solution.py:352
  87.7 6.6 %collective-permute-start.20 = (bf16[512,256]{1,0:T(8,128)(2,1)S(1)}, bf16[512,256]{1,0:T(8,128)(2,1)S(1)}, u32[]{:S(2)}, u32[]{:S(2)}) collective-permute-start(bf16[512,256]{1,0:T(8,128)(2,1)S(1)} %exchanged.34.refs_2_.refs_0_.refs_1_), channel_id=1, source_target_pairs={{8,16},{16,8},{9,17},{17,9},{10,18},{18,10},{11,19},{19,11},{12,20... | collective-permute-start | bytes 786440 | tf_op jit(solution)/shard_map/ppermute | solution.py:352
  88.5 11.6 %collective-permute-start.19 = (bf16[512,256]{1,0:T(8,128)(2,1)S(1)}, bf16[512,256]{1,0:T(8,128)(2,1)S(1)}, u32[]{:S(2)}, u32[]{:S(2)}) collective-permute-start(bf16[512,256]{1,0:T(8,128)(2,1)S(1)} %exchanged.36), channel_id=1, source_target_pairs={{0,8},{8,0},{16,24},{24,16},{1,9},{9,1},{17,25},{25,17},{2,10},{10... | collective-permute-start | bytes 786440 | tf_op jit(solution)/shard_map/ppermute | solution.py:352
  94.3 6.4 %collective-permute-start.21 = (bf16[512,256]{1,0:T(8,128)(2,1)S(1)}, bf16[512,256]{1,0:T(8,128)(2,1)S(1)}, u32[]{:S(2)}, u32[]{:S(2)}) collective-permute-start(bf16[512,256]{1,0:T(8,128)(2,1)S(1)} %exchanged.37), channel_id=1, source_target_pairs={{0,8},{8,0},{16,24},{24,16},{1,9},{9,1},{17,25},{25,17},{2,10},{10... | collective-permute-start | bytes 786440 | tf_op jit(solution)/shard_map/ppermute | solution.py:352
  106.5 14.8 %collective-permute-start.24 = (bf16[2,512,512]{2,1,0:T(8,128)(2,1)S(1)}, bf16[2,512,512]{2,1,0:T(8,128)(2,1)S(1)}, u32[]{:S(2)}, u32[]{:S(2)}) collective-permute-start(bf16[2,512,512]{2,1,0:T(8,128)(2,1)S(1)} %add_blocks.3.refs_5_), channel_id=1, source_target_pairs={{0,2},{1,5},{2,0},{3,7},{4,6},{5,1},{6,4},{7,3},{8,10},{9,13},{10,... | collective-permute-start | bytes 3145736 | tf_op jit(solution)/shard_map/ppermute | solution.py:433
  121.6 9.2 %collective-permute-start.25 = (bf16[1,512,512]{2,1,0:T(8,128)(2,1)S(1)}, bf16[1,512,512]{2,1,0:T(8,128)(2,1)S(1)}, u32[]{:S(2)}, u32[]{:S(2)}) collective-permute-start(bf16[1,512,512]{2,1,0:T(8,128)(2,1)S(1)} %get-tuple-element.19), channel_id=1, source_target_pairs={{0,4},{1,3},{2,6},{3,1},{4,0},{5,7},{6,2},{7,5},{8,12},{9,11},{10,... | collective-permute-start | bytes 1572872 | tf_op jit(solution)/shard_map/ppermute | solution.py:438
  (4 other events, 8.3 us)
